TPU v7x, 32 devices: a whole 2x2x4 slice. The times are simulated.
32 devices in a mesh: shard: 4 (over y, x), rep: 8 (over z, core).
Axes of the slice: x: 2, y: 2, z: 4, core: 2. Of those that a mesh axis runs over, the one named last changes fastest.
Arguments:
- tokens: bfloat16 [8192, 2560], P(('shard', 'rep')), may hold values from -6 to 6
- segments: int32 [32, 256], P(('shard', 'rep')), may hold values from 0 to 3, never falling along the last dimension, each value on 1 to 128 neighbouring positions
- cotangent: bfloat16 [8192, 2560], P(('shard', 'rep')), may hold values from -6 to 6
- latent_proj: bfloat16 [2560, 1056], P('shard'), may hold values from -0.125 to 0.125
- query_up: bfloat16 [768, 3840], P('shard'), may hold values from -0.21875 to 0.21875
- keyval_up: bfloat16 [256, 5120], P('shard'), may hold values from -0.375 to 0.375
- out_proj: bfloat16 [2560, 2560], P('shard'), may hold values from -2.5 to 2.5
- gate_up: bfloat16 [2560, 12800], P('shard'), may hold values from -0.125 to 0.125
- down_proj: bfloat16 [6400, 2560], P('shard'), may hold values from -0.4375 to 0.4375
- norm_gains: bfloat16 [6144], P('shard'), may hold values from 0.5 to 1.5
- latent_mean: bfloat16 [2560, 1056], P(('shard', 'rep')), may hold values from -128 to 128
- query_mean: bfloat16 [768, 3840], P(('shard', 'rep')), may hold values from -32 to 32
- keyval_mean: bfloat16 [256, 5120], P(('shard', 'rep')), may hold values from -64 to 64
- outproj_mean: bfloat16 [2560, 2560], P(('shard', 'rep')), may hold values from -3.5 to 3.5
- gateup_mean: bfloat16 [2560, 12800], P(('shard', 'rep')), may hold values from -20 to 20
- down_mean: bfloat16 [6400, 2560], P(('shard', 'rep')), may hold values from -5 to 5
- gains_mean: bfloat16 [6144], P(('shard', 'rep')), may hold values from -96 to 96
- latent_square: bfloat16 [2560, 1056], P(('shard', 'rep')), may hold values from 1144 to 17920
- query_square: bfloat16 [768, 3840], P(('shard', 'rep')), may hold values from 77 to 1224
- keyval_square: bfloat16 [256, 5120], P(('shard', 'rep')), may hold values from 212 to 3440
- outproj_square: bfloat16 [2560, 2560], P(('shard', 'rep')), may hold values from 0.81640625 to 12.25
- gateup_square: bfloat16 [2560, 12800], P(('shard', 'rep')), may hold values from 27 to 408
- down_square: bfloat16 [6400, 2560], P(('shard', 'rep')), may hold values from 1.6328125 to 27.75
- gains_square: bfloat16 [6144], P(('shard', 'rep')), may hold values from 474 to 7776
Outputs:
- block_out: bfloat16 [8192, 2560], P(('shard', 'rep'))
- input_grad: float32 [8192, 2560], P(('shard', 'rep'))
- latent_updated: float32 [2560, 1056], P(('shard', 'rep'))
- latent_mean_next: float32 [2560, 1056], P(('shard', 'rep'))
- latent_square_next: float32 [2560, 1056], P(('shard', 'rep'))
- query_updated: float32 [768, 3840], P(('shard', 'rep'))
- query_mean_next: float32 [768, 3840], P(('shard', 'rep'))
- query_square_next: float32 [768, 3840], P(('shard', 'rep'))
- keyval_updated: float32 [256, 5120], P(('shard', 'rep'))
- keyval_mean_next: float32 [256, 5120], P(('shard', 'rep'))
- keyval_square_next: float32 [256, 5120], P(('shard', 'rep'))
- outproj_updated: float32 [2560, 2560], P(('shard', 'rep'))
- outproj_mean_next: float32 [2560, 2560], P(('shard', 'rep'))
- outproj_square_next: float32 [2560, 2560], P(('shard', 'rep'))
- gateup_updated: float32 [2560, 12800], P(('shard', 'rep'))
- gateup_mean_next: float32 [2560, 12800], P(('shard', 'rep'))
- gateup_square_next: float32 [2560, 12800], P(('shard', 'rep'))
- down_updated: float32 [6400, 2560], P(('shard', 'rep'))
- down_mean_next: float32 [6400, 2560], P(('shard', 'rep'))
- down_square_next: float32 [6400, 2560], P(('shard', 'rep'))
- gains_updated: float32 [6144], P(('shard', 'rep'))
- gains_mean_next: float32 [6144], P(('shard', 'rep'))
- gains_square_next: float32 [6144], P(('shard', 'rep'))
Inputs may be any that keep to these rules, and one draw needn't show every extreme that they name: `segments`: never falling along a sequence.
All inputs are finite; a program needn't handle non-finite values.
Results may differ from a plain program's by a relative error of at most 0.033.
Values may be sent and summed in bfloat16 or wider, within the bound.
A program may use at most 512 MiB of HBM per device.

v0:
```python
import math

import jax
import jax.numpy as jnp
from jax import lax
from jax.sharding import PartitionSpec as P

D = 2560
H = 40
HD = 64
RD = 32
QR = 768
KR = 256
FF = 6400
STEP = 10


norm_eps = 1e-05
residual_scale = 1.4 / math.sqrt(62.0)
beta_one = 0.9
beta_two = 0.95
adam_eps = 1e-08
decay_rate = 0.1
gain_rate = 0.8


def inverse_rms(values):
    return lax.rsqrt(jnp.mean(values * values, axis=-1, keepdims=True) + norm_eps)


def norm_back(incoming, operand, inv_scale):
    return inv_scale * (
        incoming
        - operand * inv_scale * inv_scale * jnp.mean(incoming * operand, axis=-1, keepdims=True)
    )


def rotate(values, cos_table, sin_table):
    half_width = values.shape[-1] // 2
    first_half = values[..., :half_width]
    second_half = values[..., half_width:]
    return jnp.concatenate(
        [
            first_half * cos_table - second_half * sin_table,
            second_half * cos_table + first_half * sin_table,
        ],
        axis=-1,
    )


def rotate_back(values, cos_table, sin_table):
    half_width = values.shape[-1] // 2
    first_half = values[..., :half_width]
    second_half = values[..., half_width:]
    return jnp.concatenate(
        [
            first_half * cos_table + second_half * sin_table,
            second_half * cos_table - first_half * sin_table,
        ],
        axis=-1,
    )


def position_tables(segment_row):
    position_index = jnp.arange(segment_row.shape[0])
    same_doc = segment_row[None, :] == segment_row[:, None]
    earlier = position_index[None, :] < position_index[:, None]
    position = jnp.sum(jnp.where(same_doc & earlier, 1.0, 0.0), axis=1).astype(jnp.float32)
    frequency = 10000.0 ** (-jnp.arange(RD // 2).astype(jnp.float32) * 2.0 / RD)
    angles = position[:, None] * frequency[None, :]
    allowed = same_doc & (position_index[None, :] <= position_index[:, None])
    return (jnp.cos(angles), jnp.sin(angles), allowed)


def to_groups(heads, head_block):
    seq_len, count_heads, width = heads.shape
    return heads.transpose(1, 0, 2).reshape(count_heads // head_block, head_block, seq_len, width)


def from_groups(grouped):
    count_groups, head_block, seq_len, width = grouped.shape
    return grouped.reshape(count_groups * head_block, seq_len, width).transpose(1, 0, 2)


def own_rows(weight, gradient):
    count = gradient.shape[0]
    start = lax.axis_index("rep") * count
    return lax.dynamic_slice_in_dim(weight, start, count, 0)


def adam_step(weight, gradient, mean_old, square_old, step_rate, decay_factor):
    weight_f = own_rows(weight, gradient).astype(jnp.float32)
    mean_new = beta_one * mean_old.astype(jnp.float32) + (1.0 - beta_one) * gradient
    square_new = beta_two * square_old.astype(jnp.float32) + (1.0 - beta_two) * gradient * gradient
    ratio = (
        mean_new
        / (1.0 - beta_one**STEP)
        / (jnp.sqrt(square_new / (1.0 - beta_two**STEP)) + adam_eps)
    )
    updated = weight_f - step_rate * (ratio + decay_factor * weight_f)
    return (updated, mean_new, square_new)


def per_device(
    tokens,
    segments,
    cotangent,
    latent_proj,
    query_up,
    keyval_up,
    out_proj,
    gate_up,
    down_proj,
    norm_gains,
    latent_mean,
    query_mean,
    keyval_mean,
    outproj_mean,
    gateup_mean,
    down_mean,
    gains_mean,
    latent_square,
    query_square,
    keyval_square,
    outproj_square,
    gateup_square,
    down_square,
    gains_square,
):
    f32 = jnp.float32
    bf16 = jnp.bfloat16
    head_block = math.gcd(H, 8)
    latent_w, query_w, keyval_w, out_w, gains_all = (
        lax.all_gather(latent_proj, "shard", axis=0, tiled=True),
        lax.all_gather(query_up, "shard", axis=0, tiled=True),
        lax.all_gather(keyval_up, "shard", axis=0, tiled=True),
        lax.all_gather(out_proj, "shard", axis=0, tiled=True),
        lax.all_gather(norm_gains, "shard", axis=0, tiled=True),
    )
    gateup_w, down_w = (
        lax.all_gather(gate_up, "shard", axis=0, tiled=True),
        lax.all_gather(down_proj, "shard", axis=0, tiled=True),
    )
    gains_f = gains_all.astype(f32)
    gain_in = gains_f[:D]
    gain_query = gains_f[D : D + QR]
    gain_keyval = gains_f[D + QR : D + QR + KR]
    gain_mlp = gains_f[D + QR + KR :]
    seq_len = tokens.shape[0]
    score_scale = (HD + RD) ** (-0.5)
    cos_table, sin_table, allowed = position_tables(segments[0])
    rows_in = tokens.astype(f32)
    inv_in = inverse_rms(rows_in)
    normed_in = (rows_in * inv_in * gain_in).astype(bf16)
    latent_all = jnp.dot(normed_in, latent_w, preferred_element_type=f32)
    query_lat = latent_all[:, :QR]
    keyval_lat = latent_all[:, QR : QR + KR]
    inv_query = inverse_rms(query_lat)
    inv_keyval = inverse_rms(keyval_lat)
    normed_query = (query_lat * inv_query * gain_query).astype(bf16)
    normed_keyval = (keyval_lat * inv_keyval * gain_keyval).astype(bf16)
    query = jnp.dot(normed_query, query_w, preferred_element_type=f32).reshape(seq_len, H, HD + RD)
    keyval = jnp.dot(normed_keyval, keyval_w, preferred_element_type=f32).reshape(
        seq_len, H, 2 * HD
    )
    key_rope = rotate(latent_all[:, QR + KR :], cos_table, sin_table)
    query_heads = jnp.concatenate(
        [query[:, :, :HD], rotate(query[:, :, HD:], cos_table[:, None, :], sin_table[:, None, :])],
        axis=2,
    ).astype(bf16)
    key_heads = jnp.concatenate(
        [keyval[:, :, :HD], jnp.broadcast_to(key_rope[:, None, :], (seq_len, H, RD))], axis=2
    ).astype(bf16)
    value_heads = keyval[:, :, HD:].astype(bf16)
    query_groups = to_groups(query_heads, head_block)
    key_groups = to_groups(key_heads, head_block)
    value_groups = to_groups(value_heads, head_block)

    def attend_forward(operands):
        query_part, key_part, value_part = operands
        scores = (
            jnp.einsum("hqd,hkd->hqk", query_part, key_part, preferred_element_type=f32)
            * score_scale
        )
        masked = jnp.where(allowed[None], scores, -1e30)
        row_max = jnp.max(masked, axis=2, keepdims=True)
        exponent = jnp.exp(masked - row_max)
        row_sum = jnp.sum(exponent, axis=2, keepdims=True)
        probs_low = (exponent / row_sum).astype(bf16)
        mixed_part = jnp.einsum("hqk,hkd->hqd", probs_low, value_part, preferred_element_type=f32)
        return (mixed_part, row_max + jnp.log(row_sum))

    mixed_groups, log_total = lax.map(attend_forward, (query_groups, key_groups, value_groups))
    mixed_heads = from_groups(mixed_groups).reshape(seq_len, H * HD).astype(bf16)
    hidden = rows_in + residual_scale * jnp.dot(mixed_heads, out_w, preferred_element_type=f32)
    inv_hidden = inverse_rms(hidden)
    normed_mlp = (hidden * inv_hidden * gain_mlp).astype(bf16)
    gate_up_rows = jnp.dot(normed_mlp, gateup_w, preferred_element_type=f32)
    gate_rows = gate_up_rows[:, :FF]
    up_rows = gate_up_rows[:, FF:]
    activation = (jax.nn.silu(gate_rows) * up_rows).astype(bf16)
    block_out = (
        hidden + residual_scale * jnp.dot(activation, down_w, preferred_element_type=f32)
    ).astype(bf16)
    grad_top = cotangent.astype(f32)
    gateup_back, down_back = (
        lax.all_gather(gate_up, "shard", axis=0, tiled=True),
        lax.all_gather(down_proj, "shard", axis=0, tiled=True),
    )
    grad_branch = (residual_scale * grad_top).astype(bf16)
    down_sum = lax.psum_scatter(
        jnp.einsum("tf,td->fd", activation, grad_branch, preferred_element_type=f32).astype(
            jnp.bfloat16
        ),
        "shard",
        scatter_dimension=0,
        tiled=True,
    )
    grad_act = jnp.einsum("td,fd->tf", grad_branch, down_back, preferred_element_type=f32)
    sigmoid_gate = jax.nn.sigmoid(gate_rows)
    grad_gate = grad_act * up_rows * sigmoid_gate * (1.0 + gate_rows * (1.0 - sigmoid_gate))
    grad_up = grad_act * gate_rows * sigmoid_gate
    grad_gu = jnp.concatenate([grad_gate, grad_up], axis=1).astype(bf16)
    gateup_sum = lax.psum_scatter(
        jnp.einsum("td,tf->df", normed_mlp, grad_gu, preferred_element_type=f32).astype(
            jnp.bfloat16
        ),
        "shard",
        scatter_dimension=0,
        tiled=True,
    )
    grad_normed_mlp = jnp.einsum("tf,df->td", grad_gu, gateup_back, preferred_element_type=f32)
    grad_gain_mlp = jnp.sum(grad_normed_mlp * hidden * inv_hidden, axis=0)
    grad_hidden = grad_top + norm_back(grad_normed_mlp * gain_mlp, hidden, inv_hidden)
    latent_back, query_back, keyval_back, out_back, gains_back = (
        lax.all_gather(latent_proj, "shard", axis=0, tiled=True),
        lax.all_gather(query_up, "shard", axis=0, tiled=True),
        lax.all_gather(keyval_up, "shard", axis=0, tiled=True),
        lax.all_gather(out_proj, "shard", axis=0, tiled=True),
        lax.all_gather(norm_gains, "shard", axis=0, tiled=True),
    )
    grad_attn = (residual_scale * grad_hidden).astype(bf16)
    grad_out = jnp.einsum("ta,td->ad", mixed_heads, grad_attn, preferred_element_type=f32)
    grad_mixed = (
        jnp.einsum("td,ad->ta", grad_attn, out_back, preferred_element_type=f32)
        .astype(bf16)
        .reshape(seq_len, H, HD)
    )
    grad_mixed_groups = to_groups(grad_mixed, head_block)

    def attend_backward(operands):
        query_part, key_part, value_part, grad_part, total_part = operands
        scores_again = (
            jnp.einsum("hqd,hkd->hqk", query_part, key_part, preferred_element_type=f32)
            * score_scale
        )
        probs_again = jnp.exp(jnp.where(allowed[None], scores_again, -1e30) - total_part)
        grad_probs = jnp.einsum("hqd,hkd->hqk", grad_part, value_part, preferred_element_type=f32)
        grad_values = jnp.einsum(
            "hqk,hqd->hkd", probs_again.astype(bf16), grad_part, preferred_element_type=f32
        )
        row_delta = jnp.sum(probs_again * grad_probs, axis=2, keepdims=True)
        grad_scores = (probs_again * (grad_probs - row_delta)).astype(bf16)
        grad_qpart = (
            jnp.einsum("hqk,hkd->hqd", grad_scores, key_part, preferred_element_type=f32)
            * score_scale
        )
        grad_kpart = (
            jnp.einsum("hqk,hqd->hkd", grad_scores, query_part, preferred_element_type=f32)
            * score_scale
        )
        return (grad_qpart, grad_kpart, grad_values)

    grad_qgroups, grad_kgroups, grad_vgroups = lax.map(
        attend_backward, (query_groups, key_groups, value_groups, grad_mixed_groups, log_total)
    )
    grad_qheads = from_groups(grad_qgroups)
    grad_kheads = from_groups(grad_kgroups)
    grad_values = from_groups(grad_vgroups)
    grad_query_rows = (
        jnp.concatenate(
            [
                grad_qheads[:, :, :HD],
                rotate_back(grad_qheads[:, :, HD:], cos_table[:, None, :], sin_table[:, None, :]),
            ],
            axis=2,
        )
        .reshape(seq_len, H * (HD + RD))
        .astype(bf16)
    )
    grad_keyval_rows = (
        jnp.concatenate([grad_kheads[:, :, :HD], grad_values], axis=2)
        .reshape(seq_len, 2 * H * HD)
        .astype(bf16)
    )
    grad_key_rope = rotate_back(jnp.sum(grad_kheads[:, :, HD:], axis=1), cos_table, sin_table)
    grad_query = jnp.einsum("tr,tc->rc", normed_query, grad_query_rows, preferred_element_type=f32)
    grad_keyval = jnp.einsum(
        "tr,tc->rc", normed_keyval, grad_keyval_rows, preferred_element_type=f32
    )
    grad_normed_query = jnp.einsum(
        "tc,rc->tr", grad_query_rows, query_back, preferred_element_type=f32
    )
    grad_normed_keyval = jnp.einsum(
        "tc,rc->tr", grad_keyval_rows, keyval_back, preferred_element_type=f32
    )
    grad_gain_query = jnp.sum(grad_normed_query * query_lat * inv_query, axis=0)
    grad_gain_keyval = jnp.sum(grad_normed_keyval * keyval_lat * inv_keyval, axis=0)
    grad_latent_rows = jnp.concatenate(
        [
            norm_back(grad_normed_query * gain_query, query_lat, inv_query),
            norm_back(grad_normed_keyval * gain_keyval, keyval_lat, inv_keyval),
            grad_key_rope,
        ],
        axis=1,
    ).astype(bf16)
    grad_latent = jnp.einsum("td,tc->dc", normed_in, grad_latent_rows, preferred_element_type=f32)
    grad_normed_in = jnp.einsum(
        "tc,dc->td", grad_latent_rows, latent_back, preferred_element_type=f32
    )
    grad_gain_in = jnp.sum(grad_normed_in * rows_in * inv_in, axis=0)
    input_grad = grad_hidden + norm_back(grad_normed_in * gain_in, rows_in, inv_in)
    grad_gains = jnp.concatenate([grad_gain_in, grad_gain_query, grad_gain_keyval, grad_gain_mlp])
    latent_sum, query_sum, keyval_sum, outproj_sum, gains_sum = (
        lax.psum_scatter(
            grad_latent.astype(jnp.bfloat16), "shard", scatter_dimension=0, tiled=True
        ).astype(jnp.float32),
        lax.psum_scatter(
            grad_query.astype(jnp.bfloat16), "shard", scatter_dimension=0, tiled=True
        ).astype(jnp.float32),
        lax.psum_scatter(
            grad_keyval.astype(jnp.bfloat16), "shard", scatter_dimension=0, tiled=True
        ).astype(jnp.float32),
        lax.psum_scatter(
            grad_out.astype(jnp.bfloat16), "shard", scatter_dimension=0, tiled=True
        ).astype(jnp.float32),
        lax.psum_scatter(
            grad_gains.astype(jnp.bfloat16), "shard", scatter_dimension=0, tiled=True
        ).astype(jnp.float32),
    )
    (
        latent_total,
        query_total,
        keyval_total,
        outproj_total,
        gains_total,
        gateup_total,
        down_total,
    ) = (
        lax.psum_scatter(
            latent_sum.astype(jnp.bfloat16), "rep", scatter_dimension=0, tiled=True
        ).astype(jnp.float32),
        lax.psum_scatter(
            query_sum.astype(jnp.bfloat16), "rep", scatter_dimension=0, tiled=True
        ).astype(jnp.float32),
        lax.psum_scatter(
            keyval_sum.astype(jnp.bfloat16), "rep", scatter_dimension=0, tiled=True
        ).astype(jnp.float32),
        lax.psum_scatter(
            outproj_sum.astype(jnp.bfloat16), "rep", scatter_dimension=0, tiled=True
        ).astype(jnp.float32),
        lax.psum_scatter(
            gains_sum.astype(jnp.bfloat16), "rep", scatter_dimension=0, tiled=True
        ).astype(jnp.float32),
        lax.psum_scatter(gateup_sum, "rep", scatter_dimension=0, tiled=True).astype(jnp.float32),
        lax.psum_scatter(down_sum, "rep", scatter_dimension=0, tiled=True).astype(jnp.float32),
    )
    new_latent = adam_step(
        latent_proj, latent_total, latent_mean, latent_square, D ** (-0.5), decay_rate
    )
    new_query = adam_step(query_up, query_total, query_mean, query_square, QR ** (-0.5), decay_rate)
    new_keyval = adam_step(
        keyval_up, keyval_total, keyval_mean, keyval_square, KR ** (-0.5), decay_rate
    )
    new_outproj = adam_step(
        out_proj,
        outproj_total,
        outproj_mean,
        outproj_square,
        max(H * HD // 512, 1) ** (-0.5),
        decay_rate,
    )
    new_gateup = adam_step(
        gate_up, gateup_total, gateup_mean, gateup_square, D ** (-0.5), decay_rate
    )
    new_down = adam_step(
        down_proj, down_total, down_mean, down_square, max(FF // 32, 1) ** (-0.5), decay_rate
    )
    new_gains = adam_step(norm_gains, gains_total, gains_mean, gains_square, gain_rate, 0.0)
    return (
        block_out,
        input_grad,
        new_latent[0],
        new_latent[1],
        new_latent[2],
        new_query[0],
        new_query[1],
        new_query[2],
        new_keyval[0],
        new_keyval[1],
        new_keyval[2],
        new_outproj[0],
        new_outproj[1],
        new_outproj[2],
        new_gateup[0],
        new_gateup[1],
        new_gateup[2],
        new_down[0],
        new_down[1],
        new_down[2],
        new_gains[0],
        new_gains[1],
        new_gains[2],
    )


def solution(mesh):
    return jax.shard_map(
        per_device,
        mesh=mesh,
        in_specs=(
            P(("shard", "rep"), None),
            P(("shard", "rep"), None),
            P(("shard", "rep"), None),
            P("shard", None),
            P("shard", None),
            P("shard", None),
            P("shard", None),
            P("shard", None),
            P("shard", None),
            P("shard"),
            P(("shard", "rep"), None),
            P(("shard", "rep"), None),
            P(("shard", "rep"), None),
            P(("shard", "rep"), None),
            P(("shard", "rep"), None),
            P(("shard", "rep"), None),
            P(("shard", "rep")),
            P(("shard", "rep"), None),
            P(("shard", "rep"), None),
            P(("shard", "rep"), None),
            P(("shard", "rep"), None),
            P(("shard", "rep"), None),
            P(("shard", "rep"), None),
            P(("shard", "rep")),
        ),
        out_specs=(
            P(("shard", "rep"), None),
            P(("shard", "rep"), None),
            P(("shard", "rep"), None),
            P(("shard", "rep"), None),
            P(("shard", "rep"), None),
            P(("shard", "rep"), None),
            P(("shard", "rep"), None),
            P(("shard", "rep"), None),
            P(("shard", "rep"), None),
            P(("shard", "rep"), None),
            P(("shard", "rep"), None),
            P(("shard", "rep"), None),
            P(("shard", "rep"), None),
            P(("shard", "rep"), None),
            P(("shard", "rep"), None),
            P(("shard", "rep"), None),
            P(("shard", "rep"), None),
            P(("shard", "rep"), None),
            P(("shard", "rep"), None),
            P(("shard", "rep"), None),
            P(("shard", "rep")),
            P(("shard", "rep")),
            P(("shard", "rep")),
        ),
        check_vma=False,
    )
```

profile of v0, /device:TPU:0, one launch (start us, length us, event | category | flops | bytes accessed | tf_op | source)
XLA Modules:
  0.0 2852.8 jit_solution(14076047380873667394)
XLA Ops:
  11.3 9.6 all-gather
  21.8 53.6 %all-gather.8.cloned.1.call-done = bf16[2560,1056]{0,1:T(8,128)(2,1)} async-done(((bf16[640,1056]{0,1:T(8,128)(2,1)}), bf16[2560,1056]{0,1:T(8,128)(2,1)}) %all-gather.8.cloned.1.call-update) | async-done | bytes 5406736 | tf_op jit(solution)/shard_map/all_gather | solution.py:134
  80.0 36.9 %all-gather.12.cloned.1.call-done = bf16[256,5120]{1,0:T(8,128)(2,1)} async-done(((bf16[64,5120]{1,0:T(8,128)(2,1)}), bf16[256,5120]{1,0:T(8,128)(2,1)}) %all-gather.12.cloned.1.call-update) | async-done | bytes 2621456 | tf_op jit(solution)/shard_map/all_gather | solution.py:136
  136.6 49.1 %all-gather.10.cloned.1.call-done = bf16[768,3840]{1,0:T(8,128)(2,1)} async-done(((bf16[192,3840]{1,0:T(8,128)(2,1)}), bf16[768,3840]{1,0:T(8,128)(2,1)}) %all-gather.10.cloned.1.call-update) | async-done | bytes 5898256 | tf_op jit(solution)/shard_map/all_gather | solution.py:135
  194.4 22.6 while.28
  217.0 97.3 %all-gather.14.cloned.1.call-done = bf16[2560,2560]{1,0:T(8,128)(2,1)} async-done(((bf16[640,2560]{1,0:T(8,128)(2,1)}), bf16[2560,2560]{1,0:T(8,128)(2,1)}) %all-gather.14.cloned.1.call-update) | async-done | bytes 13107216 | tf_op jit(solution)/shard_map/all_gather | solution.py:137
  314.3 11.3 multiply_reduce_fusion.3
  325.6 554.2 %all-gather.16.cloned.1.call-done = bf16[2560,12800]{1,0:T(8,128)(2,1)} async-done(((bf16[640,12800]{1,0:T(8,128)(2,1)}), bf16[2560,12800]{1,0:T(8,128)(2,1)}) %all-gather.16.cloned.1.call-update) | async-done | bytes 65536016 | tf_op jit(solution)/shard_map/all_gather | solution.py:141
  879.8 36.3 %fusion.125 = f32[256,12800]{1,0:T(8,128)} fusion(bf16[2560,12800]{1,0:T(8,128)(2,1)} %all-gather.16.cloned.1.call-done, f32[256,2560]{1,0:T(8,128)} %get-tuple-element.337, f32[2560]{0:T(1024)S(1)} %get-tuple-element.332, f32[256]{0:T(256)S(1)} %add_rsqrt_fusion), kind=kOutput, calls=%fused_computation.227 | convolution fusion | flops 16779182080 | bytes 81275904 | tf_op jit(solution)/shard_map/dot_general | solution.py:198
  916.1 256.1 %all-gather.18.cloned.1.call-done = bf16[6400,2560]{1,0:T(8,128)(2,1)} async-done(((bf16[1600,2560]{1,0:T(8,128)(2,1)}), bf16[6400,2560]{1,0:T(8,128)(2,1)}) %all-gather.18.cloned.1.call-update) | async-done | bytes 32768016 | tf_op jit(solution)/shard_map/all_gather | solution.py:142
  1172.2 21.4 multiply_convert_fusion.2
  1193.6 30.7 %multiply_reduce_fusion.1 = (bf16[2560]{0:T(1024)(128)(2,1)}, f32[256]{0:T(256)S(1)}, f32[256,2560]{1,0:T(8,128)}) fusion(f32[256,2560]{1,0:T(8,128)} %get-tuple-element.337, f32[256]{0:T(256)S(1)} %add_rsqrt_fusion, f32[2560]{0:T(1024)S(1)} %get-tuple-element.332, bf16[2560,12800]{1,0:T(8,128)(2,1)} %all-gather.16.cloned.1.call-done, ...), kind=kOutput, calls=%fused_computation.114 | convolution fusion | flops 16794253312 | bytes 77349888 | tf_op jit(solution)/shard_map/tf,df->td/dot_general | solution.py:232
  1229.7 9.4 convolution_convert_fusion.7
  1242.7 47.8 %while.29 = (s32[]{:T(128)}, f32[5,8,256,96]{2,3,1,0:T(8,128)}, f32[5,8,256,96]{2,3,1,0:T(8,128)}, bf16[5,8,256,64]{2,3,1,0:T(8,128)(2,1)}, bf16[5,8,256,96]{2,3...) while((s32[]{:T(128)}, f32[5,8,256,96]{2,3,1,0:T(8,128)}, ...), condition=%wide.region_12.13_spmd.clone, body=%wide.region_10.12_spmd.clone.sunk | while | flops 441513984 | bytes 20363376 | solution.py:274
  1316.4 8.7 copy.120
  1332.7 8.0 convolution_convert_fusion.2
  1342.1 17.0 convolution_convert_fusion.1
  1360.9 28.8 %convolution_convert_fusion = bf16[2560,12800]{1,0:T(8,128)(2,1)} fusion(bf16[256,6400]{1,0:T(8,128)(2,1)} %get-tuple-element.317, bf16[256,6400]{1,0:T(8,128)(2,1)} %get-tuple-element.316, f32[256,2560]{1,0:T(8,128)S(1)} %copy-done, f32[2560]{0:T(1024)S(1)} %get-tuple-element.332, f32[256]{0:T(256)S(1)} %add_rsqrt_fusion), kind=kOutput, calls=%fused_computation.62 | convolution fusion | flops 16825057280 | bytes 74722304 | tf_op jit(solution)/shard_map/td,tf->df/dot_general | solution.py:225
  1390.5 17.3 reduce-scatter.37.cloned.1.call-done
  1407.9 69.9 %reduce-scatter.19.cloned.1.call-done = bf16[192,3840]{1,0:T(8,128)(2,1)} async-done(((bf16[768,3840]{1,0:T(8,128)(2,1)}), bf16[192,3840]{1,0:T(8,128)(2,1)}) %reduce-scatter.19.cloned.1.call-update) | async-done | bytes 1474576 | tf_op jit(solution)/shard_map/reduce_scatter | solution.py:328
  1477.8 128.0 %reduce-scatter.27.cloned.1.call-done = bf16[640,2560]{1,0:T(8,128)(2,1)} async-done(((bf16[2560,2560]{1,0:T(8,128)(2,1)}), bf16[640,2560]{1,0:T(8,128)(2,1)}) %reduce-scatter.27.cloned.1.call-update) | async-done | bytes 3276816 | tf_op jit(solution)/shard_map/reduce_scatter | solution.py:334
  1605.9 285.5 %reduce-scatter.41.cloned.1.call-done = bf16[1600,2560]{1,0:T(8,128)(2,1)} async-done(((bf16[6400,2560]{1,0:T(8,128)(2,1)}), bf16[1600,2560]{1,0:T(8,128)(2,1)}) %reduce-scatter.41.cloned.1.call-update) | async-done | bytes 8192016
  1891.4 549.0 %reduce-scatter.31.cloned.1.call-done = bf16[640,12800]{1,0:T(8,128)(2,1)} async-done(((bf16[2560,12800]{1,0:T(8,128)(2,1)}), bf16[640,12800]{1,0:T(8,128)(2,1)}) %reduce-scatter.31.cloned.1.call-update) | async-done | bytes 16384016 | tf_op jit(solution)/shard_map/reduce_scatter | solution.py:224
  2444.9 7.3 fusion.68
  2452.2 15.0 all-reduce.1
  2467.3 13.6 all-reduce.2
  2488.4 16.6 fusion.56
  2513.9 28.6 %reduce-scatter.21.cloned.1.call-done = bf16[24,3840]{1,0:T(8,128)(2,1)} async-done(((bf16[192,3840]{1,0:T(8,128)(2,1)}), bf16[24,3840]{1,0:T(8,128)(2,1)}) %reduce-scatter.21.cloned.1.call-update) | async-done | bytes 184336 | tf_op jit(solution)/shard_map/reduce_scatter | solution.py:353
  2544.7 39.4 %reduce-scatter.29.cloned.1.call-done = bf16[80,2560]{1,0:T(8,128)(2,1)} async-done(((bf16[640,2560]{1,0:T(8,128)(2,1)}), bf16[80,2560]{1,0:T(8,128)(2,1)}) %reduce-scatter.29.cloned.1.call-update) | async-done | bytes 409616 | tf_op jit(solution)/shard_map/reduce_scatter | solution.py:359
  2587.1 85.8 %reduce-scatter.35.cloned.1.call-done = bf16[200,2560]{1,0:T(8,128)(2,1)} async-done(((bf16[1600,2560]{1,0:T(8,128)(2,1)}), bf16[200,2560]{1,0:T(8,128)(2,1)}) %reduce-scatter.35.cloned.1.call-update) | async-done | bytes 1024016 | tf_op jit(solution)/shard_map/reduce_scatter | solution.py:366
  2679.0 159.1 %reduce-scatter.33.cloned.1.call-done = bf16[80,12800]{1,0:T(8,128)(2,1)} async-done(((bf16[640,12800]{1,0:T(8,128)(2,1)}), bf16[80,12800]{1,0:T(8,128)(2,1)}) %reduce-scatter.33.cloned.1.call-update) | async-done | bytes 2048016 | tf_op jit(solution)/shard_map/reduce_scatter | solution.py:365
  2838.1 7.6 convert_subtract_fusion
  (278 shorter events, 184.9 us)
Async XLA Ops:
  7.2 68.2 %all-gather.8.cloned.1.call-start = ((), (), s32[]{:S(2)}) async-start(), calls=%async_computation.12 | async-start | bytes 6758400 | tf_op jit(solution)/shard_map/all_gather | solution.py:134
  7.9 109.0 %all-gather.12.cloned.1.call-start = ((), (), s32[]{:S(2)}) async-start(), calls=%async_computation.14 | async-start | bytes 3276800 | tf_op jit(solution)/shard_map/all_gather | solution.py:136
  8.7 177.0 %all-gather.10.cloned.1.call-start = ((), (), s32[]{:S(2)}) async-start(), calls=%async_computation.13 | async-start | bytes 7372800 | tf_op jit(solution)/shard_map/all_gather | solution.py:135
  9.4 304.9 %all-gather.14.cloned.1.call-start = ((), (), s32[]{:S(2)}) async-start(), calls=%async_computation.15 | async-start | bytes 16384000 | tf_op jit(solution)/shard_map/all_gather | solution.py:137
  10.0 869.8 %all-gather.16.cloned.1.call-start = ((), (), s32[]{:S(2)}) async-start(), calls=%async_computation.16 | async-start | bytes 81920000 | tf_op jit(solution)/shard_map/all_gather | solution.py:141
  10.6 1161.6 %all-gather.18.cloned.1.call-start = ((), (), s32[]{:S(2)}) async-start(), calls=%async_computation.17 | async-start | bytes 40960000 | tf_op jit(solution)/shard_map/all_gather | solution.py:142
  11.2 1378.6 %reduce-scatter.23.cloned.1.call-start = ((), (), s32[]{:S(2)}) async-start(), calls=%async_computation.20 | async-start | bytes 3276800 | tf_op jit(solution)/shard_map/reduce_scatter | solution.py:331
  20.9 164.8 %copy-start.17 = (f32[768]{0:T(1024)}, f32[768]{0:T(1024)S(1)}, u32[]{:S(2)}) copy-start(f32[768]{0:T(1024)S(1)} %slice.104) | copy-start | bytes 9220
  20.9 96.0 %copy-start.29 = (f32[256]{0:T(256)}, f32[256]{0:T(256)S(1)}, u32[]{:S(2)}) copy-start(f32[256]{0:T(256)S(1)} %slice.109) | copy-start | bytes 3076
  21.0 58.6 %copy-start.43 = (f32[16]{0:T(128)}, f32[16]{0:T(128)S(1)}, u32[]{:S(2)}) copy-start(f32[16]{0:T(128)S(1)} %multiply_power_fusion) | copy-start | bytes 196
  21.2 58.4 %copy-start.37 = (f32[256]{0:T(256)}, f32[256]{0:T(256)S(1)}, u32[]{:S(2)}) copy-start(f32[256]{0:T(256)S(1)} %select_reduce_fusion) | copy-start | bytes 3076
  21.6 58.1 %copy-start.45 = (f32[256]{0:T(256)}, f32[256]{0:T(256)S(1)}, u32[]{:S(2)}) copy-start(f32[256]{0:T(256)S(1)} %add_rsqrt_fusion.3) | copy-start | bytes 3076
  21.7 169.8 %copy-start.22 = (f32[256,16]{0,1:T(8,128)}, f32[256,16]{0,1:T(8,128)S(1)}, u32[]{:S(2)}) copy-start(f32[256,16]{0,1:T(8,128)S(1)} %get-tuple-element.334) | copy-start | bytes 49156
  21.7 169.8 %copy-start.24 = (f32[256,16]{0,1:T(8,128)}, f32[256,16]{0,1:T(8,128)S(1)}, u32[]{:S(2)}) copy-start(f32[256,16]{0,1:T(8,128)S(1)} %get-tuple-element.335) | copy-start | bytes 49156
  21.8 57.9 %copy-start.31 = (f32[2560]{0:T(1024)}, f32[2560]{0:T(1024)S(1)}, u32[]{:S(2)}) copy-start(f32[2560]{0:T(1024)S(1)} %get-tuple-element.333) | copy-start | bytes 30724
  79.7 37.3 %copy-start.3 = (f32[256,1056]{0,1:T(8,128)}, f32[256,1056]{0,1:T(8,128)S(1)}, u32[]{:S(2)}) copy-start(f32[256,1056]{0,1:T(8,128)S(1)} %fusion.86) | copy-start | bytes 3244036
  80.0 36.9 %copy-start.33 = (f32[256]{0:T(256)}, f32[256]{0:T(256)S(1)}, u32[]{:S(2)}) copy-start(f32[256]{0:T(256)S(1)} %add_rsqrt_fusion.1) | copy-start | bytes 3076
  136.6 54.7 %copy-start.35 = (f32[256]{0:T(256)}, f32[256]{0:T(256)S(1)}, u32[]{:S(2)}) copy-start(f32[256]{0:T(256)S(1)} %add_rsqrt_fusion.2) | copy-start | bytes 3076
  1298.1 109.7 %reduce-scatter.37.cloned.1.call-start = ((), (), s32[]{:S(2)}) async-start(), calls=%async_computation.27 | async-start | bytes 7372800
  1325.1 152.7 %reduce-scatter.19.cloned.1.call-start = ((), (), s32[]{:S(2)}) async-start(), calls=%async_computation.18 | async-start | bytes 7372800 | tf_op jit(solution)/shard_map/reduce_scatter | solution.py:328
  1331.0 274.8 %reduce-scatter.27.cloned.1.call-start = ((), (), s32[]{:S(2)}) async-start(), calls=%async_computation.22 | async-start | bytes 16384000 | tf_op jit(solution)/shard_map/reduce_scatter | solution.py:334
  1340.8 550.6 %reduce-scatter.41.cloned.1.call-start = ((), (), s32[]{:S(2)}) async-start(), calls=%async_computation.29 | async-start | bytes 40960000
  1359.1 1081.3 %reduce-scatter.31.cloned.1.call-start = ((), (), s32[]{:S(2)}) async-start(), calls=%async_computation.24 | async-start | bytes 81920000 | tf_op jit(solution)/shard_map/reduce_scatter | solution.py:224
  1389.7 1115.2 %reduce-scatter.25.cloned.1.call-start = ((), (), s32[]{:S(2)}) async-start(), calls=%async_computation.21 | async-start | bytes 737280 | tf_op jit(solution)/shard_map/reduce_scatter | solution.py:356
  1390.5 1117.7 %reduce-scatter.39.cloned.1.call-start = ((), (), s32[]{:S(2)}) async-start(), calls=%async_computation.28 | async-start | bytes 1658880
  1407.8 1134.6 %reduce-scatter.21.cloned.1.call-start = ((), (), s32[]{:S(2)}) async-start(), calls=%async_computation.19 | async-start | bytes 1658880 | tf_op jit(solution)/shard_map/reduce_scatter | solution.py:353
  1477.8 1106.3 %reduce-scatter.29.cloned.1.call-start = ((), (), s32[]{:S(2)}) async-start(), calls=%async_computation.23 | async-start | bytes 3686400 | tf_op jit(solution)/shard_map/reduce_scatter | solution.py:359
  1605.8 1067.1 %reduce-scatter.35.cloned.1.call-start = ((), (), s32[]{:S(2)}) async-start(), calls=%async_computation.26 | async-start | bytes 9216000 | tf_op jit(solution)/shard_map/reduce_scatter | solution.py:366
  1891.4 946.7 %reduce-scatter.33.cloned.1.call-start = ((), (), s32[]{:S(2)}) async-start(), calls=%async_computation.25 | async-start | bytes 18432000 | tf_op jit(solution)/shard_map/reduce_scatter | solution.py:365
  2511.0 73.1 %copy-start.15 = (bf16[80,2560]{1,0:T(8,128)(2,1)S(1)}, bf16[80,2560]{1,0:T(8,128)(2,1)}, u32[]{:S(2)}) copy-start(bf16[80,2560]{1,0:T(8,128)(2,1)} %param.41) | copy-start | bytes 1228804
  2511.0 73.1 %copy-start.16 = (bf16[80,2560]{1,0:T(8,128)(2,1)S(1)}, bf16[80,2560]{1,0:T(8,128)(2,1)}, u32[]{:S(2)}) copy-start(bf16[80,2560]{1,0:T(8,128)(2,1)} %param.48) | copy-start | bytes 1228804
  2587.1 251.0 %copy-start.13 = (bf16[80,12800]{1,0:T(8,128)(2,1)S(1)}, bf16[80,12800]{1,0:T(8,128)(2,1)}, u32[]{:S(2)}) copy-start(bf16[80,12800]{1,0:T(8,128)(2,1)} %param.42) | copy-start | bytes 6144004
  (37 other events, 221.4 us)
Sparse Core Ops, SparseCore 0:
  9.9 65.4 all-gather.7
  77.2 39.6 all-gather.11
  118.8 66.8 all-gather.9
  187.4 126.8 all-gather.13
  316.0 563.7 all-gather.15
  881.5 290.6 all-gather.17
  1298.2 39.5 reduce-scatter.22
  1340.9 66.8 reduce-scatter.36
  1410.8 66.8 reduce-scatter.18
  1480.8 124.9 reduce-scatter.26
  1609.0 282.2 reduce-scatter.40
  1894.7 545.6 reduce-scatter.30
  2442.7 31.2 reduce-scatter.24
  2476.1 32.0 reduce-scatter.38
  2510.3 32.0 reduce-scatter.20
  2544.6 39.4 reduce-scatter.28
  2586.4 86.5 reduce-scatter.34
  2675.2 162.8 reduce-scatter.32
where the time goes:
time: 2860 us; the launch traced here: 2850 us
  waiting for transfers between devices  2420 us (85%)
  matrix products  284 us (10%)
  other arithmetic  51.1 us (2%)
  local copies, waits for them, and re-layouts  46.3 us (2%)
  blocking collectives  38.2 us (1%)
    all_gather x1, waiting for transfers between devices, per_device(): lax.all_gather(gate_up, 'shard', axis=0, tiled=True)  554 us
    reduce_scatter x1, waiting for transfers between devices, per_device(): lax.psum_scatter(jnp.einsum('td,tf->df', normed_mlp, grad_gu, preferred_e...  549 us
    unnamed x21, waiting for transfers between devices  309 us
    all_gather x1, waiting for transfers between devices, per_device(): lax.all_gather(down_proj, 'shard', axis=0, tiled=True)  256 us
    reduce_scatter x1, waiting for transfers between devices, per_device(): lax.psum_scatter(gateup_sum, 'rep', scatter_dimension=0, tiled=True)  159 us
    reduce_scatter x1, waiting for transfers between devices, per_device(): lax.psum_scatter(grad_out.astype(jnp.bfloat16), 'shard', scatter_dimensio...  128 us
    all_gather x1, waiting for transfers between devices, per_device(): lax.all_gather(out_proj, 'shard', axis=0, tiled=True)  97.3 us
    reduce_scatter x1, waiting for transfers between devices, per_device(): lax.psum_scatter(down_sum, 'rep', scatter_dimension=0, tiled=True)  85.8 us
  transfers between devices with their start and end apart: 18, of which 16 were waited for; matrix products, arithmetic and copies ran while one was open for 8% of the time, Pallas kernels for 0%

commit v1 on v0

v1 whole, which is shorter than its diff:
```python
import functools
import math

import jax
import jax.numpy as jnp
from jax import lax
from jax.experimental import pallas as pl
from jax.experimental.pallas import tpu as pltpu
from jax.sharding import PartitionSpec as P

D = 2560
H = 40
HD = 64
RD = 32
QR = 768
KR = 256
FF = 6400
STEP = 10


norm_eps = 1e-05
residual_scale = 1.4 / math.sqrt(62.0)
beta_one = 0.9
beta_two = 0.95
adam_eps = 1e-08
decay_rate = 0.1
gain_rate = 0.8


def inverse_rms(values):
    return lax.rsqrt(jnp.mean(values * values, axis=-1, keepdims=True) + norm_eps)


def norm_back(incoming, operand, inv_scale):
    return inv_scale * (
        incoming
        - operand * inv_scale * inv_scale * jnp.mean(incoming * operand, axis=-1, keepdims=True)
    )


def rotation_rates():
    rates = [0.0] * LANES
    for i in range(RD // 2):
        rates[HD + i] = rates[HD + RD // 2 + i] = 10000.0 ** (-2.0 * i / RD)
    return jnp.array([rates], jnp.float32)


def own_rows(weight, gradient):
    count = gradient.shape[0]
    start = lax.axis_index("rep") * count
    return lax.dynamic_slice_in_dim(weight, start, count, 0)


def adam_step(weight, gradient, mean_old, square_old, step_rate, decay_factor):
    weight_f = own_rows(weight, gradient).astype(jnp.float32)
    gradient = gradient.astype(jnp.float32)
    mean_new = beta_one * mean_old.astype(jnp.float32) + (1.0 - beta_one) * gradient
    square_new = beta_two * square_old.astype(jnp.float32) + (1.0 - beta_two) * gradient * gradient
    ratio = (
        mean_new
        / (1.0 - beta_one**STEP)
        / (jnp.sqrt(square_new / (1.0 - beta_two**STEP)) + adam_eps)
    )
    updated = weight_f - step_rate * (ratio + decay_factor * weight_f)
    return (updated, mean_new, square_new)


TILE = 256
TAIL = 128
LANES = 128
LATENT = QR + KR + LANES
score_scale = (HD + RD) ** (-0.5)
VMEM_BYTES = 48 * 1024 * 1024


def across(a, b):
    return lax.dot_general(a, b, (((1,), (1,)), ((), ())), preferred_element_type=jnp.float32)


def along(a, b):
    return lax.dot_general(a, b, (((1,), (0,)), ((), ())), preferred_element_type=jnp.float32)


def mlp_kernel(group, tiles, tail, rows_d, order_ref, normed_ref, branch_ref, *refs):
    blocks = refs[:group]
    tails = refs[group : 2 * group]
    down_ref, down_tail_ref = refs[2 * group : 2 * group + 2]
    out_refs = refs[-9:]
    act_ref, grad_ref, sum_ref, back_ref, whole, whole_tail, down_wide, sum_acc, back_acc = out_refs
    step = pl.program_id(0)
    bf16 = jnp.bfloat16

    for j in range(group):
        start = pl.multiple_of(order_ref[j] * rows_d, 16)
        whole[pl.ds(start, rows_d), :] = blocks[j][...]

    def part(weights, down, width):
        both = along(normed_ref[...], weights)
        gate = both[:, :width]
        up = both[:, width:]
        sigmoid = 1.0 / (1.0 + jnp.exp(-gate))
        silu = gate * sigmoid
        act = (silu * up).astype(bf16)
        grad_act = across(branch_ref[...], down)
        grad_gate = grad_act * up * sigmoid * (1.0 + gate * (1.0 - sigmoid))
        grad_up = grad_act * silu
        grad = jnp.concatenate([grad_gate.astype(bf16), grad_up.astype(bf16)], axis=1)
        return act, grad, along(act, down), across(grad, weights)

    act, grad, term, back = part(whole[...], down_ref[...], TILE)
    first = pl.multiple_of(step * TILE, TILE)
    act_ref[:, pl.ds(first, TILE)] = act
    grad_ref[:, pl.ds(pl.multiple_of(2 * first, 2 * TILE), 2 * TILE)] = grad

    @pl.when(step == 0)
    def _():
        sum_acc[...] = term
        back_acc[...] = back

    @pl.when(step > 0)
    def _():
        sum_acc[...] += term
        back_acc[...] += back

    @pl.when(step == tiles - 1)
    def _():
        for j in range(group):
            start = pl.multiple_of(order_ref[j] * rows_d, 16)
            whole_tail[pl.ds(start, rows_d), :] = tails[j][...]
        down_wide[...] = jnp.zeros_like(down_wide)
        down_wide[:tail, :] = down_tail_ref[...]
        act, grad, term, back = part(whole_tail[...], down_wide[...], TAIL)
        act_ref[:, tiles * TILE :] = act
        grad_ref[:, 2 * tiles * TILE :] = grad
        sum_ref[...] = (sum_acc[...] + term).astype(bf16)
        back_ref[...] = (back_acc[...] + back).astype(bf16)


def mlp_part(order, normed, branch, own, gathered, down, earlier, index, group):
    tokens, width = normed.shape
    hidden = down.shape[0]
    tiles = hidden // TILE
    tail = hidden - tiles * TILE
    rows_d = width // group
    bf16 = jnp.bfloat16
    f32 = jnp.float32
    fixed = lambda t: (0, 0)
    weights = [own] + [gathered] * (group - 1)
    return pl.pallas_call(
        functools.partial(mlp_kernel, group, tiles, tail, rows_d),
        grid=(tiles,),
        in_specs=[
            pl.BlockSpec(memory_space=pltpu.SMEM),
            pl.BlockSpec((tokens, width), fixed),
            pl.BlockSpec((tokens, width), fixed),
        ]
        + [pl.BlockSpec((rows_d, 2 * TILE), lambda t: (0, t))]
        + [
            pl.BlockSpec((rows_d, 2 * TILE), lambda t, j=j: (0, j * tiles + t))
            for j in range(group - 1)
        ]
        + [pl.BlockSpec((rows_d, 2 * TAIL), lambda t: (0, tiles * TILE // TAIL))]
        + [
            pl.BlockSpec(
                (rows_d, 2 * TAIL), lambda t, j=j: (0, (group - 1) * tiles * TILE // TAIL + j)
            )
            for j in range(group - 1)
        ]
        + [
            pl.BlockSpec((TILE, width), lambda t: (t, 0)),
            pl.BlockSpec((tail, width), lambda t: (tiles * TILE // tail, 0)),
        ]
        + [pl.BlockSpec(memory_space=pl.ANY)] * len(earlier),
        out_specs=[
            pl.BlockSpec((tokens, tiles * TILE + TAIL), lambda t: (index, 0)),
            pl.BlockSpec((tokens, 2 * (tiles * TILE + TAIL)), lambda t: (index, 0)),
            pl.BlockSpec((tokens, width), fixed),
            pl.BlockSpec((tokens, width), fixed),
        ],
        out_shape=[
            jax.ShapeDtypeStruct((group * tokens, tiles * TILE + TAIL), bf16),
            jax.ShapeDtypeStruct((group * tokens, 2 * (tiles * TILE + TAIL)), bf16),
            jax.ShapeDtypeStruct((tokens, width), bf16),
            jax.ShapeDtypeStruct((tokens, width), bf16),
        ],
        scratch_shapes=[
            pltpu.VMEM((width, 2 * TILE), bf16),
            pltpu.VMEM((width, 2 * TAIL), bf16),
            pltpu.VMEM((TAIL, width), bf16),
            pltpu.VMEM((tokens, width), f32),
            pltpu.VMEM((tokens, width), f32),
        ],
        input_output_aliases={5 + 2 * group + i: i for i in range(len(earlier))},
        compiler_params=pltpu.CompilerParams(vmem_limit_bytes=VMEM_BYTES),
        cost_estimate=pl.CostEstimate(
            flops=12 * tokens * width * hidden,
            bytes_accessed=6 * width * hidden + 8 * tokens * width,
            transcendentals=tokens * hidden,
        ),
        name="mlp_part",
    )(order, normed, branch, *weights, *weights, down, down, *earlier)


def layer_kernel(group, base, tiles, tail, rows_d, shares, last, order_ref, *refs):
    normed_in = refs[:group]
    top_in = refs[group : 2 * group]
    at = 2 * group
    blocks = refs[at : at + group]
    at += group
    if last:
        tails = refs[at : at + group]
        at += group
        down_ref, down_tail_ref, act_old, acc_in = refs[at : at + 4]
        at += 4
    else:
        down_ref = refs[at]
        at += 1
    act_out, grad_out, back_out = refs[at : at + 3]
    normed, turned, branch, whole, acc, stage, act_stage, in_sems, out_sems, back_sem = refs[
        at + 3 : at + 13
    ]
    if last:
        whole_tail, down_wide, tail_stage, tail_act, tail_sems = refs[at + 13 :]
    bf16 = jnp.bfloat16
    f32 = jnp.float32
    step = pl.program_id(0)
    slot = lax.rem(step, 2)
    tokens = normed_in[0].shape[0]
    width = normed.shape[1]
    rows = rows_d // shares

    def arrivals():
        copies = []
        for j in range(group):
            copies.append(
                pltpu.make_async_copy(
                    normed_in[j], normed.at[pl.ds(j * tokens, tokens), :], in_sems.at[j]
                )
            )
            copies.append(
                pltpu.make_async_copy(
                    top_in[j], branch.at[pl.ds(j * tokens, tokens), :], in_sems.at[group + j]
                )
            )
        return copies

    @pl.when(step == 0)
    def _():
        copies = arrivals()
        for copy in copies:
            copy.start()
        if last:
            pltpu.make_async_copy(acc_in, acc, back_sem).start()
        else:
            acc[...] = jnp.zeros_like(acc)
        for j in range(group):
            at = pl.ds(j * tokens, tokens)
            copies[2 * j].wait()
            turned[:, j * tokens : (j + 1) * tokens] = normed[at, :].T
            copies[2 * j + 1].wait()
            branch[at, :] = (residual_scale * branch[at, :].astype(f32)).astype(bf16)
        if last:
            pltpu.make_async_copy(acc_in, acc, back_sem).wait()

    for j in range(group):
        start = pl.multiple_of(order_ref[j] * rows_d, 16)
        whole[pl.ds(start, rows_d), :] = blocks[j][...]

    def part(weights_ref, down, wide, act_to, grad_to):
        both = along(normed[...], weights_ref[...])
        gate = both[:, :wide]
        up = both[:, wide:]
        sigmoid = 1.0 / (1.0 + jnp.exp(-gate))
        silu = gate * sigmoid
        act_to[...] = (silu * up).astype(bf16)
        grad_act = across(branch[...], down)
        grad_gate = grad_act * up * sigmoid * (1.0 + gate * (1.0 - sigmoid))
        grad_up = grad_act * silu
        grad = jnp.concatenate([grad_gate.astype(bf16), grad_up.astype(bf16)], axis=1)
        cut = 512
        for c in range(width // cut):
            here = slice(c * cut, (c + 1) * cut)
            acc[:, here] += across(grad, weights_ref[here, :])
        for g in range(group):
            result = along(turned[g * rows_d : (g + 1) * rows_d, :], grad).astype(bf16)
            for r in range(shares):
                grad_to[r, g] = result[r * rows : (r + 1) * rows, :]

    def leaving(index, slot_index):
        first = pl.multiple_of((base + index) * TILE, TILE)
        return (
            pltpu.make_async_copy(
                act_stage.at[slot_index],
                act_out.at[:, pl.ds(first, TILE)],
                out_sems.at[0, slot_index],
            ),
            pltpu.make_async_copy(
                stage.at[slot_index],
                grad_out.at[:, :, :, pl.ds(pl.multiple_of(index * 2 * TILE, 2 * TILE), 2 * TILE)],
                out_sems.at[1, slot_index],
            ),
        )

    @pl.when(step >= 2)
    def _():
        for copy in leaving(step - 2, slot):
            copy.wait()

    part(whole, down_ref[...], TILE, act_stage.at[slot], stage.at[slot])
    for copy in leaving(step, slot):
        copy.start()

    @pl.when(step == tiles - 1)
    def _():
        if last:
            for j in range(group):
                start = pl.multiple_of(order_ref[j] * rows_d, 16)
                whole_tail[pl.ds(start, rows_d), :] = tails[j][...]
            down_wide[...] = jnp.zeros_like(down_wide)
            down_wide[:tail, :] = down_tail_ref[...]
            part(whole_tail, down_wide[...], TAIL, tail_act, tail_stage)
            final = [
                pltpu.make_async_copy(
                    tail_act, act_out.at[:, pl.ds((base + tiles) * TILE, TAIL)], tail_sems.at[0]
                ),
                pltpu.make_async_copy(
                    tail_stage,
                    grad_out.at[:, :, :, pl.ds(2 * tiles * TILE, 2 * TAIL)],
                    tail_sems.at[1],
                ),
            ]
            normed[...] = acc[...].astype(bf16)
            final.append(pltpu.make_async_copy(normed, back_out, back_sem))
        else:
            final = [pltpu.make_async_copy(acc, back_out, back_sem)]
        for copy in final:
            copy.start()
        for k in range(max(tiles - 2, 0), tiles):
            for copy in leaving(k, k % 2):
                copy.wait()
        for copy in final:
            copy.wait()


def layer_part(order, normed, top, own, gathered, down, earlier, tiles_from, tiles, group, shares):
    tokens, width = normed[0].shape
    hidden = down.shape[0]
    all_tiles = hidden // TILE
    tail = hidden - all_tiles * TILE
    rows_d = width // group
    rows = rows_d // shares
    bf16 = jnp.bfloat16
    f32 = jnp.float32
    last = earlier is not None
    total = group * tokens
    once = pl.Buffered(1)
    any_spec = pl.BlockSpec(memory_space=pl.ANY)
    weights = [own] + [gathered] * (group - 1)
    in_specs = [pl.BlockSpec(memory_space=pltpu.SMEM)] + [any_spec] * (2 * group)
    in_specs += [pl.BlockSpec((rows_d, 2 * TILE), lambda t: (0, tiles_from + t))]
    in_specs += [
        pl.BlockSpec((rows_d, 2 * TILE), lambda t, j=j: (0, j * all_tiles + tiles_from + t))
        for j in range(group - 1)
    ]
    inputs = [order] + normed + top + weights
    scratch = [
        pltpu.VMEM((total, width), bf16),
        pltpu.VMEM((width, total), bf16),
        pltpu.VMEM((total, width), bf16),
        pltpu.VMEM((width, 2 * TILE), bf16),
        pltpu.VMEM((total, width), f32),
        pltpu.VMEM((2, shares, group, rows, 2 * TILE), bf16),
        pltpu.VMEM((2, total, TILE), bf16),
        pltpu.SemaphoreType.DMA((2 * group,)),
        pltpu.SemaphoreType.DMA((2, 2)),
        pltpu.SemaphoreType.DMA,
    ]
    cols = 2 * tiles * TILE
    aliases = {}
    if last:
        first_tail = all_tiles * TILE // TAIL
        in_specs += [
            pl.BlockSpec((rows_d, 2 * TAIL), lambda t: (0, first_tail), pipeline_mode=once)
        ]
        in_specs += [
            pl.BlockSpec(
                (rows_d, 2 * TAIL),
                lambda t, j=j: (0, (group - 1) * first_tail + j),
                pipeline_mode=once,
            )
            for j in range(group - 1)
        ]
        inputs += weights
        cols += 2 * TAIL
    in_specs.append(pl.BlockSpec((TILE, width), lambda t: (tiles_from + t, 0)))
    inputs.append(down)
    if last:
        in_specs.append(
            pl.BlockSpec(
                (tail, width), lambda t: (all_tiles * TILE // tail, 0), pipeline_mode=once
            )
        )
        inputs.append(down)
        in_specs += [any_spec, any_spec]
        aliases = {len(inputs): 0}
        inputs += [earlier[0], earlier[2]]
        scratch += [
            pltpu.VMEM((width, 2 * TAIL), bf16),
            pltpu.VMEM((TAIL, width), bf16),
            pltpu.VMEM((shares, group, rows, 2 * TAIL), bf16),
            pltpu.VMEM((total, TAIL), bf16),
            pltpu.SemaphoreType.DMA((2,)),
        ]
    part_hidden = tiles * TILE + (tail if last else 0)
    return pl.pallas_call(
        functools.partial(
            layer_kernel, group, tiles_from, tiles, tail, rows_d, shares, last
        ),
        grid=(tiles,),
        in_specs=in_specs,
        out_specs=[any_spec] * 3,
        out_shape=[
            jax.ShapeDtypeStruct((total, all_tiles * TILE + TAIL), bf16),
            jax.ShapeDtypeStruct((shares, group, rows, cols), bf16),
            jax.ShapeDtypeStruct((total, width), bf16 if last else f32),
        ],
        scratch_shapes=scratch,
        input_output_aliases=aliases,
        compiler_params=pltpu.CompilerParams(vmem_limit_bytes=61 * 1024 * 1024),
        cost_estimate=pl.CostEstimate(
            flops=14 * total * width * part_hidden,
            bytes_accessed=12 * width * part_hidden + 16 * total * width,
            transcendentals=total * part_hidden,
        ),
        name="layer_part",
    )(*inputs)


def down_grad_kernel(group, tokens, act_ref, *refs):
    top = refs[:group]
    out_ref, whole = refs[group:]

    @pl.when(pl.program_id(0) == 0)
    def _():
        for j in range(group):
            whole[j * tokens : (j + 1) * tokens, :] = (
                residual_scale * top[j][...].astype(jnp.float32)
            ).astype(jnp.bfloat16)

    out_ref[...] = along(act_ref[...].T, whole[...]).astype(jnp.bfloat16)


def down_grad(act_all, top_parts, hidden, group):
    tokens, width = top_parts[0].shape
    tiles = (hidden + TILE - 1) // TILE
    return pl.pallas_call(
        functools.partial(down_grad_kernel, group, tokens),
        grid=(tiles,),
        in_specs=[pl.BlockSpec((group * tokens, TILE), lambda t: (0, t))]
        + [pl.BlockSpec((tokens, width), lambda t: (0, 0))] * group,
        out_specs=pl.BlockSpec((TILE, width), lambda t: (t, 0)),
        out_shape=jax.ShapeDtypeStruct((hidden, width), jnp.bfloat16),
        scratch_shapes=[pltpu.VMEM((group * tokens, width), jnp.bfloat16)],
        compiler_params=pltpu.CompilerParams(vmem_limit_bytes=VMEM_BYTES),
        cost_estimate=pl.CostEstimate(
            flops=2 * group * tokens * width * hidden,
            bytes_accessed=2 * width * hidden + 2 * group * tokens * (width + hidden),
            transcendentals=0,
        ),
        name="down_grad",
    )(act_all, *top_parts)


def lane_index(rows):
    return lax.broadcasted_iota(jnp.int32, (rows, LANES), 1)


def turn(values, table_ref, sign):
    ahead = pltpu.roll(values, LANES - RD // 2, 1)
    behind = pltpu.roll(values, RD // 2, 1)
    return values * table_ref[0] + sign * (ahead * table_ref[1] + behind * table_ref[2])


def seg_column(seg_ref):
    return seg_ref[...].T[:, :1]


def causal_mask(seg_ref):
    tokens = seg_ref.shape[1]
    row = lax.broadcasted_iota(jnp.int32, (tokens, tokens), 0)
    col = lax.broadcasted_iota(jnp.int32, (tokens, tokens), 1)
    return (seg_column(seg_ref) == seg_ref[:1, :]) & (col <= row)


def softmax_rows(query, key, allowed):
    scores = across(query, key) * score_scale
    masked = jnp.where(allowed, scores, -1e30)
    exponent = jnp.exp(masked - jnp.max(masked, axis=1, keepdims=True))
    return exponent * (1.0 / jnp.sum(exponent, axis=1, keepdims=True))


def key_lanes(keyval, latent_ref, lane):
    return jnp.where(lane < HD, keyval, latent_ref[:, QR + KR :])


def attend_kernel(
    heads,
    latent_ref,
    table_ref,
    seg_ref,
    query_w_ref,
    keyval_w_ref,
    out_w_ref,
    term_ref,
    query_ref,
    keyval_ref,
    mixed_ref,
):
    bf16 = jnp.bfloat16
    tokens = latent_ref.shape[0]
    lane = lane_index(tokens)
    allowed = causal_mask(seg_ref)
    query = along(latent_ref[:, :QR], query_w_ref[...])
    keyval_ref[...] = along(latent_ref[:, QR : QR + KR], keyval_w_ref[...]).astype(bf16)
    even = None
    for h in range(heads):
        at = slice(h * LANES, (h + 1) * LANES)
        query_h = turn(query[:, at], table_ref, 1.0).astype(bf16)
        query_ref[:, at] = query_h
        keyval_h = keyval_ref[:, at]
        probs = softmax_rows(query_h, key_lanes(keyval_h, latent_ref, lane), allowed).astype(bf16)
        mixed = along(probs, keyval_h)
        if h % 2 == 0:
            even = pltpu.roll(mixed, HD, 1)
            if h == heads - 1:
                mixed_ref[:, h * HD :] = even[:, :HD].astype(bf16)
        else:
            mixed_ref[:, (h - 1) * HD : (h + 1) * HD] = jnp.where(lane < HD, even, mixed).astype(
                bf16
            )
    term_ref[...] = along(mixed_ref[...], out_w_ref[...]).astype(bf16)


def nth(array, index):
    return pl.BlockSpec((None,) + array.shape[1:], lambda i: (index,) + (0,) * (array.ndim - 1))


def entire(array):
    return pl.BlockSpec(array.shape, lambda i: (0,) * array.ndim)


def attend(index, latent, table, seg, query_w, keyval_w, out_w):
    tokens = latent.shape[1]
    heads = query_w.shape[1] // LANES
    width = out_w.shape[1]
    bf16 = jnp.bfloat16
    return pl.pallas_call(
        functools.partial(attend_kernel, heads),
        grid=(1,),
        out_specs=[
            pl.BlockSpec((tokens, cols), lambda i: (0, 0))
            for cols in (width, heads * LANES, heads * LANES, heads * HD)
        ],
        in_specs=[nth(array, index) for array in (latent, table, seg)]
        + [entire(array) for array in (query_w, keyval_w, out_w)],
        out_shape=[
            jax.ShapeDtypeStruct((tokens, width), bf16),
            jax.ShapeDtypeStruct((tokens, heads * LANES), bf16),
            jax.ShapeDtypeStruct((tokens, heads * LANES), bf16),
            jax.ShapeDtypeStruct((tokens, heads * HD), bf16),
        ],
        compiler_params=pltpu.CompilerParams(vmem_limit_bytes=VMEM_BYTES),
        cost_estimate=pl.CostEstimate(
            flops=2 * tokens * (heads * LANES * (QR + KR + 2 * tokens) + heads * HD * width),
            bytes_accessed=2 * (heads * LANES * (QR + KR) + heads * HD * width + tokens * width),
            transcendentals=heads * tokens * tokens,
        ),
        name="attend",
    )(latent, table, seg, query_w, keyval_w, out_w)


def attend_back_kernel(
    heads,
    grad_ref,
    query_ref,
    keyval_ref,
    latent_ref,
    table_ref,
    seg_ref,
    query_w_ref,
    keyval_w_ref,
    out_w_ref,
    term_ref,
    grad_query_ref,
    grad_keyval_ref,
):
    bf16 = jnp.bfloat16
    f32 = jnp.float32
    tokens = latent_ref.shape[0]
    lane = lane_index(tokens)
    allowed = causal_mask(seg_ref)
    grad_mixed = across(grad_ref[...], out_w_ref[...])
    grad_rope = jnp.zeros((tokens, LANES), f32)
    for h in range(heads):
        at = slice(h * LANES, (h + 1) * LANES)
        query_h = query_ref[:, at]
        keyval_h = keyval_ref[:, at]
        key_h = key_lanes(keyval_h, latent_ref, lane)
        probs = softmax_rows(query_h, key_h, allowed)
        if h % 2 == 0:
            if h == heads - 1:
                one = jnp.concatenate([grad_mixed[:, h * HD :]] * 2, axis=1)
            else:
                pair = grad_mixed[:, h * HD : (h + 2) * HD]
                one = pltpu.roll(pair, HD, 1)
        else:
            one = pair
        value_grad = jnp.where(lane >= HD, one, 0.0).astype(bf16)
        turned = probs.astype(bf16).T
        grad_values = along(turned, value_grad)
        grad_probs = across(value_grad, keyval_h)
        delta = jnp.sum(probs * grad_probs, axis=1, keepdims=True)
        grad_scores = (probs * (grad_probs - delta)).astype(bf16)
        grad_q = along(grad_scores, key_h) * score_scale
        grad_k = along(grad_scores.T, query_h) * score_scale
        grad_query_ref[:, at] = turn(grad_q, table_ref, -1.0).astype(bf16)
        grad_keyval_ref[:, at] = jnp.where(lane < HD, grad_k, grad_values).astype(bf16)
        grad_rope = grad_rope + grad_k
    rope = jnp.where(lane >= HD, turn(grad_rope, table_ref, -1.0), 0.0)
    term_ref[:, :QR] = across(grad_query_ref[...], query_w_ref[...]).astype(bf16)
    term_ref[:, QR : QR + KR] = across(grad_keyval_ref[...], keyval_w_ref[...]).astype(bf16)
    term_ref[:, QR + KR :] = rope.astype(bf16)


def attend_back(
    index, grad, query, keyval, latent, table, seg, query_w, keyval_w, out_w
):
    tokens = latent.shape[1]
    heads = query_w.shape[1] // LANES
    width = out_w.shape[1]
    bf16 = jnp.bfloat16
    return pl.pallas_call(
        functools.partial(attend_back_kernel, heads),
        grid=(1,),
        out_specs=[
            pl.BlockSpec((tokens, cols), lambda i: (0, 0))
            for cols in (LATENT, heads * LANES, heads * LANES)
        ],
        in_specs=[entire(array) for array in (grad, query, keyval)]
        + [nth(array, index) for array in (latent, table, seg)]
        + [entire(array) for array in (query_w, keyval_w, out_w)],
        out_shape=[
            jax.ShapeDtypeStruct((tokens, LATENT), bf16),
            jax.ShapeDtypeStruct((tokens, heads * LANES), bf16),
            jax.ShapeDtypeStruct((tokens, heads * LANES), bf16),
        ],
        compiler_params=pltpu.CompilerParams(vmem_limit_bytes=VMEM_BYTES),
        cost_estimate=pl.CostEstimate(
            flops=2 * tokens * (heads * LANES * (QR + KR + 5 * tokens) + heads * HD * width),
            bytes_accessed=2 * (heads * LANES * (QR + KR) + heads * HD * width + tokens * width),
            transcendentals=heads * tokens * tokens,
        ),
        name="attend_back",
    )(grad, query, keyval, latent, table, seg, query_w, keyval_w, out_w)


def token_grad_kernel(count, *refs):
    left = refs[:count]
    right = refs[count : 2 * count]
    out_ref, turned, whole = refs[2 * count :]
    tokens = left[0].shape[0]
    for j in range(count):
        turned[:, j * tokens : (j + 1) * tokens] = left[j][...].T
        whole[j * tokens : (j + 1) * tokens, :] = right[j][...]
    out_ref[...] = along(turned[...], whole[...]).astype(jnp.bfloat16)


def token_grad(left, right, first, rows, name):
    count = len(right)
    tokens, cols = right[0].shape
    at = first // rows
    if isinstance(left, list):
        left_specs = [pl.BlockSpec((tokens, rows), lambda i: (0, at))] * count
    else:
        left_specs = [
            pl.BlockSpec((None, tokens, rows), lambda i, j=j: (j, 0, at)) for j in range(count)
        ]
        left = [left] * count
    return pl.pallas_call(
        functools.partial(token_grad_kernel, count),
        grid=(1,),
        in_specs=left_specs + [pl.BlockSpec((tokens, cols), lambda i: (0, 0))] * count,
        out_specs=pl.BlockSpec((rows, cols), lambda i: (0, 0)),
        out_shape=jax.ShapeDtypeStruct((rows, cols), jnp.bfloat16),
        scratch_shapes=[
            pltpu.VMEM((rows, count * tokens), jnp.bfloat16),
            pltpu.VMEM((count * tokens, cols), jnp.bfloat16),
        ],
        compiler_params=pltpu.CompilerParams(vmem_limit_bytes=VMEM_BYTES),
        cost_estimate=pl.CostEstimate(
            flops=2 * count * tokens * rows * cols,
            bytes_accessed=2 * (rows * cols + count * tokens * (rows + cols)),
            transcendentals=0,
        ),
        name=name,
    )(*left, *right)


MESH = pl.DeviceIdType.MESH


def partner(me, distance):
    bit = 1
    while bit <= distance:
        if distance & bit:
            me = me + bit - 2 * bit * lax.rem(lax.div(me, bit), 2)
        bit *= 2
    return me


def greet(peers, count):
    barrier = pltpu.get_barrier_semaphore()
    for peer in peers:
        pl.semaphore_signal(barrier, inc=1, device_id=peer, device_id_type=MESH)
    pl.semaphore_wait(barrier, count)


def send(src, dst, sems, index, peer):
    copy = pltpu.make_async_remote_copy(
        src_ref=src,
        dst_ref=dst,
        send_sem=sems.at[0, index],
        recv_sem=sems.at[1, index],
        device_id=peer,
        device_id_type=MESH,
    )
    copy.start()
    return copy


def tile_format(gate, up, store, tiles, tail):
    bf16 = jnp.bfloat16
    for t in range(tiles):
        store(2 * t * TILE, gate[:, t * TILE : (t + 1) * TILE].astype(bf16))
        store((2 * t + 1) * TILE, up[:, t * TILE : (t + 1) * TILE].astype(bf16))
    lane = lax.broadcasted_iota(jnp.int32, (gate.shape[0], TAIL), 1)
    for second, values in enumerate((gate, up)):
        last = values[:, tiles * TILE : tiles * TILE + TAIL]
        store(
            2 * tiles * TILE + second * TAIL, jnp.where(lane < tail, last, 0.0).astype(bf16)
        )


def head_table(seg_ref, rates_ref, table_ref):
    tokens = seg_ref.shape[1]
    row = lax.broadcasted_iota(jnp.int32, (tokens, tokens), 0)
    col = lax.broadcasted_iota(jnp.int32, (tokens, tokens), 1)
    before = (seg_column(seg_ref) == seg_ref[:1, :]) & (col < row)
    position = jnp.sum(jnp.where(before, 1.0, 0.0), axis=1, keepdims=True)
    angles = position * rates_ref[...]
    sine = jnp.sin(angles)
    lane = lane_index(tokens)
    middle = HD + RD // 2
    end = HD + RD
    table_ref[0] = jnp.where(lane < end, jnp.cos(angles), 0.0)
    table_ref[1] = jnp.where((lane >= HD) & (lane < middle), -sine, 0.0)
    table_ref[2] = jnp.where((lane >= middle) & (lane < end), sine, 0.0)


def share_small(group, me, peers, gains_ref, seg_ref, gains_all_ref, segs_ref, sems):
    mine = pl.ds(pl.multiple_of(me * 8, 8), 8)
    gains_all_ref[mine, :] = gains_ref[...]
    segs_ref[0] = seg_ref[...]
    copies = []
    for j in range(1, group):
        copies.append(send(gains_ref, gains_all_ref.at[mine, :], sems, 2 * (j - 1), peers[j - 1]))
        copies.append(send(seg_ref, segs_ref.at[j], sems, 2 * (j - 1) + 1, peers[j - 1]))
    return copies


def small_kernel(
    group, gains_ref, seg_ref, rates_ref, gains_all_ref, segs_ref, table_ref, small_sems
):
    me = lax.axis_index("shard")
    rep = lax.axis_index("rep")
    peers = [(partner(me, j), rep) for j in range(1, group)]
    greet(peers, group - 1)
    for copy in share_small(group, me, peers, gains_ref, seg_ref, gains_all_ref, segs_ref, small_sems):
        copy.wait()
    for j in range(group):
        head_table(segs_ref.at[j], rates_ref, table_ref.at[j])


def columns_kernel(
    group,
    replicas,
    hidden,
    slab,
    gate_up_ref,
    gains_ref,
    seg_ref,
    rates_ref,
    own_ref,
    pieces_ref,
    gains_all_ref,
    segs_ref,
    table_ref,
    own_slab,
    slabs,
    out_pieces,
    local_sems,
    sems,
    small_sems,
):
    me = lax.axis_index("shard")
    rep = lax.axis_index("rep")
    rows, share = own_slab.shape[1], slabs.shape[1]
    tiles = hidden // TILE
    tail = hidden - tiles * TILE
    main = 2 * tiles * TILE

    def begin(index, second):
        offset = index * hidden
        return pl.multiple_of(second * FF + offset - lax.rem(offset, LANES), LANES)

    loads = []
    for j in range(1, group):
        for second in range(2):
            at = 2 * (j - 1) + second
            copy = pltpu.make_async_copy(
                gate_up_ref.at[
                    pl.ds(pl.multiple_of(rep * share, 16), share), pl.ds(begin(partner(me, j), second), slab)
                ],
                slabs.at[at],
                local_sems.at[at],
            )
            copy.start()
            loads.append(copy)
    for second in range(2):
        at = 2 * (group - 1) + second
        copy = pltpu.make_async_copy(
            gate_up_ref.at[:, pl.ds(begin(me, second), slab)],
            own_slab.at[second],
            local_sems.at[at],
        )
        copy.start()
        loads.append(copy)
    peers = [(partner(me, j), rep) for j in range(1, group)]
    greet(peers, group - 1)
    small = share_small(group, me, peers, gains_ref, seg_ref, gains_all_ref, segs_ref, small_sems)

    def shifted(ref, index):
        amount = lax.rem(slab - lax.rem(index * hidden, LANES), slab)
        return pltpu.roll(ref[...].astype(jnp.float32), amount, 1)

    sent = []
    for j in range(1, group):
        for second in range(2):
            loads[2 * (j - 1) + second].wait()

        def store(first, values, j=j):
            out_pieces[j - 1, :, first : first + values.shape[1]] = values

        tile_format(
            shifted(slabs.at[2 * (j - 1)], partner(me, j)),
            shifted(slabs.at[2 * (j - 1) + 1], partner(me, j)),
            store,
            tiles,
            tail,
        )
        sent.append(
            send(
                out_pieces.at[j - 1, :, pl.ds(0, main)],
                pieces_ref.at[:, pl.ds((j - 1) * main, main)],
                sems,
                2 * (j - 1),
                peers[j - 1],
            )
        )
        sent.append(
            send(
                out_pieces.at[j - 1, :, pl.ds(main, 2 * TAIL)],
                pieces_ref.at[:, pl.ds((group - 1) * main + (j - 1) * 2 * TAIL, 2 * TAIL)],
                sems,
                2 * (j - 1) + 1,
                peers[j - 1],
            )
        )
    for second in range(2):
        loads[2 * (group - 1) + second].wait()

    def store_own(first, values):
        own_ref[:, first : first + values.shape[1]] = values

    tile_format(
        shifted(own_slab.at[0], me), shifted(own_slab.at[1], me), store_own, tiles, tail
    )
    for copy in small:
        copy.wait()
    for j in range(group):
        head_table(segs_ref.at[j], rates_ref, table_ref.at[j])
    for copy in sent:
        copy.wait()


def small_shapes(gains, seg, group):
    rows, tokens = seg.shape
    f32 = jnp.float32
    return [
        jax.ShapeDtypeStruct((group * rows, gains.shape[1]), f32),
        jax.ShapeDtypeStruct((group, rows, tokens), f32),
        jax.ShapeDtypeStruct((group, 3, tokens, LANES), f32),
    ]


def small_things(gains, seg, group):
    return pl.pallas_call(
        functools.partial(small_kernel, group),
        in_specs=[pl.BlockSpec(memory_space=pltpu.VMEM)] * 3,
        out_specs=[pl.BlockSpec(memory_space=pltpu.VMEM)] * 3,
        out_shape=small_shapes(gains, seg, group),
        scratch_shapes=[pltpu.SemaphoreType.DMA((2, 2 * (group - 1)))],
        compiler_params=pltpu.CompilerParams(
            collective_id=3, has_side_effects=True, vmem_limit_bytes=VMEM_BYTES
        ),
        name="small_things",
    )(gains, seg, rotation_rates())


def hidden_pieces(gate_up, gains, seg, group, replicas):
    rows = gate_up.shape[0]
    share = rows // replicas
    hidden = FF // group
    whole = 2 * (hidden // TILE * TILE + TAIL)
    slab = -(-(hidden + LANES - math.gcd(hidden, LANES)) // LANES) * LANES
    bf16 = jnp.bfloat16
    others = group - 1
    return pl.pallas_call(
        functools.partial(columns_kernel, group, replicas, hidden, slab),
        in_specs=[pl.BlockSpec(memory_space=pl.ANY)] + [pl.BlockSpec(memory_space=pltpu.VMEM)] * 3,
        out_specs=[pl.BlockSpec(memory_space=pltpu.VMEM)] * 5,
        out_shape=[
            jax.ShapeDtypeStruct((rows, whole), bf16),
            jax.ShapeDtypeStruct((share, others * whole), bf16),
        ]
        + small_shapes(gains, seg, group),
        scratch_shapes=[
            pltpu.VMEM((2, rows, slab), bf16),
            pltpu.VMEM((2 * others, share, slab), bf16),
            pltpu.VMEM((others, share, whole), bf16),
            pltpu.SemaphoreType.DMA((2 * group,)),
            pltpu.SemaphoreType.DMA((2, 2 * others)),
            pltpu.SemaphoreType.DMA((2, 2 * others)),
        ],
        compiler_params=pltpu.CompilerParams(
            collective_id=1, has_side_effects=True, vmem_limit_bytes=VMEM_BYTES
        ),
        cost_estimate=pl.CostEstimate(flops=0, bytes_accessed=100_000_000, transcendentals=0),
        name="hidden_pieces",
    )(gate_up, gains, seg, rotation_rates())


def latent_kernel(
    group,
    tokens_ref,
    gains_ref,
    latent_gains_ref,
    table_ref,
    latent_proj_ref,
    query_ref,
    keyval_ref,
    parts_ref,
    rows_ref,
    normed_ref,
    latent_w_ref,
    query_w_ref,
    keyval_w_ref,
    local_sems,
    fetch_sems,
    swap_sems,
    weight_sems,
    weight_swap_sems,
    part_sems,
):
    f32 = jnp.float32
    bf16 = jnp.bfloat16
    me = lax.axis_index("shard")
    rep = lax.axis_index("rep")
    core = lax.rem(rep, 2)
    tokens = tokens_ref.shape[0]
    rows_d = latent_proj_ref.shape[0]
    half = rows_d // 2
    query_rows = query_ref.shape[0]
    keyval_rows = keyval_ref.shape[0]
    width = query_w_ref.shape[1]
    others = range(1, group)
    peers = [None] + [(partner(me, j), rep) for j in others]
    sibling = (me, rep + 1 - 2 * core)
    greet(peers[1:] + [sibling], group)

    def block(index, which):
        return pl.ds(pl.multiple_of(index * rows_d + which * half, 16), half)

    fetched = [None] + [
        send(
            latent_proj_ref.at[pl.ds(pl.multiple_of(core * half, 16), half), :],
            latent_w_ref.at[block(me, core), :],
            fetch_sems,
            j - 1,
            peers[j],
        )
        for j in others
    ]
    own = pltpu.make_async_copy(
        latent_proj_ref,
        latent_w_ref.at[pl.ds(pl.multiple_of(me * rows_d, 16), rows_d), :],
        local_sems.at[0],
    )
    own.start()
    kinds = ((query_ref, query_w_ref, query_rows), (keyval_ref, keyval_w_ref, keyval_rows))

    def weight_rows(index, rows):
        return pl.ds(pl.multiple_of(index * rows + core * (rows // 2), 16), rows // 2)

    def fetch_weights():
        return [
            send(
                ref.at[
                    pl.ds(pl.multiple_of(core * (rows // 2), 16), rows // 2),
                    pl.ds(pl.multiple_of(partner(me, j) * width, LANES), width),
                ],
                out_ref.at[weight_rows(me, rows), :],
                weight_sems,
                kind * (group - 1) + j - 1,
                peers[j],
            )
            for kind, (ref, out_ref, rows) in enumerate(kinds)
            for j in others
        ]

    def swap_weights(copies):
        swaps = []
        for kind, (ref, out_ref, rows) in enumerate(kinds):
            for j in others:
                index = kind * (group - 1) + j - 1
                copies[index].wait_recv()
                where = weight_rows(partner(me, j), rows)
                swaps.append(
                    send(
                        out_ref.at[where, :],
                        out_ref.at[where, :],
                        weight_swap_sems,
                        index,
                        sibling,
                    )
                )
        return swaps

    mine = []
    for at, (ref, out_ref, rows) in enumerate(kinds):
        copy = pltpu.make_async_copy(
            ref.at[:, pl.ds(pl.multiple_of(me * width, LANES), width)],
            out_ref.at[pl.ds(pl.multiple_of(me * rows, 16), rows), :],
            local_sems.at[1 + at],
        )
        copy.start()
        mine.append(copy)

    rows_in = tokens_ref[...].astype(f32)
    scale = lax.rsqrt(jnp.mean(rows_in * rows_in, axis=1, keepdims=True) + norm_eps)
    normed_ref[...] = (rows_in * scale * gains_ref[...]).astype(bf16)

    swaps = []
    for j in others:
        fetched[j].wait_recv()
        where = block(partner(me, j), core)
        swaps.append(
            send(latent_w_ref.at[where, :], latent_w_ref.at[where, :], swap_sems, j - 1, sibling)
        )
    weights = fetch_weights()
    own.wait()
    for copy in swaps:
        copy.wait()
    for j in others:
        fetched[j].wait_send()
    latent = along(normed_ref[...], latent_w_ref[...])
    rows_ref[...] = latent

    def rms(values):
        return values * lax.rsqrt(jnp.mean(values * values, axis=1, keepdims=True) + norm_eps)

    query = rms(latent[:, :QR]) * latent_gains_ref[:, :QR]
    keyval = rms(latent[:, QR : QR + KR]) * latent_gains_ref[:, QR:]
    rope = latent[:, QR + KR :]
    wide = jnp.concatenate(
        [jnp.zeros((tokens, HD), f32), rope, jnp.zeros((tokens, LANES - HD - RD), f32)], axis=1
    )
    parts_ref[0, :, :QR] = query.astype(bf16)
    parts_ref[0, :, QR : QR + KR] = keyval.astype(bf16)
    parts_ref[0, :, QR + KR :] = turn(wide, table_ref, 1.0).astype(bf16)

    direct = (1, 2) if group == 4 else others
    near = [
        send(parts_ref.at[0], parts_ref.at[j], part_sems, j - 1, peers[j]) for j in direct
    ]
    swaps = swap_weights(weights)
    far = []
    if group == 4:
        part = tokens // 2
        top = pl.ds(0, part)
        low = pl.ds(part, part)
        near[0].wait_recv()
        far.append(send(parts_ref.at[1, top], parts_ref.at[3, top], part_sems, 2, peers[2]))
        near[1].wait_recv()
        far.append(send(parts_ref.at[2, low], parts_ref.at[3, low], part_sems, 3, peers[1]))
        for copy in near:
            copy.wait_send()
    else:
        for copy in near:
            copy.wait()
    for copy in far + swaps + mine:
        copy.wait()
    for copy in weights:
        copy.wait_send()


def latent_front(tokens, gain_in, latent_gains, table, latent_proj, query_pad, keyval, group):
    rows = tokens.shape[0]
    heads = query_pad.shape[1] // LANES // group
    bf16 = jnp.bfloat16
    others = group - 1
    dma = pltpu.SemaphoreType.DMA
    width = latent_proj.shape[1]
    return pl.pallas_call(
        functools.partial(latent_kernel, group),
        in_specs=[pl.BlockSpec(memory_space=pltpu.VMEM)] * 7,
        out_specs=[pl.BlockSpec(memory_space=pltpu.VMEM)] * 6,
        out_shape=[
            jax.ShapeDtypeStruct((group, rows, LATENT), bf16),
            jax.ShapeDtypeStruct((rows, width), jnp.float32),
            jax.ShapeDtypeStruct((rows, D), bf16),
            jax.ShapeDtypeStruct((D, width), bf16),
            jax.ShapeDtypeStruct((QR, heads * LANES), bf16),
            jax.ShapeDtypeStruct((KR, heads * LANES), bf16),
        ],
        scratch_shapes=[
            dma((3,)),
            dma((2, others)),
            dma((2, others)),
            dma((2, 2 * others)),
            dma((2, 2 * others)),
            dma((2, max(others, 4))),
        ],
        compiler_params=pltpu.CompilerParams(
            collective_id=2, has_side_effects=True, vmem_limit_bytes=VMEM_BYTES
        ),
        cost_estimate=pl.CostEstimate(
            flops=2 * rows * D * width, bytes_accessed=60_000_000, transcendentals=0
        ),
        name="latent_front",
    )(tokens, gain_in, latent_gains, table, latent_proj, query_pad, keyval)


def hop(array, group, distance):
    return lax.ppermute(array, "shard", [(i, i ^ distance) for i in range(group)])


def near_blocks(array, group):
    return [hop(array, group, j) for j in ((1, 2) if group == 4 else range(1, group))]


def all_blocks(array, near, group):
    if group != 4:
        return [array] + near
    half = array.shape[0] // 2
    far_top = hop(near[0][:half], group, 2)
    far_low = hop(near[1][half:], group, 1)
    return [array] + near + [jnp.concatenate([far_top, far_low], axis=0)]


def gather_blocks(array, group):
    return all_blocks(array, near_blocks(array, group), group)


def scatter_sum(parts, group):
    low = jnp.bfloat16
    f32 = jnp.float32
    total = parts[0].astype(f32)
    if group != 4:
        for j in range(1, group):
            total = total + hop(parts[j], group, j).astype(f32)
        return total
    half = parts[0].shape[0] // 2
    top = hop(parts[3][:half], group, 1)
    bottom = hop(parts[3][half:], group, 2)

    def add(left, right):
        return (left.astype(f32) + right.astype(f32)).astype(low)

    two = jnp.concatenate([add(parts[2][:half], top), parts[2][half:]], axis=0)
    one = jnp.concatenate([parts[1][:half], add(parts[1][half:], bottom)], axis=0)
    return total + hop(one, group, 1).astype(f32) + hop(two, group, 2).astype(f32)


def place(blocks, me):
    rows = blocks[0].shape[0]
    whole = jnp.zeros((rows * len(blocks),) + blocks[0].shape[1:], blocks[0].dtype)
    for j, block in enumerate(blocks):
        whole = lax.dynamic_update_slice_in_dim(whole, block, (me ^ j) * rows, 0)
    return whole


def pick(whole, me, group):
    rows = whole.shape[0] // group
    return [lax.dynamic_slice_in_dim(whole, (me ^ j) * rows, rows, 0) for j in range(group)]


def columns(array, index, width):
    return lax.dynamic_slice_in_dim(array, index * width, width, 1)


def per_device(
    group,
    replicas,
    tokens,
    segments,
    cotangent,
    latent_proj,
    query_up,
    keyval_up,
    out_proj,
    gate_up,
    down_proj,
    norm_gains,
    latent_mean,
    query_mean,
    keyval_mean,
    outproj_mean,
    gateup_mean,
    down_mean,
    gains_mean,
    latent_square,
    query_square,
    keyval_square,
    outproj_square,
    gateup_square,
    down_square,
    gains_square,
):
    f32 = jnp.float32
    bf16 = jnp.bfloat16
    me = lax.axis_index("shard")
    rep = lax.axis_index("rep")
    seq_len = tokens.shape[0]
    heads = H // group
    hidden_part = FF // group
    tiles = hidden_part // TILE
    tail = hidden_part - tiles * TILE
    rows_d = D // group
    others = range(1, group)
    order = jnp.stack([me ^ j for j in range(group)]).astype(jnp.int32)

    share = rows_d // replicas
    fast = group == 4 and share % 16 == 0
    gains_rows = jnp.broadcast_to(norm_gains.astype(f32), (8,) + norm_gains.shape)
    seg_rows = jnp.broadcast_to(segments.astype(f32), (8, seq_len))
    query_pad = jnp.pad(
        query_up.reshape(-1, H, HD + RD), ((0, 0), (0, 0), (0, LANES - HD - RD))
    ).reshape(-1, H * LANES)

    def hidden_columns(array, index):
        gate = columns(array, index, hidden_part)
        up = lax.dynamic_slice_in_dim(array, FF + index * hidden_part, hidden_part, 1)
        cut = []
        for t in range(tiles):
            cut += [gate[:, t * TILE : (t + 1) * TILE], up[:, t * TILE : (t + 1) * TILE]]
        for last in (gate, up):
            cut.append(jnp.pad(last[:, tiles * TILE :], ((0, 0), (0, TAIL - tail))))
        return jnp.concatenate(cut, axis=1)

    share = rows_d // replicas
    cot_near = near_blocks(cotangent, group)
    if share % 16 == 0:
        own_columns, pieces, gains_all, segs, tables = hidden_pieces(
            gate_up, gains_rows, seg_rows, group, replicas
        )
    else:
        gains_all, segs, tables = small_things(gains_rows, seg_rows, group)
        own_share = lax.dynamic_slice_in_dim(gate_up, rep * share, share, 0)
        own_columns = hidden_columns(gate_up, me)
        main = 2 * tiles * TILE
        pieces = [hop(hidden_columns(own_share, me ^ j), group, j) for j in others]
        pieces = jnp.concatenate(
            [piece[:, :main] for piece in pieces] + [piece[:, main:] for piece in pieces], axis=1
        )
    gathered_columns = lax.all_gather(pieces, "rep", axis=0, tiled=True)
    gains_f = gains_all.reshape(group, 8, -1)[:, 0, :].reshape(-1)
    gain_in = gains_f[:D]
    gain_query = gains_f[D : D + QR]
    gain_keyval = gains_f[D + QR : D + QR + KR]
    gain_mlp = gains_f[D + QR + KR :]

    latent_late, _ = lax.optimization_barrier((latent_proj, pieces))
    latent_parts, latent_all, normed_in, latent_w, query_w, keyval_w = latent_front(
        tokens,
        gain_in.reshape(1, D),
        gains_f[D : D + QR + KR].reshape(1, QR + KR),
        tables[0],
        latent_late,
        query_pad,
        keyval_up,
        group,
    )
    rows_in = tokens.astype(f32)
    inv_in = inverse_rms(rows_in)
    query_lat = latent_all[:, :QR]
    keyval_lat = latent_all[:, QR : QR + KR]
    inv_query = inverse_rms(query_lat)
    inv_keyval = inverse_rms(keyval_lat)

    attention = [None] * group
    latents_next = latent_parts
    for at, j in enumerate((*reversed(others), 0)):
        if at == 1:
            latents_next, cot_near = lax.optimization_barrier((latents_next, cot_near))
            cot_parts = all_blocks(cotangent, cot_near, group)
        if j == 0:
            latents_next, _ = lax.optimization_barrier((latents_next, cot_parts[1:]))
        attention[j] = attend(j, latents_next, tables, segs, query_w, keyval_w, out_proj)
        latents_next, _ = lax.optimization_barrier((latent_parts, attention[j][0]))
    out_terms = [part[0] for part in attention]
    hidden = rows_in + residual_scale * scatter_sum(out_terms, group)
    inv_hidden = inverse_rms(hidden)
    normed_mlp = (hidden * inv_hidden * gain_mlp).astype(bf16)

    near = near_blocks(normed_mlp, group)
    half_tiles = tiles // 2
    if fast:
        mlp_parts = all_blocks(normed_mlp, near, group)

        def some_tiles(earlier, first, count):
            return layer_part(
                order,
                mlp_parts,
                cot_parts,
                own_columns,
                gathered_columns,
                down_proj,
                earlier,
                first,
                count,
                group,
                replicas,
            )

        early = some_tiles(None, 0, half_tiles)
        act_all, grad_late, back_all = some_tiles(early, half_tiles, tiles - half_tiles)
        cuts = [(0, half_tiles), (half_tiles, tiles)]
        grad_cuts = [early[1].reshape(D, -1), grad_late.reshape(D, -1)]
        hidden_terms = [back_all[j * seq_len : (j + 1) * seq_len] for j in range(group)]
    else:
        branch_parts = [(residual_scale * part.astype(f32)).astype(bf16) for part in cot_parts]

        def mlp_block(j, normed, earlier):
            return mlp_part(
                order,
                normed,
                branch_parts[j],
                own_columns,
                gathered_columns,
                down_proj,
                earlier,
                j,
                group,
            )

        first = mlp_block(0, normed_mlp, ())
        near, first = lax.optimization_barrier((near, first))
        mlp_parts = all_blocks(normed_mlp, near, group)
        terms = [first]
        for j in others:
            terms.append(mlp_block(j, mlp_parts[j], terms[-1][:2]))
        act_all, grad_all = terms[-1][:2]
        down_terms = [term[2] for term in terms]
        hidden_terms = [term[3] for term in terms]
        cuts = [(0, tiles)]
        grad_gateup = jnp.einsum(
            "td,tf->df", jnp.concatenate(mlp_parts), grad_all, preferred_element_type=f32
        )
        grad_cuts = [
            grad_gateup.astype(bf16)
            .reshape(group, replicas, share, -1)
            .transpose(1, 0, 2, 3)
            .reshape(D, -1)
        ]
    normed_late, _ = lax.optimization_barrier((normed_in, mlp_parts[1:]))
    normed_columns = [columns(normed_late, me, rows_d)] + [
        hop(columns(normed_late, me ^ j, rows_d), group, j) for j in others
    ]
    grad_normed_mlp = scatter_sum(hidden_terms, group)

    grad_down = down_grad(act_all, cot_parts, hidden_part, group)

    def to_owner_rows(block_rows):
        blocks = pick(block_rows, me, group)
        blocks = [blocks[0]] + [hop(blocks[j], group, j) for j in others]
        return place(blocks, me).reshape((group,) + blocks[0].shape)

    grad_top = cotangent.astype(f32)
    grad_gain_mlp = jnp.sum(grad_normed_mlp * hidden * inv_hidden, axis=0)
    grad_hidden = grad_top + norm_back(grad_normed_mlp * gain_mlp, hidden, inv_hidden)
    grad_attn = (residual_scale * grad_hidden).astype(bf16)
    grad_attn, grad_down = lax.optimization_barrier((grad_attn, grad_down))

    def back_block(j, grad):
        return attend_back(
            j,
            grad,
            attention[j][1],
            attention[j][2],
            latent_parts,
            tables,
            segs,
            query_w,
            keyval_w,
            out_proj,
        )

    near = near_blocks(grad_attn, group)
    back = [back_block(0, grad_attn)]
    near, back = lax.optimization_barrier((near, back))
    attn_parts = all_blocks(grad_attn, near, group)
    back += [back_block(j, attn_parts[j]) for j in others]
    summed = []
    for at, grad_cut in enumerate(grad_cuts):
        if at:
            grad_cut, _ = lax.optimization_barrier((grad_cut, (summed[-1], grad_attn)))
        summed.append(lax.psum_scatter(grad_cut, "rep", scatter_dimension=0, tiled=True))
    owned = [to_owner_rows(rows) for rows in summed]

    def unpack(q, second):
        pieces = []
        for (start, stop), rows in zip(cuts, owned):
            for t in range(stop - start):
                first = (2 * t + second) * TILE
                pieces.append(rows[q, :, first : first + TILE])
        first = 2 * (cuts[-1][1] - cuts[-1][0]) * TILE + second * TAIL
        return pieces + [owned[-1][q, :, first : first + tail]]

    gateup_total = jnp.concatenate(
        [piece for second in (0, 1) for q in range(group) for piece in unpack(q, second)], axis=1
    )
    latent_terms = [part[0] for part in back]
    grad_out = token_grad([part[3] for part in attention], attn_parts, 0, heads * HD, "out_grad")
    grad_query = token_grad(latent_parts, [part[1] for part in back], 0, QR, "query_grad")
    grad_keyval = token_grad(latent_parts, [part[2] for part in back], QR, KR, "keyval_grad")
    query_rows = QR // (group * replicas)
    keyval_rows = KR // (group * replicas)
    unit = heads * LANES
    pair_rows = group * (query_rows + keyval_rows)
    out_units = D // unit
    out_count = heads * HD // replicas
    pair = (
        jnp.concatenate(
            [
                grad_query.reshape(group, replicas, query_rows, unit),
                grad_keyval.reshape(group, replicas, keyval_rows, unit),
            ],
            axis=2,
        )
        .transpose(1, 0, 2, 3)
        .reshape(replicas, pair_rows, unit)
    )
    grad_out = grad_out.reshape(replicas, out_count, D)
    grad_out = [grad_out[:, :, k * unit : (k + 1) * unit] for k in range(out_units)]

    grad_latent_low = scatter_sum(latent_terms, group)
    grad_normed_query = grad_latent_low[:, :QR]
    grad_normed_keyval = grad_latent_low[:, QR : QR + KR]
    grad_key_rope = grad_latent_low[:, QR + KR + HD : QR + KR + HD + RD]
    grad_gain_query = jnp.sum(grad_normed_query * query_lat * inv_query, axis=0)
    grad_gain_keyval = jnp.sum(grad_normed_keyval * keyval_lat * inv_keyval, axis=0)
    grad_latent_rows = jnp.concatenate(
        [
            norm_back(grad_normed_query * gain_query, query_lat, inv_query),
            norm_back(grad_normed_keyval * gain_keyval, keyval_lat, inv_keyval),
            grad_key_rope,
        ],
        axis=1,
    ).astype(bf16)
    grad_latent_parts = gather_blocks(grad_latent_rows, group)
    act_late, _ = lax.optimization_barrier((act_all, grad_latent_rows))
    if fast:
        down_all = jnp.dot(
            act_late[:, :hidden_part], down_proj, preferred_element_type=f32
        ).astype(bf16)
        down_terms = [down_all[j * seq_len : (j + 1) * seq_len] for j in range(group)]
    block_out = (hidden + residual_scale * scatter_sum(down_terms, group)).astype(bf16)
    grad_down, _ = lax.optimization_barrier((grad_down, (summed[-1], grad_latent_rows)))
    down_total = lax.psum_scatter(grad_down, "rep", scatter_dimension=0, tiled=True)
    grad_normed_in = jnp.einsum(
        "tc,dc->td", grad_latent_rows, latent_w, preferred_element_type=f32
    )
    grad_gain_in = jnp.sum(grad_normed_in * rows_in * inv_in, axis=0)
    input_grad = grad_hidden + norm_back(grad_normed_in * gain_in, rows_in, inv_in)
    grad_gains = jnp.concatenate([grad_gain_in, grad_gain_query, grad_gain_keyval, grad_gain_mlp])
    gain_blocks = pick(grad_gains, me, group)
    gains_sum = gain_blocks[0]
    for j in others:
        gains_sum = gains_sum + hop(gain_blocks[j].astype(bf16), group, j).astype(f32)
    grad_latent = jnp.einsum(
        "td,tc->dc",
        jnp.concatenate(normed_columns, axis=0),
        jnp.concatenate(grad_latent_parts, axis=0),
        preferred_element_type=f32,
    ).astype(bf16)
    width = grad_latent.shape[1]
    latent_units = -(-width // unit)
    grad_latent = jnp.pad(
        grad_latent.reshape(replicas, share, width), ((0, 0), (0, 0), (0, latent_units * unit - width))
    )
    grad_latent = [grad_latent[:, :, k * unit : (k + 1) * unit] for k in range(latent_units)]
    gains_row = gains_sum.reshape(replicas, 1, -1).astype(bf16)
    gains_row = jnp.pad(gains_row, ((0, 0), (0, 15), (0, unit - gains_row.shape[2])))
    last = jnp.concatenate([pair] + grad_out + grad_latent + [gains_row], axis=1)
    last, _ = lax.optimization_barrier((last.reshape(-1, unit), down_total))
    last = lax.psum_scatter(last, "rep", scatter_dimension=0, tiled=True)
    pair_own = to_owner_rows(last[:pair_rows])
    query_total = (
        pair_own[:, :query_rows]
        .reshape(group, query_rows, heads, LANES)[..., : HD + RD]
        .transpose(1, 0, 2, 3)
        .reshape(query_rows, H * (HD + RD))
    )
    keyval_total = pair_own[:, query_rows:].transpose(1, 0, 2).reshape(keyval_rows, 2 * H * HD)

    def side_by_side(first, count, pieces):
        return jnp.concatenate(
            [last[first + k * count : first + (k + 1) * count] for k in range(pieces)], axis=1
        )

    outproj_total = side_by_side(pair_rows, out_count, out_units)
    latent_at = pair_rows + out_units * out_count
    latent_total = side_by_side(latent_at, share, latent_units)[:, :width]
    gains_total = last[latent_at + latent_units * share, : gains_mean.shape[0]]

    updates = [
        adam_step(latent_proj, latent_total, latent_mean, latent_square, D ** (-0.5), decay_rate),
        adam_step(query_up, query_total, query_mean, query_square, QR ** (-0.5), decay_rate),
        adam_step(keyval_up, keyval_total, keyval_mean, keyval_square, KR ** (-0.5), decay_rate),
        adam_step(
            out_proj,
            outproj_total,
            outproj_mean,
            outproj_square,
            max(H * HD // 512, 1) ** (-0.5),
            decay_rate,
        ),
        adam_step(gate_up, gateup_total, gateup_mean, gateup_square, D ** (-0.5), decay_rate),
        adam_step(
            down_proj, down_total, down_mean, down_square, max(FF // 32, 1) ** (-0.5), decay_rate
        ),
        adam_step(norm_gains, gains_total, gains_mean, gains_square, gain_rate, 0.0),
    ]
    return (block_out, input_grad) + tuple(value for update in updates for value in update)


def solution(mesh):
    return jax.shard_map(
        functools.partial(per_device, mesh.shape["shard"], mesh.shape["rep"]),
        mesh=mesh,
        in_specs=(
            P(("shard", "rep"), None),
            P(("shard", "rep"), None),
            P(("shard", "rep"), None),
            P("shard", None),
            P("shard", None),
            P("shard", None),
            P("shard", None),
            P("shard", None),
            P("shard", None),
            P("shard"),
            P(("shard", "rep"), None),
            P(("shard", "rep"), None),
            P(("shard", "rep"), None),
            P(("shard", "rep"), None),
            P(("shard", "rep"), None),
            P(("shard", "rep"), None),
            P(("shard", "rep")),
            P(("shard", "rep"), None),
            P(("shard", "rep"), None),
            P(("shard", "rep"), None),
            P(("shard", "rep"), None),
            P(("shard", "rep"), None),
            P(("shard", "rep"), None),
            P(("shard", "rep")),
        ),
        out_specs=(
            P(("shard", "rep"), None),
            P(("shard", "rep"), None),
            P(("shard", "rep"), None),
            P(("shard", "rep"), None),
            P(("shard", "rep"), None),
            P(("shard", "rep"), None),
            P(("shard", "rep"), None),
            P(("shard", "rep"), None),
            P(("shard", "rep"), None),
            P(("shard", "rep"), None),
            P(("shard", "rep"), None),
            P(("shard", "rep"), None),
            P(("shard", "rep"), None),
            P(("shard", "rep"), None),
            P(("shard", "rep"), None),
            P(("shard", "rep"), None),
            P(("shard", "rep"), None),
            P(("shard", "rep"), None),
            P(("shard", "rep"), None),
            P(("shard", "rep"), None),
            P(("shard", "rep")),
            P(("shard", "rep")),
            P(("shard", "rep")),
        ),
        check_vma=False,
    )
```

time: 2860 us -> 760 us (0.27)
  waiting for transfers between devices: 2420 us -> 204 us
  Pallas kernels: 0 us -> 321 us
  matrix products: 284 us -> 25.1 us
  starting transfers between devices: 1.09 us -> 54.4 us
  blocking collectives: 38.2 us -> 0 us
  local copies, waits for them, and re-layouts: 46.3 us -> 75.6 us
    all_gather x6 -> x1, waiting for transfers between devices: 1050 us -> 0.01 us  [per_device(): gathered_columns = lax.all_gather(pieces, 'rep', axis=0, tiled=True)]
    reduce_scatter x9 -> x4, waiting for transfers between devices: 1060 us -> 17.1 us  [the longest x1 14.5 us: per_device(): lax.psum_scatter(grad_down, 'rep', scatter_dimension=0, tiled=True)]
    pallas_call x0 -> x16, Pallas kernels: none -> 321 us  [the longest x2 99.1 us: layer_part(): pl.pallas_call(functools.partial(layer_kernel, group, tiles_from, tiles,...]
    unnamed x21 -> x5, waiting for transfers between devices: 309 us -> 0.08 us
    dot_general x53 -> x3, matrix products: 284 us -> 25.1 us  [the longest x1 13.1 us: per_device(): jnp.dot(act_late[:, :hidden_part], down_proj, preferred_element_type=f32)]
    ppermute x0 -> x47, waiting for transfers between devices: none -> 187 us  [hop(): lax.ppermute(array, 'shard', [(i, i ^ distance) for i in range(group)])]
    ppermute x0 -> x47, starting transfers between devices: none -> 54.2 us  [hop(): lax.ppermute(array, 'shard', [(i, i ^ distance) for i in range(group)])]
    unnamed x2 -> x0, blocking collectives: 28.6 us -> none
  transfers between devices with their start and end apart: 18 -> 52, of which waited for: 16 -> 26; matrix products, arithmetic and copies ran while one was open for 8% -> 17% of each run, Pallas kernels for 0% -> 33%
where the time goes in v1:
time: 760 us; the launch traced here: 750 us
  Pallas kernels  321 us (42%)
  waiting for transfers between devices  204 us (27%)
  local copies, waits for them, and re-layouts  75.6 us (10%)
  starting transfers between devices  54.4 us (7%)
  other arithmetic  53.6 us (7%)
  matrix products  25.1 us (3%)
  between operations  15.7 us (2%)
    ppermute x47, waiting for transfers between devices, hop(): lax.ppermute(array, 'shard', [(i, i ^ distance) for i in range(group)])  187 us
    pallas_call x2, Pallas kernels, layer_part(): pl.pallas_call(functools.partial(layer_kernel, group, tiles_from, tiles,...  99.1 us
    pallas_call x1, Pallas kernels, latent_front(): pl.pallas_call(functools.partial(latent_kernel, group), in_specs=[pl.Bloc...  85.8 us
    ppermute x47, starting transfers between devices, hop(): lax.ppermute(array, 'shard', [(i, i ^ distance) for i in range(group)])  54.2 us
    pallas_call x4, Pallas kernels, attend_back(): pl.pallas_call(functools.partial(attend_back_kernel, heads), grid=(1,), o...  42.4 us
    pallas_call x4, Pallas kernels, attend(): pl.pallas_call(functools.partial(attend_kernel, heads), grid=(1,), out_sp...  35.4 us
    unnamed x202, local copies, waits for them, and re-layouts  33.8 us
    pallas_call x1, Pallas kernels, hidden_pieces(): pl.pallas_call(functools.partial(columns_kernel, group, replicas, hidden,...  32.4 us
  transfers between devices with their start and end apart: 52, of which 26 were waited for; matrix products, arithmetic and copies ran while one was open for 17% of the time, Pallas kernels for 33%

profile of v1, /device:TPU:0, one launch (start us, length us, event | category | flops | bytes accessed | tf_op | source)
XLA Modules:
  0.0 749.5 jit_solution(11767636281334928297)
XLA Ops:
  9.3 32.4 %hidden_pieces.1 = (bf16[640,3328]{1,0:T(8,128)(2,1)}, bf16[80,9984]{1,0:T(8,128)(2,1)S(1)}, f32[32,1536]{1,0:T(8,128)S(1)}, f32[4,8,256]{2,1,0:T(8,128)S(1)}, f32[4,3,256,128]{3,2,1,0:T(8,128)S(1)}) custom-call(bf16[640,12800]{1,0:T(8,128)(2,1)} %gate_up_ref.1, f32[8,1536]{1,0:T(8,128)S(1)} %broadcast_in_dim.12.gains_ref, ...), custom_call_target="tpu_custom_call" | custom-call | bytes 100000000 | tf_op jit(solution)/shard_map/hidden_pieces/pallas_call | solution.py:938
  49.5 5.2 reshape.174
  58.7 85.8 %latent_front.1 = (bf16[4,256,1152]{2,1,0:T(8,128)(2,1)}, f32[256,1056]{1,0:T(8,128)S(1)}, bf16[256,2560]{1,0:T(8,128)(2,1)S(1)}, bf16[2560,1056]{1,0:T(8,128)(2...) custom-call(bf16[256,2560]{1,0:T(8,128)(2,1)S(1)} %copy-done.2, f32[1,2560]{1,0:T(1,128)S(1)} %reshape.172.gains_ref, ...), custom_call_target="tpu_custom_call" | custom-call | flops 1384120320 | bytes 60000000 | tf_op jit(solution)/shard_map/latent_front/pallas_call | solution.py:1134
  146.7 8.6 %attend.4 = (bf16[256,2560]{1,0:T(8,128)(2,1)S(1)}, bf16[256,1280]{1,0:T(8,128)(2,1)S(1)}, bf16[256,1280]{1,0:T(8,128)(2,1)S(1)}, bf16[256,640]{1,0:T(8,128)(2,1)S(1)}) custom-call(bf16[4,256,1152]{2,1,0:T(8,128)(2,1)} %get-tuple-element.105.latent_ref.refs_0_.refs_1_.refs_2_.refs_3_, f32[4,3,256,128]{3,2,1,0:T(8,128)S(1)} %get-tuple-element.89.table_ref, ...), custom_call_target="tpu_custom_call" | custom-call | flops 1845493760 | bytes 7208960 | tf_op jit(solution)/shard_map/attend/pallas_call | solution.py:557
  156.8 9.0 %attend.5 = (bf16[256,2560]{1,0:T(8,128)(2,1)S(1)}, bf16[256,1280]{1,0:T(8,128)(2,1)S(1)}, bf16[256,1280]{1,0:T(8,128)(2,1)S(1)}, bf16[256,640]{1,0:T(8,128)(2,1)S(1)}) custom-call(bf16[4,256,1152]{2,1,0:T(8,128)(2,1)} %get-tuple-element.105.latent_ref.refs_0_.refs_1_.refs_2_.refs_3_, f32[4,3,256,128]{3,2,1,0:T(8,128)S(1)} %get-tuple-element.89.table_ref, ...), custom_call_target="tpu_custom_call" | custom-call | flops 1845493760 | bytes 7208960 | tf_op jit(solution)/shard_map/attend/pallas_call | solution.py:557
  169.0 8.6 %attend.6 = (bf16[256,2560]{1,0:T(8,128)(2,1)S(1)}, bf16[256,1280]{1,0:T(8,128)(2,1)S(1)}, bf16[256,1280]{1,0:T(8,128)(2,1)S(1)}, bf16[256,640]{1,0:T(8,128)(2,1)S(1)}) custom-call(bf16[4,256,1152]{2,1,0:T(8,128)(2,1)} %get-tuple-element.105.latent_ref.refs_0_.refs_1_.refs_2_.refs_3_, f32[4,3,256,128]{3,2,1,0:T(8,128)S(1)} %get-tuple-element.89.table_ref, ...), custom_call_target="tpu_custom_call" | custom-call | flops 1845493760 | bytes 7208960 | tf_op jit(solution)/shard_map/attend/pallas_call | solution.py:557
  186.0 34.3 %collective-permute-done.3 = bf16[128,2560]{1,0:T(8,128)(2,1)S(1)} collective-permute-done((bf16[128,2560]{1,0:T(8,128)(2,1)S(1)}, bf16[128,2560]{1,0:T(8,128)(2,1)S(1)}, u32[]{:S(2)}, u32[]{:S(2)}) %collective-permute-start.3) | collective-permute-done | bytes 655392 | tf_op jit(solution)/shard_map/ppermute | solution.py:1165
  220.4 9.1 %attend.7 = (bf16[256,2560]{1,0:T(8,128)(2,1)S(1)}, bf16[256,1280]{1,0:T(8,128)(2,1)S(1)}, bf16[256,1280]{1,0:T(8,128)(2,1)S(1)}, bf16[256,640]{1,0:T(8,128)(2,1)S(1)}) custom-call(bf16[4,256,1152]{2,1,0:T(8,128)(2,1)} %get-tuple-element.105.latent_ref.refs_0_.refs_1_.refs_2_.refs_3_, f32[4,3,256,128]{3,2,1,0:T(8,128)S(1)} %get-tuple-element.89.table_ref, ...), custom_call_target="tpu_custom_call" | custom-call | flops 1845493760 | bytes 7208960 | tf_op jit(solution)/shard_map/attend/pallas_call | solution.py:557
  233.7 24.8 %collective-permute-done.8.refs_1_ = bf16[256,2560]{1,0:T(8,128)(2,1)S(1)} collective-permute-done((bf16[256,2560]{1,0:T(8,128)(2,1)S(1)}, bf16[256,2560]{1,0:T(8,128)(2,1)S(1)}, u32[]{:S(2)}, u32[]{:S(2)}) %collective-permute-start.8) | collective-permute-done | bytes 1310752 | tf_op jit(solution)/shard_map/ppermute | solution.py:1165
  265.2 7.6 %collective-permute-done.10 = bf16[128,2560]{1,0:T(8,128)(2,1)} collective-permute-done((bf16[128,2560]{1,0:T(8,128)(2,1)}, bf16[128,2560]{1,0:T(8,128)(2,1)}, u32[]{:S(2)}, u32[]{:S(2)}) %collective-permute-start.10) | collective-permute-done | bytes 655392 | tf_op jit(solution)/shard_map/ppermute | solution.py:1165
  276.7 44.7 %layer_part.2 = (bf16[1024,1664]{1,0:T(8,128)(2,1)}, bf16[8,4,80,1536]{3,2,1,0:T(8,128)(2,1)}, f32[1024,2560]{1,0:T(8,128)}) custom-call(s32[4]{0:T(128)} %pad_add_fusion.order_ref, bf16[256,2560]{1,0:T(8,128)(2,1)} %copy-done.61, bf16[256,2560]{1,0:T(8,128)(2,1)} %copy-done.66, bf16[256,2560]{1,0:T(8,128)(2,1)} %copy-done.67, ...), custom_call_target="tpu_custom_call" | custom-call | flops 28185722880 | bytes 65536000 | tf_op jit(solution)/shard_map/layer_part/pallas_call | solution.py:415
  321.5 54.4 %layer_part.3 = (bf16[1024,1664]{1,0:T(8,128)(2,1)}, bf16[8,4,80,1792]{3,2,1,0:T(8,128)(2,1)}, bf16[1024,2560]{1,0:T(8,128)(2,1)}) custom-call(s32[4]{0:T(128)} %pad_add_fusion.order_ref, bf16[256,2560]{1,0:T(8,128)(2,1)} %copy-done.61, bf16[256,2560]{1,0:T(8,128)(2,1)} %copy-done.66, ...), custom_call_target="tpu_custom_call", output_to_operand_aliasing={{0}: (19, {})} | custom-call | flops 30534533120 | bytes 67502080 | tf_op jit(solution)/shard_map/layer_part/pallas_call | solution.py:415
  380.0 9.1 %collective-permute-done.12 = bf16[128,2560]{1,0:T(8,128)(2,1)S(1)} collective-permute-done((bf16[128,2560]{1,0:T(8,128)(2,1)S(1)}, bf16[128,2560]{1,0:T(8,128)(2,1)S(1)}, u32[]{:S(2)}, u32[]{:S(2)}) %collective-permute-start.12) | collective-permute-done | bytes 655392 | tf_op jit(solution)/shard_map/ppermute | solution.py:1165
  397.9 15.0 %down_grad.1 = bf16[1600,2560]{1,0:T(8,128)(2,1)} custom-call(bf16[1024,1664]{1,0:T(8,128)(2,1)} %get-tuple-element.131.act_ref, bf16[256,2560]{1,0:T(8,128)(2,1)} %refs_0_.1, bf16[256,2560]{1,0:T(8,128)(2,1)} %collective-permute-done.refs_5_.refs_1_, bf16[256,2560]{1,0:T(8,128)(2,1)} %collective-permute-done.1.refs_6_.refs_2_, bf16[256,2560]{1,0:T(8,128)(2,1)S(1)} %copy-done.9), custom_call_target="tpu_custom_call" | custom-call | flops 8388608000 | bytes 16711680 | tf_op jit(solution)/shard_map/down_grad/pallas_call | solution.py:456
  412.9 6.6 collective-permute-done.13
  426.4 5.4 multiply_convert_fusion
  435.9 10.2 %attend_back.4 = (bf16[256,1152]{1,0:T(8,128)(2,1)S(1)}, bf16[256,1280]{1,0:T(8,128)(2,1)S(1)}, bf16[256,1280]{1,0:T(8,128)(2,1)S(1)}) custom-call(bf16[256,2560]{1,0:T(8,128)(2,1)S(1)} %get-tuple-element.113.grad_ref.refs_4_, bf16[256,1280]{1,0:T(8,128)(2,1)S(1)} %copy-done.31, bf16[256,1280]{1,0:T(8,128)(2,1)S(1)} %copy-done.33, ...), custom_call_target="tpu_custom_call" | custom-call | flops 2348810240 | bytes 7208960 | tf_op jit(solution)/shard_map/attend_back/pallas_call | solution.py:642
  447.0 12.8 %collective-permute-done.16.grad_ref.refs_5_ = bf16[256,2560]{1,0:T(8,128)(2,1)S(1)} collective-permute-done((bf16[256,2560]{1,0:T(8,128)(2,1)S(1)}, bf16[256,2560]{1,0:T(8,128)(2,1)S(1)}, u32[]{:S(2)}, u32[]{:S(2)}) %collective-permute-start.16) | collective-permute-done | bytes 1310752 | tf_op jit(solution)/shard_map/ppermute | solution.py:1165
  464.5 7.0 collective-permute-done.18
  473.2 11.2 %attend_back.6 = (bf16[256,1152]{1,0:T(8,128)(2,1)S(1)}, bf16[256,1280]{1,0:T(8,128)(2,1)S(1)}, bf16[256,1280]{1,0:T(8,128)(2,1)S(1)}) custom-call(bf16[256,2560]{1,0:T(8,128)(2,1)S(1)} %constant_dynamic-update-slice_fusion.4.grad_ref.refs_7_, bf16[256,1280]{1,0:T(8,128)(2,1)S(1)} %copy-done.21, bf16[256,1280]{1,0:T(8,128)(2,1)S(1)} %copy-done.23, ...), custom_call_target="tpu_custom_call" | custom-call | flops 2348810240 | bytes 7208960 | tf_op jit(solution)/shard_map/attend_back/pallas_call | solution.py:642
  485.9 10.4 %attend_back.5 = (bf16[256,1152]{1,0:T(8,128)(2,1)S(1)}, bf16[256,1280]{1,0:T(8,128)(2,1)S(1)}, bf16[256,1280]{1,0:T(8,128)(2,1)S(1)}) custom-call(bf16[256,2560]{1,0:T(8,128)(2,1)S(1)} %collective-permute-done.16.grad_ref.refs_5_, bf16[256,1280]{1,0:T(8,128)(2,1)S(1)} %copy-done.25, bf16[256,1280]{1,0:T(8,128)(2,1)S(1)} %copy-done.27, ...), custom_call_target="tpu_custom_call" | custom-call | flops 2348810240 | bytes 7208960 | tf_op jit(solution)/shard_map/attend_back/pallas_call | solution.py:642
  497.2 10.6 %attend_back.7 = (bf16[256,1152]{1,0:T(8,128)(2,1)S(1)}, bf16[256,1280]{1,0:T(8,128)(2,1)S(1)}, bf16[256,1280]{1,0:T(8,128)(2,1)S(1)}) custom-call(bf16[256,2560]{1,0:T(8,128)(2,1)S(1)} %collective-permute-done.17.grad_ref.refs_6_, bf16[256,1280]{1,0:T(8,128)(2,1)S(1)} %get-tuple-element.128.query_ref, bf16[256,1280]{1,0:T(8,128)(2,1)S(1)} %copy-done.19, ...), custom_call_target="tpu_custom_call" | custom-call | flops 2348810240 | bytes 7208960 | tf_op jit(solution)/shard_map/attend_back/pallas_call | solution.py:642
  545.4 6.6 out_grad.1
  559.6 7.1 fusion.13
  580.4 11.1 %collective-permute-done.33 = bf16[128,1056]{1,0:T(8,128)(2,1)} collective-permute-done((bf16[128,1056]{1,0:T(8,128)(2,1)}, bf16[128,1056]{1,0:T(8,128)(2,1)}, u32[]{:S(2)}, u32[]{:S(2)}) %collective-permute-start.33) | collective-permute-done | bytes 270368 | tf_op jit(solution)/shard_map/ppermute | solution.py:1165
  603.8 14.5 %reduce-scatter.9.cloned.1.call-done = bf16[200,2560]{1,0:T(8,128)(2,1)} async-done(((bf16[1600,2560]{1,0:T(8,128)(2,1)}), bf16[200,2560]{1,0:T(8,128)(2,1)}) %reduce-scatter.9.cloned.1.call-update) | async-done | bytes 1024016 | tf_op jit(solution)/shard_map/reduce_scatter | solution.py:1500
  618.3 13.1 %convolution_convert_fusion = bf16[1024,2560]{1,0:T(8,128)(2,1)S(1)} fusion(bf16[1600,2560]{1,0:T(8,128)(2,1)} %refs_17_.1, bf16[1024,1664]{1,0:T(8,128)(2,1)} %get-tuple-element.131.act_ref), kind=kOutput, calls=%fused_computation.1 | convolution fusion | flops 8391229440 | bytes 16842752 | tf_op jit(solution)/shard_map/dot_general | solution.py:1494
  638.6 10.3 %collective-permute-done.24 = bf16[128,2560]{1,0:T(8,128)(2,1)} collective-permute-done((bf16[128,2560]{1,0:T(8,128)(2,1)}, bf16[128,2560]{1,0:T(8,128)(2,1)}, u32[]{:S(2)}, u32[]{:S(2)}) %collective-permute-start.24) | collective-permute-done | bytes 655392 | tf_op jit(solution)/shard_map/ppermute | solution.py:1165
  659.2 23.2 %collective-permute-done.25 = bf16[256,2560]{1,0:T(8,128)(2,1)S(1)} collective-permute-done((bf16[256,2560]{1,0:T(8,128)(2,1)S(1)}, bf16[256,2560]{1,0:T(8,128)(2,1)S(1)}, u32[]{:S(2)}, u32[]{:S(2)}) %collective-permute-start.25) | collective-permute-done | bytes 1310752 | tf_op jit(solution)/shard_map/ppermute | solution.py:1165
  689.9 6.4 collective-permute-done.43
  699.4 6.7 collective-permute-done.45
  711.2 8.0 %convert_subtract_fusion = (f32[80,12800]{1,0:T(8,128)}, f32[80,12800]{1,0:T(8,128)}, f32[80,12800]{1,0:T(8,128)}) fusion(bf16[640,12800]{1,0:T(8,128)(2,1)} %gate_up_ref.1, s32[]{:T(128)S(6)} %select_n.81, bf16[80,12800]{1,0:T(8,128)(2,1)S(1)} %concatenate.76, bf16[80,12800]{1,0:T(8,128)(2,1)} %param.39, bf16[80,12800]{1,0:T(8,128)(2,1)} %param.46), kind=kLoop, calls=%fused_computation.8 | loop fusion | flops 19456000 | bytes 20480004 | tf_op jit(solution)/shard_map/sub | solution.py:64
  (418 shorter events, 204.1 us)
Async XLA Ops:
  7.2 269.5 %all-gather.2.cloned.1.call-start = ((), (), s32[]{:S(2)}) async-start(), calls=%async_computation.4 | async-start | bytes 14376960 | tf_op jit(solution)/shard_map/all_gather | solution.py:1296
  42.9 389.0 %reduce-scatter.5.cloned.1.call-start = ((), (), s32[]{:S(2)}) async-start(), calls=%async_computation.5 | async-start | bytes 8847360 | tf_op jit(solution)/shard_map/reduce_scatter | solution.py:1438
  42.9 113.9 %collective-permute-start = (bf16[256,2560]{1,0:T(8,128)(2,1)}, bf16[256,2560]{1,0:T(8,128)(2,1)}, u32[]{:S(2)}, u32[]{:S(2)}) collective-permute-start(bf16[256,2560]{1,0:T(8,128)(2,1)} %refs_0_.1), channel_id=1, source_target_pairs={{0,8},{8,0},{16,24},{24,16},{1,9},{9,1},{17,25},{25,17},{2,10},{10... | collective-permute-start | bytes 3932168 | tf_op jit(solution)/shard_map/ppermute | solution.py:1165
  44.4 112.4 %collective-permute-start.1 = (bf16[256,2560]{1,0:T(8,128)(2,1)}, bf16[256,2560]{1,0:T(8,128)(2,1)}, u32[]{:S(2)}, u32[]{:S(2)}) collective-permute-start(bf16[256,2560]{1,0:T(8,128)(2,1)} %refs_0_.1), channel_id=1, source_target_pairs={{0,16},{8,24},{16,0},{24,8},{1,17},{9,25},{17,1},{25,9},{2,18},{10... | collective-permute-start | bytes 3932168 | tf_op jit(solution)/shard_map/ppermute | solution.py:1165
  155.5 22.2 %collective-permute-start.4 = (bf16[128,2560]{1,0:T(8,128)(2,1)S(1)}, bf16[128,2560]{1,0:T(8,128)(2,1)S(1)}, u32[]{:S(2)}, u32[]{:S(2)}) collective-permute-start(bf16[128,2560]{1,0:T(8,128)(2,1)S(1)} %get-tuple-element.203), channel_id=1, source_target_pairs={{0,16},{8,24},{16,0},{24,8},{1,17},{9,25},{17,1},{25,9},{2,18},{10... | collective-permute-start | bytes 1966088 | tf_op jit(solution)/shard_map/ppermute | solution.py:1165
  155.6 25.2 %collective-permute-start.6 = (bf16[128,2560]{1,0:T(8,128)(2,1)S(1)}, bf16[128,2560]{1,0:T(8,128)(2,1)S(1)}, u32[]{:S(2)}, u32[]{:S(2)}) collective-permute-start(bf16[128,2560]{1,0:T(8,128)(2,1)S(1)} %get-tuple-element.204), channel_id=1, source_target_pairs={{0,8},{8,0},{16,24},{24,16},{1,9},{9,1},{17,25},{25,17},{2,10},{10... | collective-permute-start | bytes 1966088 | tf_op jit(solution)/shard_map/ppermute | solution.py:1165
  168.2 17.7 %collective-permute-start.2 = (bf16[128,2560]{1,0:T(8,128)(2,1)}, bf16[128,2560]{1,0:T(8,128)(2,1)S(1)}, u32[]{:S(2)}, u32[]{:S(2)}) collective-permute-start(bf16[128,2560]{1,0:T(8,128)(2,1)} %slice.364), channel_id=1, source_target_pairs={{0,16},{8,24},{16,0},{24,8},{1,17},{9,25},{17,1},{25,9},{2,18},{10... | collective-permute-start | bytes 1966088 | tf_op jit(solution)/shard_map/ppermute | solution.py:1165
  178.8 50.7 %collective-permute-start.5 = (bf16[256,2560]{1,0:T(8,128)(2,1)S(1)}, bf16[256,2560]{1,0:T(8,128)(2,1)S(1)}, u32[]{:S(2)}, u32[]{:S(2)}) collective-permute-start(bf16[256,2560]{1,0:T(8,128)(2,1)S(1)} %pad_maximum_fusion.1), channel_id=1, source_target_pairs={{0,8},{8,0},{16,24},{24,16},{1,9},{9,1},{17,25},{25,17},{2,10},{10... | collective-permute-start | bytes 3932168 | tf_op jit(solution)/shard_map/ppermute | solution.py:1165
  181.0 48.5 %collective-permute-start.7 = (bf16[256,2560]{1,0:T(8,128)(2,1)S(1)}, bf16[256,2560]{1,0:T(8,128)(2,1)S(1)}, u32[]{:S(2)}, u32[]{:S(2)}) collective-permute-start(bf16[256,2560]{1,0:T(8,128)(2,1)S(1)} %pad_maximum_fusion.2), channel_id=1, source_target_pairs={{0,16},{8,24},{16,0},{24,8},{1,17},{9,25},{17,1},{25,9},{2,18},{10... | collective-permute-start | bytes 3932168 | tf_op jit(solution)/shard_map/ppermute | solution.py:1165
  182.3 38.0 %collective-permute-start.3 = (bf16[128,2560]{1,0:T(8,128)(2,1)S(1)}, bf16[128,2560]{1,0:T(8,128)(2,1)S(1)}, u32[]{:S(2)}, u32[]{:S(2)}) collective-permute-start(bf16[128,2560]{1,0:T(8,128)(2,1)S(1)} %slice.365), channel_id=1, source_target_pairs={{0,8},{8,0},{16,24},{24,16},{1,9},{9,1},{17,25},{25,17},{2,10},{10... | collective-permute-start | bytes 1966088 | tf_op jit(solution)/shard_map/ppermute | solution.py:1165
  231.9 26.6 %collective-permute-start.8 = (bf16[256,2560]{1,0:T(8,128)(2,1)S(1)}, bf16[256,2560]{1,0:T(8,128)(2,1)S(1)}, u32[]{:S(2)}, u32[]{:S(2)}) collective-permute-start(bf16[256,2560]{1,0:T(8,128)(2,1)S(1)} %multiply_convert_fusion.1.refs_0_), channel_id=1, source_target_pairs={{0,8},{8,0},{16,24},{24,16},{1,9},{9,1},{17,25},{25,17},{2,10},{10... | collective-permute-start | bytes 3932168 | tf_op jit(solution)/shard_map/ppermute | solution.py:1165
  232.7 27.4 %collective-permute-start.9 = (bf16[256,2560]{1,0:T(8,128)(2,1)S(1)}, bf16[256,2560]{1,0:T(8,128)(2,1)S(1)}, u32[]{:S(2)}, u32[]{:S(2)}) collective-permute-start(bf16[256,2560]{1,0:T(8,128)(2,1)S(1)} %multiply_convert_fusion.1.refs_0_), channel_id=1, source_target_pairs={{0,16},{8,24},{16,0},{24,8},{1,17},{9,25},{17,1},{25,9},{2,18},{10... | collective-permute-start | bytes 3932168 | tf_op jit(solution)/shard_map/ppermute | solution.py:1165
  321.5 208.7 %reduce-scatter.7.cloned.1.call-start = ((), (), s32[]{:S(2)}) async-start(), calls=%async_computation.6 | async-start | bytes 10321920 | tf_op jit(solution)/shard_map/reduce_scatter | solution.py:1438
  393.3 26.1 %collective-permute-start.13 = (bf16[256,2560]{1,0:T(8,128)(2,1)}, bf16[256,2560]{1,0:T(8,128)(2,1)S(1)}, u32[]{:S(2)}, u32[]{:S(2)}) collective-permute-start(bf16[256,2560]{1,0:T(8,128)(2,1)} %pad_maximum_fusion.3), channel_id=1, source_target_pairs={{0,8},{8,0},{16,24},{24,16},{1,9},{9,1},{17,25},{25,17},{2,10},{10... | collective-permute-start | bytes 3932168 | tf_op jit(solution)/shard_map/ppermute | solution.py:1165
  396.2 25.9 %collective-permute-start.15 = (bf16[256,2560]{1,0:T(8,128)(2,1)}, bf16[256,2560]{1,0:T(8,128)(2,1)}, u32[]{:S(2)}, u32[]{:S(2)}) collective-permute-start(bf16[256,2560]{1,0:T(8,128)(2,1)} %pad_maximum_fusion.4), channel_id=1, source_target_pairs={{0,16},{8,24},{16,0},{24,8},{1,17},{9,25},{17,1},{25,9},{2,18},{10... | collective-permute-start | bytes 3932168 | tf_op jit(solution)/shard_map/ppermute | solution.py:1165
  431.9 186.5 %reduce-scatter.9.cloned.1.call-start = ((), (), s32[]{:S(2)}) async-start(), calls=%async_computation.7 | async-start | bytes 9216000 | tf_op jit(solution)/shard_map/reduce_scatter | solution.py:1500
  431.9 27.9 %collective-permute-start.16 = (bf16[256,2560]{1,0:T(8,128)(2,1)S(1)}, bf16[256,2560]{1,0:T(8,128)(2,1)S(1)}, u32[]{:S(2)}, u32[]{:S(2)}) collective-permute-start(bf16[256,2560]{1,0:T(8,128)(2,1)S(1)} %get-tuple-element.113.grad_ref.refs_4_), channel_id=1, source_target_pairs={{0,8},{8,0},{16,24},{24,16},{1,9},{9,1},{17,25},{25,17},{2,10},{10... | collective-permute-start | bytes 3932168 | tf_op jit(solution)/shard_map/ppermute | solution.py:1165
  432.2 28.6 %collective-permute-start.17 = (bf16[256,2560]{1,0:T(8,128)(2,1)S(1)}, bf16[256,2560]{1,0:T(8,128)(2,1)S(1)}, u32[]{:S(2)}, u32[]{:S(2)}) collective-permute-start(bf16[256,2560]{1,0:T(8,128)(2,1)S(1)} %get-tuple-element.113.grad_ref.refs_4_), channel_id=1, source_target_pairs={{0,16},{8,24},{16,0},{24,8},{1,17},{9,25},{17,1},{25,9},{2,18},{10... | collective-permute-start | bytes 3932168 | tf_op jit(solution)/shard_map/ppermute | solution.py:1165
  485.3 24.6 %collective-permute-start.20 = (bf16[128,1152]{1,0:T(8,128)(2,1)S(1)}, bf16[128,1152]{1,0:T(8,128)(2,1)S(1)}, u32[]{:S(2)}, u32[]{:S(2)}) collective-permute-start(bf16[128,1152]{1,0:T(8,128)(2,1)S(1)} %get-tuple-element.273), channel_id=1, source_target_pairs={{0,16},{8,24},{16,0},{24,8},{1,17},{9,25},{17,1},{25,9},{2,18},{10... | collective-permute-start | bytes 884744 | tf_op jit(solution)/shard_map/ppermute | solution.py:1165
  530.2 194.2 %reduce-scatter.11.cloned.1.call-start = ((), (), s32[]{:S(2)}) async-start(), calls=%async_computation.8 | async-start | bytes 8847360 | tf_op jit(solution)/shard_map/reduce_scatter | solution.py:1527
  556.4 18.8 %collective-permute-start.31 = (bf16[256,1056]{0,1:T(8,128)(2,1)S(1)}, bf16[256,1056]{0,1:T(8,128)(2,1)}, u32[]{:S(2)}, u32[]{:S(2)}) collective-permute-start(bf16[256,1056]{0,1:T(8,128)(2,1)S(1)} %copy.64), channel_id=1, source_target_pairs={{0,8},{8,0},{16,24},{24,16},{1,9},{9,1},{17,25},{25,17},{2,10},{10... | collective-permute-start | bytes 1622024 | tf_op jit(solution)/shard_map/ppermute | solution.py:1165
  558.1 20.7 %collective-permute-start.32 = (bf16[256,1056]{0,1:T(8,128)(2,1)S(1)}, bf16[256,1056]{0,1:T(8,128)(2,1)S(1)}, u32[]{:S(2)}, u32[]{:S(2)}) collective-permute-start(bf16[256,1056]{0,1:T(8,128)(2,1)S(1)} %copy.64), channel_id=1, source_target_pairs={{0,16},{8,24},{16,0},{24,8},{1,17},{9,25},{17,1},{25,9},{2,18},{10... | collective-permute-start | bytes 1622024 | tf_op jit(solution)/shard_map/ppermute | solution.py:1165
  571.6 22.4 %collective-permute-start.28 = (bf16[256,640]{1,0:T(8,128)(2,1)}, bf16[256,640]{1,0:T(8,128)(2,1)}, u32[]{:S(2)}, u32[]{:S(2)}) collective-permute-start(bf16[256,640]{1,0:T(8,128)(2,1)} %get-tuple-element.201), channel_id=1, source_target_pairs={{0,8},{8,0},{16,24},{24,16},{1,9},{9,1},{17,25},{25,17},{2,10},{10... | collective-permute-start | bytes 983048 | tf_op jit(solution)/shard_map/ppermute | solution.py:1165
  572.2 21.8 %collective-permute-start.29 = (bf16[256,640]{1,0:T(8,128)(2,1)}, bf16[256,640]{1,0:T(8,128)(2,1)}, u32[]{:S(2)}, u32[]{:S(2)}) collective-permute-start(bf16[256,640]{1,0:T(8,128)(2,1)} %get-tuple-element.200), channel_id=1, source_target_pairs={{0,16},{8,24},{16,0},{24,8},{1,17},{9,25},{17,1},{25,9},{2,18},{10... | collective-permute-start | bytes 983048 | tf_op jit(solution)/shard_map/ppermute | solution.py:1165
  572.5 21.4 %collective-permute-start.30 = (bf16[256,640]{1,0:T(8,128)(2,1)}, bf16[256,640]{1,0:T(8,128)(2,1)}, u32[]{:S(2)}, u32[]{:S(2)}) collective-permute-start(bf16[256,640]{1,0:T(8,128)(2,1)} %get-tuple-element.199), channel_id=1, source_target_pairs={{0,24},{8,16},{16,8},{24,0},{1,25},{9,17},{17,9},{25,1},{2,26},{10... | collective-permute-start | bytes 983048 | tf_op jit(solution)/shard_map/ppermute | solution.py:1165
  577.3 14.2 %collective-permute-start.33 = (bf16[128,1056]{1,0:T(8,128)(2,1)}, bf16[128,1056]{1,0:T(8,128)(2,1)}, u32[]{:S(2)}, u32[]{:S(2)}) collective-permute-start(bf16[128,1056]{1,0:T(8,128)(2,1)} %slice.493), channel_id=1, source_target_pairs={{0,16},{8,24},{16,0},{24,8},{1,17},{9,25},{17,1},{25,9},{2,18},{10... | collective-permute-start | bytes 811016 | tf_op jit(solution)/shard_map/ppermute | solution.py:1165
  634.2 14.7 %collective-permute-start.24 = (bf16[128,2560]{1,0:T(8,128)(2,1)}, bf16[128,2560]{1,0:T(8,128)(2,1)}, u32[]{:S(2)}, u32[]{:S(2)}) collective-permute-start(bf16[128,2560]{1,0:T(8,128)(2,1)} %get-tuple-element.189), channel_id=1, source_target_pairs={{0,16},{8,24},{16,0},{24,8},{1,17},{9,25},{17,1},{25,9},{2,18},{10... | collective-permute-start | bytes 1966088 | tf_op jit(solution)/shard_map/ppermute | solution.py:1165
  635.7 14.4 %collective-permute-start.26 = (bf16[128,2560]{1,0:T(8,128)(2,1)}, bf16[128,2560]{1,0:T(8,128)(2,1)}, u32[]{:S(2)}, u32[]{:S(2)}) collective-permute-start(bf16[128,2560]{1,0:T(8,128)(2,1)} %get-tuple-element.188), channel_id=1, source_target_pairs={{0,8},{8,0},{16,24},{24,16},{1,9},{9,1},{17,25},{25,17},{2,10},{10... | collective-permute-start | bytes 1966088 | tf_op jit(solution)/shard_map/ppermute | solution.py:1165
  652.3 30.0 %collective-permute-start.25 = (bf16[256,2560]{1,0:T(8,128)(2,1)S(1)}, bf16[256,2560]{1,0:T(8,128)(2,1)S(1)}, u32[]{:S(2)}, u32[]{:S(2)}) collective-permute-start(bf16[256,2560]{1,0:T(8,128)(2,1)S(1)} %pad_maximum_fusion.5), channel_id=1, source_target_pairs={{0,8},{8,0},{16,24},{24,16},{1,9},{9,1},{17,25},{25,17},{2,10},{10... | collective-permute-start | bytes 3932168 | tf_op jit(solution)/shard_map/ppermute | solution.py:1165
  653.9 30.2 %collective-permute-start.27 = (bf16[256,2560]{1,0:T(8,128)(2,1)S(1)}, bf16[256,2560]{1,0:T(8,128)(2,1)S(1)}, u32[]{:S(2)}, u32[]{:S(2)}) collective-permute-start(bf16[256,2560]{1,0:T(8,128)(2,1)S(1)} %pad_maximum_fusion.6), channel_id=1, source_target_pairs={{0,16},{8,24},{16,0},{24,8},{1,17},{9,25},{17,1},{25,9},{2,18},{10... | collective-permute-start | bytes 3932168 | tf_op jit(solution)/shard_map/ppermute | solution.py:1165
  657.3 30.4 %collective-permute-start.41 = (bf16[80,1536]{1,0:T(8,128)(2,1)S(1)}, bf16[80,1536]{1,0:T(8,128)(2,1)S(1)}, u32[]{:S(2)}, u32[]{:S(2)}) collective-permute-start(bf16[80,1536]{1,0:T(8,128)(2,1)S(1)} %get-tuple-element.267), channel_id=1, source_target_pairs={{0,8},{8,0},{16,24},{24,16},{1,9},{9,1},{17,25},{25,17},{2,10},{10... | collective-permute-start | bytes 737288 | tf_op jit(solution)/shard_map/ppermute | solution.py:1165
  658.8 29.9 %collective-permute-start.42 = (bf16[80,1536]{1,0:T(8,128)(2,1)S(1)}, bf16[80,1536]{1,0:T(8,128)(2,1)S(1)}, u32[]{:S(2)}, u32[]{:S(2)}) collective-permute-start(bf16[80,1536]{1,0:T(8,128)(2,1)S(1)} %get-tuple-element.266), channel_id=1, source_target_pairs={{0,16},{8,24},{16,0},{24,8},{1,17},{9,25},{17,1},{25,9},{2,18},{10... | collective-permute-start | bytes 737288 | tf_op jit(solution)/shard_map/ppermute | solution.py:1165
  (115 other events, 951.7 us)
Sparse Core Ops, SparseCore 0:
  43.0 119.4 all-gather.1
  321.6 85.2 reduce-scatter.4
  432.0 98.1 reduce-scatter.6
  532.4 85.9 reduce-scatter.8
  620.6 83.0 reduce-scatter.10

commit v2 on v1

--- a/solution.py
+++ b/solution.py
@@ -1321,11 +1321,11 @@
     attention = [None] * group
     latents_next = latent_parts
     for at, j in enumerate((*reversed(others), 0)):
-        if at == 1:
+        if at == 0:
             latents_next, cot_near = lax.optimization_barrier((latents_next, cot_near))
             cot_parts = all_blocks(cotangent, cot_near, group)
-        if j == 0:
-            latents_next, _ = lax.optimization_barrier((latents_next, cot_parts[1:]))
+        if at == 1:
+            latents_next, cot_parts = lax.optimization_barrier((latents_next, cot_parts))
         attention[j] = attend(j, latents_next, tables, segs, query_w, keyval_w, out_proj)
         latents_next, _ = lax.optimization_barrier((latent_parts, attention[j][0]))
     out_terms = [part[0] for part in attention]
@@ -1406,6 +1406,11 @@
         blocks = [blocks[0]] + [hop(blocks[j], group, j) for j in others]
         return place(blocks, me).reshape((group,) + blocks[0].shape)
 
+    summed = [lax.psum_scatter(grad_cuts[0], "rep", scatter_dimension=0, tiled=True)]
+    grad_normed_mlp, summed[0] = lax.optimization_barrier((grad_normed_mlp, summed[0]))
+    for grad_cut in grad_cuts[1:]:
+        grad_cut, _ = lax.optimization_barrier((grad_cut, summed[-1]))
+        summed.append(lax.psum_scatter(grad_cut, "rep", scatter_dimension=0, tiled=True))
     grad_top = cotangent.astype(f32)
     grad_gain_mlp = jnp.sum(grad_normed_mlp * hidden * inv_hidden, axis=0)
     grad_hidden = grad_top + norm_back(grad_normed_mlp * gain_mlp, hidden, inv_hidden)
@@ -1428,14 +1433,17 @@
 
     near = near_blocks(grad_attn, group)
     back = [back_block(0, grad_attn)]
-    near, back = lax.optimization_barrier((near, back))
+    if fast:
+        act_late, _ = lax.optimization_barrier((act_all, grad_attn))
+        down_all = jnp.dot(
+            act_late[:, :hidden_part], down_proj, preferred_element_type=f32
+        ).astype(bf16)
+        down_terms = [down_all[j * seq_len : (j + 1) * seq_len] for j in range(group)]
+    near, back, down_terms = lax.optimization_barrier((near, back, down_terms))
     attn_parts = all_blocks(grad_attn, near, group)
     back += [back_block(j, attn_parts[j]) for j in others]
-    summed = []
-    for at, grad_cut in enumerate(grad_cuts):
-        if at:
-            grad_cut, _ = lax.optimization_barrier((grad_cut, (summed[-1], grad_attn)))
-        summed.append(lax.psum_scatter(grad_cut, "rep", scatter_dimension=0, tiled=True))
+    down_terms, _ = lax.optimization_barrier((down_terms, attn_parts[1:]))
+    block_out = (hidden + residual_scale * scatter_sum(down_terms, group)).astype(bf16)
     owned = [to_owner_rows(rows) for rows in summed]
 
     def unpack(q, second):
@@ -1451,9 +1459,35 @@
         [piece for second in (0, 1) for q in range(group) for piece in unpack(q, second)], axis=1
     )
     latent_terms = [part[0] for part in back]
-    grad_out = token_grad([part[3] for part in attention], attn_parts, 0, heads * HD, "out_grad")
-    grad_query = token_grad(latent_parts, [part[1] for part in back], 0, QR, "query_grad")
-    grad_keyval = token_grad(latent_parts, [part[2] for part in back], QR, KR, "keyval_grad")
+    grad_latent_low = scatter_sum(latent_terms, group)
+    grad_normed_query = grad_latent_low[:, :QR]
+    grad_normed_keyval = grad_latent_low[:, QR : QR + KR]
+    grad_key_rope = grad_latent_low[:, QR + KR + HD : QR + KR + HD + RD]
+    grad_gain_query = jnp.sum(grad_normed_query * query_lat * inv_query, axis=0)
+    grad_gain_keyval = jnp.sum(grad_normed_keyval * keyval_lat * inv_keyval, axis=0)
+    grad_latent_rows = jnp.concatenate(
+        [
+            norm_back(grad_normed_query * gain_query, query_lat, inv_query),
+            norm_back(grad_normed_keyval * gain_keyval, keyval_lat, inv_keyval),
+            grad_key_rope,
+        ],
+        axis=1,
+    ).astype(bf16)
+    grad_latent_parts = gather_blocks(grad_latent_rows, group)
+    block_out, grad_latent_parts = lax.optimization_barrier((block_out, grad_latent_parts))
+    grad_down, _ = lax.optimization_barrier((grad_down, (summed[-1], grad_latent_rows)))
+    down_total = lax.psum_scatter(grad_down, "rep", scatter_dimension=0, tiled=True)
+    mixed_late, late_query, late_keyval, _ = lax.optimization_barrier(
+        (
+            [part[3] for part in attention],
+            [part[1] for part in back],
+            [part[2] for part in back],
+            grad_latent_rows,
+        )
+    )
+    grad_out = token_grad(mixed_late, attn_parts, 0, heads * HD, "out_grad")
+    grad_query = token_grad(latent_parts, late_query, 0, QR, "query_grad")
+    grad_keyval = token_grad(latent_parts, late_keyval, QR, KR, "keyval_grad")
     query_rows = QR // (group * replicas)
     keyval_rows = KR // (group * replicas)
     unit = heads * LANES
@@ -1474,30 +1508,6 @@
     grad_out = grad_out.reshape(replicas, out_count, D)
     grad_out = [grad_out[:, :, k * unit : (k + 1) * unit] for k in range(out_units)]
 
-    grad_latent_low = scatter_sum(latent_terms, group)
-    grad_normed_query = grad_latent_low[:, :QR]
-    grad_normed_keyval = grad_latent_low[:, QR : QR + KR]
-    grad_key_rope = grad_latent_low[:, QR + KR + HD : QR + KR + HD + RD]
-    grad_gain_query = jnp.sum(grad_normed_query * query_lat * inv_query, axis=0)
-    grad_gain_keyval = jnp.sum(grad_normed_keyval * keyval_lat * inv_keyval, axis=0)
-    grad_latent_rows = jnp.concatenate(
-        [
-            norm_back(grad_normed_query * gain_query, query_lat, inv_query),
-            norm_back(grad_normed_keyval * gain_keyval, keyval_lat, inv_keyval),
-            grad_key_rope,
-        ],
-        axis=1,
-    ).astype(bf16)
-    grad_latent_parts = gather_blocks(grad_latent_rows, group)
-    act_late, _ = lax.optimization_barrier((act_all, grad_latent_rows))
-    if fast:
-        down_all = jnp.dot(
-            act_late[:, :hidden_part], down_proj, preferred_element_type=f32
-        ).astype(bf16)
-        down_terms = [down_all[j * seq_len : (j + 1) * seq_len] for j in range(group)]
-    block_out = (hidden + residual_scale * scatter_sum(down_terms, group)).astype(bf16)
-    grad_down, _ = lax.optimization_barrier((grad_down, (summed[-1], grad_latent_rows)))
-    down_total = lax.psum_scatter(grad_down, "rep", scatter_dimension=0, tiled=True)
     grad_normed_in = jnp.einsum(
         "tc,dc->td", grad_latent_rows, latent_w, preferred_element_type=f32
     )

time: 760 us -> 737 us (0.970)
  waiting for transfers between devices: 204 us -> 194 us
    reduce_scatter x1, waiting for transfers between devices: 0.01 us -> 39.2 us  [per_device(): last = lax.psum_scatter(last, 'rep', scatter_dimension=0, tiled=True)]
    ppermute x47, waiting for transfers between devices: 187 us -> 155 us  [hop(): lax.ppermute(array, 'shard', [(i, i ^ distance) for i in range(group)])]
    reduce_scatter x1, waiting for transfers between devices: 14.5 us -> 0.01 us  [per_device(): lax.psum_scatter(grad_down, 'rep', scatter_dimension=0, tiled=True)]
    unnamed x202 -> x214, local copies, waits for them, and re-layouts: 33.8 us -> 27.5 us
  transfers between devices with their start and end apart: 52 -> 52, of which waited for: 26 -> 25; matrix products, arithmetic and copies ran while one was open for 17% -> 17% of each run, Pallas kernels for 33% -> 33%
where the time goes in v2:
time: 737 us; the launch traced here: 728 us
  Pallas kernels  321 us (44%)
  waiting for transfers between devices  194 us (26%)
  local copies, waits for them, and re-layouts  71.4 us (10%)
  other arithmetic  55.8 us (8%)
  starting transfers between devices  46.9 us (6%)
  matrix products  22.6 us (3%)
  between operations  15.9 us (2%)
    ppermute x47, waiting for transfers between devices, hop(): lax.ppermute(array, 'shard', [(i, i ^ distance) for i in range(group)])  155 us
    pallas_call x2, Pallas kernels, layer_part(): pl.pallas_call(functools.partial(layer_kernel, group, tiles_from, tiles,...  99.2 us
    pallas_call x1, Pallas kernels, latent_front(): pl.pallas_call(functools.partial(latent_kernel, group), in_specs=[pl.Bloc...  85.8 us
    ppermute x47, starting transfers between devices, hop(): lax.ppermute(array, 'shard', [(i, i ^ distance) for i in range(group)])  46.7 us
    pallas_call x4, Pallas kernels, attend_back(): pl.pallas_call(functools.partial(attend_back_kernel, heads), grid=(1,), o...  42.5 us
    reduce_scatter x1, waiting for transfers between devices, per_device(): last = lax.psum_scatter(last, 'rep', scatter_dimension=0, tiled=True)  39.2 us
    pallas_call x4, Pallas kernels, attend(): pl.pallas_call(functools.partial(attend_kernel, heads), grid=(1,), out_sp...  34.9 us
    pallas_call x1, Pallas kernels, hidden_pieces(): pl.pallas_call(functools.partial(columns_kernel, group, replicas, hidden,...  32.4 us
  transfers between devices with their start and end apart: 52, of which 25 were waited for; matrix products, arithmetic and copies ran while one was open for 17% of the time, Pallas kernels for 33%

profile of v2, /device:TPU:0, one launch (start us, length us, event | category | flops | bytes accessed | tf_op | source)
XLA Modules:
  0.0 728.0 jit_solution(8015094493119270897)
XLA Ops:
  9.3 32.4 %hidden_pieces.1 = (bf16[640,3328]{1,0:T(8,128)(2,1)}, bf16[80,9984]{1,0:T(8,128)(2,1)S(1)}, f32[32,1536]{1,0:T(8,128)S(1)}, f32[4,8,256]{2,1,0:T(8,128)S(1)}, f32[4,3,256,128]{3,2,1,0:T(8,128)S(1)}) custom-call(bf16[640,12800]{1,0:T(8,128)(2,1)} %gate_up_ref.1, f32[8,1536]{1,0:T(8,128)S(1)} %broadcast_in_dim.12.gains_ref, ...), custom_call_target="tpu_custom_call" | custom-call | bytes 100000000 | tf_op jit(solution)/shard_map/hidden_pieces/pallas_call | solution.py:938
  49.5 5.2 reshape.174
  58.7 85.8 %latent_front.1 = (bf16[4,256,1152]{2,1,0:T(8,128)(2,1)}, f32[256,1056]{1,0:T(8,128)S(1)}, bf16[256,2560]{1,0:T(8,128)(2,1)S(1)}, bf16[2560,1056]{1,0:T(8,128)(2...) custom-call(bf16[256,2560]{1,0:T(8,128)(2,1)S(1)} %copy-done.2, f32[1,2560]{1,0:T(1,128)S(1)} %reshape.172.gains_ref, ...), custom_call_target="tpu_custom_call" | custom-call | flops 1384120320 | bytes 60000000 | tf_op jit(solution)/shard_map/latent_front/pallas_call | solution.py:1134
  149.7 8.6 %attend.4 = (bf16[256,2560]{1,0:T(8,128)(2,1)S(1)}, bf16[256,1280]{1,0:T(8,128)(2,1)S(1)}, bf16[256,1280]{1,0:T(8,128)(2,1)S(1)}, bf16[256,640]{1,0:T(8,128)(2,1)S(1)}) custom-call(bf16[4,256,1152]{2,1,0:T(8,128)(2,1)} %get-tuple-element.136.latent_ref.refs_0_.refs_1_.refs_2_.refs_3_, f32[4,3,256,128]{3,2,1,0:T(8,128)S(1)} %get-tuple-element.120.table_ref, ...), custom_call_target="tpu_custom_call" | custom-call | flops 1845493760 | bytes 7208960 | tf_op jit(solution)/shard_map/attend/pallas_call | solution.py:557
  167.3 9.0 %attend.5 = (bf16[256,2560]{1,0:T(8,128)(2,1)S(1)}, bf16[256,1280]{1,0:T(8,128)(2,1)S(1)}, bf16[256,1280]{1,0:T(8,128)(2,1)S(1)}, bf16[256,640]{1,0:T(8,128)(2,1)S(1)}) custom-call(bf16[4,256,1152]{2,1,0:T(8,128)(2,1)} %get-tuple-element.136.latent_ref.refs_0_.refs_1_.refs_2_.refs_3_, f32[4,3,256,128]{3,2,1,0:T(8,128)S(1)} %get-tuple-element.120.table_ref, ...), custom_call_target="tpu_custom_call" | custom-call | flops 1845493760 | bytes 7208960 | tf_op jit(solution)/shard_map/attend/pallas_call | solution.py:557
  178.8 8.6 %attend.6 = (bf16[256,2560]{1,0:T(8,128)(2,1)S(1)}, bf16[256,1280]{1,0:T(8,128)(2,1)S(1)}, bf16[256,1280]{1,0:T(8,128)(2,1)S(1)}, bf16[256,640]{1,0:T(8,128)(2,1)S(1)}) custom-call(bf16[4,256,1152]{2,1,0:T(8,128)(2,1)} %get-tuple-element.136.latent_ref.refs_0_.refs_1_.refs_2_.refs_3_, f32[4,3,256,128]{3,2,1,0:T(8,128)S(1)} %get-tuple-element.120.table_ref, ...), custom_call_target="tpu_custom_call" | custom-call | flops 1845493760 | bytes 7208960 | tf_op jit(solution)/shard_map/attend/pallas_call | solution.py:557
  188.7 8.6 %attend.7 = (bf16[256,2560]{1,0:T(8,128)(2,1)S(1)}, bf16[256,1280]{1,0:T(8,128)(2,1)S(1)}, bf16[256,1280]{1,0:T(8,128)(2,1)S(1)}, bf16[256,640]{1,0:T(8,128)(2,1)S(1)}) custom-call(bf16[4,256,1152]{2,1,0:T(8,128)(2,1)} %get-tuple-element.136.latent_ref.refs_0_.refs_1_.refs_2_.refs_3_, f32[4,3,256,128]{3,2,1,0:T(8,128)S(1)} %get-tuple-element.120.table_ref, ...), custom_call_target="tpu_custom_call" | custom-call | flops 1845493760 | bytes 7208960 | tf_op jit(solution)/shard_map/attend/pallas_call | solution.py:557
  197.4 7.2 collective-permute-done.7
  204.5 10.6 %collective-permute-done.5 = bf16[256,2560]{1,0:T(8,128)(2,1)S(1)} collective-permute-done((bf16[256,2560]{1,0:T(8,128)(2,1)S(1)}, bf16[256,2560]{1,0:T(8,128)(2,1)S(1)}, u32[]{:S(2)}, u32[]{:S(2)}) %collective-permute-start.5) | collective-permute-done | bytes 1310752 | tf_op jit(solution)/shard_map/ppermute | solution.py:1165
  218.5 24.7 %collective-permute-done.8.refs_1_ = bf16[256,2560]{1,0:T(8,128)(2,1)S(1)} collective-permute-done((bf16[256,2560]{1,0:T(8,128)(2,1)S(1)}, bf16[256,2560]{1,0:T(8,128)(2,1)S(1)}, u32[]{:S(2)}, u32[]{:S(2)}) %collective-permute-start.8) | collective-permute-done | bytes 1310752 | tf_op jit(solution)/shard_map/ppermute | solution.py:1165
  247.4 8.1 %collective-permute-done.10 = bf16[128,2560]{1,0:T(8,128)(2,1)} collective-permute-done((bf16[128,2560]{1,0:T(8,128)(2,1)}, bf16[128,2560]{1,0:T(8,128)(2,1)}, u32[]{:S(2)}, u32[]{:S(2)}) %collective-permute-start.10) | collective-permute-done | bytes 655392 | tf_op jit(solution)/shard_map/ppermute | solution.py:1165
  259.5 44.7 %layer_part.2 = (bf16[1024,1664]{1,0:T(8,128)(2,1)}, bf16[8,4,80,1536]{3,2,1,0:T(8,128)(2,1)}, f32[1024,2560]{1,0:T(8,128)}) custom-call(s32[4]{0:T(128)} %pad_add_fusion.order_ref, bf16[256,2560]{1,0:T(8,128)(2,1)} %copy-done.60, bf16[256,2560]{1,0:T(8,128)(2,1)} %copy-done.67, bf16[256,2560]{1,0:T(8,128)(2,1)} %copy-done.68, ...), custom_call_target="tpu_custom_call" | custom-call | flops 28185722880 | bytes 65536000 | tf_op jit(solution)/shard_map/layer_part/pallas_call | solution.py:415
  304.3 54.4 %layer_part.3 = (bf16[1024,1664]{1,0:T(8,128)(2,1)}, bf16[8,4,80,1792]{3,2,1,0:T(8,128)(2,1)}, bf16[1024,2560]{1,0:T(8,128)(2,1)}) custom-call(s32[4]{0:T(128)} %pad_add_fusion.order_ref, bf16[256,2560]{1,0:T(8,128)(2,1)} %copy-done.60, bf16[256,2560]{1,0:T(8,128)(2,1)} %copy-done.67, ...), custom_call_target="tpu_custom_call", output_to_operand_aliasing={{0}: (19, {})} | custom-call | flops 30534533120 | bytes 67502080 | tf_op jit(solution)/shard_map/layer_part/pallas_call | solution.py:415
  362.6 12.2 %collective-permute-done.12 = bf16[128,2560]{1,0:T(8,128)(2,1)S(1)} collective-permute-done((bf16[128,2560]{1,0:T(8,128)(2,1)S(1)}, bf16[128,2560]{1,0:T(8,128)(2,1)S(1)}, u32[]{:S(2)}, u32[]{:S(2)}) %collective-permute-start.12) | collective-permute-done | bytes 655392 | tf_op jit(solution)/shard_map/ppermute | solution.py:1165
  378.6 20.9 %collective-permute-done.15 = bf16[256,2560]{1,0:T(8,128)(2,1)S(1)} collective-permute-done((bf16[256,2560]{1,0:T(8,128)(2,1)S(1)}, bf16[256,2560]{1,0:T(8,128)(2,1)S(1)}, u32[]{:S(2)}, u32[]{:S(2)}) %collective-permute-start.15) | collective-permute-done | bytes 1310752 | tf_op jit(solution)/shard_map/ppermute | solution.py:1165
  404.1 14.9 %down_grad.1 = bf16[1600,2560]{1,0:T(8,128)(2,1)} custom-call(bf16[1024,1664]{1,0:T(8,128)(2,1)} %get-tuple-element.155.act_ref, bf16[256,2560]{1,0:T(8,128)(2,1)} %refs_0_, bf16[256,2560]{1,0:T(8,128)(2,1)} %collective-permute-done.refs_5_.refs_1_, bf16[256,2560]{1,0:T(8,128)(2,1)} %collective-permute-done.1.refs_6_.refs_2_, bf16[256,2560]{1,0:T(8,128)(2,1)S(1)} %copy-done.6), custom_call_target="tpu_custom_call" | custom-call | flops 8388608000 | bytes 16711680 | tf_op jit(solution)/shard_map/down_grad/pallas_call | solution.py:456
  427.3 12.3 %convolution_convert_fusion = bf16[1024,2560]{1,0:T(8,128)(2,1)S(1)} fusion(bf16[1600,2560]{1,0:T(8,128)(2,1)} %refs_17_.1, bf16[1024,1664]{1,0:T(8,128)(2,1)S(1)} %copy-done.65), kind=kOutput, calls=%fused_computation.1 | convolution fusion | flops 8391229440 | bytes 16842752 | tf_op jit(solution)/shard_map/dot_general | solution.py:1438
  439.6 10.3 %attend_back.4 = (bf16[256,1152]{1,0:T(8,128)(2,1)S(1)}, bf16[256,1280]{1,0:T(8,128)(2,1)S(1)}, bf16[256,1280]{1,0:T(8,128)(2,1)S(1)}) custom-call(bf16[256,2560]{1,0:T(8,128)(2,1)S(1)} %multiply_convert_fusion.grad_ref.refs_4_, bf16[256,1280]{1,0:T(8,128)(2,1)S(1)} %copy-done.37, bf16[256,1280]{1,0:T(8,128)(2,1)S(1)} %copy-done.39, ...), custom_call_target="tpu_custom_call" | custom-call | flops 2348810240 | bytes 7208960 | tf_op jit(solution)/shard_map/attend_back/pallas_call | solution.py:642
  455.2 7.9 %collective-permute-done.18 = bf16[128,2560]{1,0:T(8,128)(2,1)S(1)} collective-permute-done((bf16[128,2560]{1,0:T(8,128)(2,1)S(1)}, bf16[128,2560]{1,0:T(8,128)(2,1)S(1)}, u32[]{:S(2)}, u32[]{:S(2)}) %collective-permute-start.18) | collective-permute-done | bytes 655392 | tf_op jit(solution)/shard_map/ppermute | solution.py:1165
  464.2 11.2 %attend_back.6 = (bf16[256,1152]{1,0:T(8,128)(2,1)S(1)}, bf16[256,1280]{1,0:T(8,128)(2,1)S(1)}, bf16[256,1280]{1,0:T(8,128)(2,1)S(1)}) custom-call(bf16[256,2560]{1,0:T(8,128)(2,1)S(1)} %constant_dynamic-update-slice_fusion.2.grad_ref.refs_7_, bf16[256,1280]{1,0:T(8,128)(2,1)S(1)} %get-tuple-element.171.query_ref, bf16[256,1280]{1,0:T(8,128)(2,1)S(1)} %copy-done.19, ...), custom_call_target="tpu_custom_call" | custom-call | flops 2348810240 | bytes 7208960 | tf_op jit(solution)/shard_map/attend_back/pallas_call | solution.py:642
  477.9 10.3 %attend_back.7 = (bf16[256,1152]{1,0:T(8,128)(2,1)S(1)}, bf16[256,1280]{1,0:T(8,128)(2,1)S(1)}, bf16[256,1280]{1,0:T(8,128)(2,1)S(1)}) custom-call(bf16[256,2560]{1,0:T(8,128)(2,1)S(1)} %collective-permute-done.17.grad_ref.refs_6_, bf16[256,1280]{1,0:T(8,128)(2,1)S(1)} %copy-done.21, bf16[256,1280]{1,0:T(8,128)(2,1)S(1)} %copy-done.23, ...), custom_call_target="tpu_custom_call" | custom-call | flops 2348810240 | bytes 7208960 | tf_op jit(solution)/shard_map/attend_back/pallas_call | solution.py:642
  489.2 10.6 %attend_back.5 = (bf16[256,1152]{1,0:T(8,128)(2,1)S(1)}, bf16[256,1280]{1,0:T(8,128)(2,1)S(1)}, bf16[256,1280]{1,0:T(8,128)(2,1)S(1)}) custom-call(bf16[256,2560]{1,0:T(8,128)(2,1)S(1)} %collective-permute-done.16.grad_ref.refs_5_, bf16[256,1280]{1,0:T(8,128)(2,1)S(1)} %copy-done.25, bf16[256,1280]{1,0:T(8,128)(2,1)S(1)} %copy-done.27, ...), custom_call_target="tpu_custom_call" | custom-call | flops 2348810240 | bytes 7208960 | tf_op jit(solution)/shard_map/attend_back/pallas_call | solution.py:642
  507.8 5.2 collective-permute-done.27
  513.0 7.6 %collective-permute-done.25 = bf16[256,1152]{1,0:T(8,128)(2,1)S(1)} collective-permute-done((bf16[256,1152]{1,0:T(8,128)(2,1)S(1)}, bf16[256,1152]{1,0:T(8,128)(2,1)S(1)}, u32[]{:S(2)}, u32[]{:S(2)}) %collective-permute-start.25) | collective-permute-done | bytes 589856 | tf_op jit(solution)/shard_map/ppermute | solution.py:1165
  528.1 12.3 %collective-permute-done.22 = bf16[128,2560]{1,0:T(8,128)(2,1)} collective-permute-done((bf16[128,2560]{1,0:T(8,128)(2,1)}, bf16[128,2560]{1,0:T(8,128)(2,1)}, u32[]{:S(2)}, u32[]{:S(2)}) %collective-permute-start.22) | collective-permute-done | bytes 655392 | tf_op jit(solution)/shard_map/ppermute | solution.py:1165
  561.4 7.0 fusion.13
  571.4 6.6 out_grad.1
  600.3 7.1 fusion.10
  627.0 6.6 collective-permute-done.42
  650.5 8.0 %convert_subtract_fusion = (f32[80,12800]{1,0:T(8,128)}, f32[80,12800]{1,0:T(8,128)}, f32[80,12800]{1,0:T(8,128)}) fusion(bf16[640,12800]{1,0:T(8,128)(2,1)} %gate_up_ref.1, s32[]{:T(128)S(6)} %select_n.81, bf16[80,12800]{1,0:T(8,128)(2,1)S(1)} %concatenate.80, bf16[80,12800]{1,0:T(8,128)(2,1)} %param.39, bf16[80,12800]{1,0:T(8,128)(2,1)} %param.46), kind=kLoop, calls=%fused_computation.8 | loop fusion | flops 19456000 | bytes 20480004 | tf_op jit(solution)/shard_map/sub | solution.py:64
  658.5 5.2 convert_subtract_fusion.1
  663.7 39.2 %reduce-scatter.11.cloned.1.call-done = bf16[384,1280]{1,0:T(8,128)(2,1)} async-done(((bf16[3072,1280]{1,0:T(8,128)(2,1)}), bf16[384,1280]{1,0:T(8,128)(2,1)}) %reduce-scatter.11.cloned.1.call-update) | async-done | bytes 983056 | tf_op jit(solution)/shard_map/reduce_scatter | solution.py:1537
  (434 shorter events, 188.5 us)
Async XLA Ops:
  7.2 252.3 %all-gather.2.cloned.1.call-start = ((), (), s32[]{:S(2)}) async-start(), calls=%async_computation.4 | async-start | bytes 14376960 | tf_op jit(solution)/shard_map/all_gather | solution.py:1296
  42.9 359.9 %reduce-scatter.5.cloned.1.call-start = ((), (), s32[]{:S(2)}) async-start(), calls=%async_computation.5 | async-start | bytes 8847360 | tf_op jit(solution)/shard_map/reduce_scatter | solution.py:1409
  42.9 102.7 %collective-permute-start = (bf16[256,2560]{1,0:T(8,128)(2,1)}, bf16[256,2560]{1,0:T(8,128)(2,1)}, u32[]{:S(2)}, u32[]{:S(2)}) collective-permute-start(bf16[256,2560]{1,0:T(8,128)(2,1)} %refs_0_), channel_id=1, source_target_pairs={{0,8},{8,0},{16,24},{24,16},{1,9},{9,1},{17,25},{25,17},{2,10},{10... | collective-permute-start | bytes 3932168 | tf_op jit(solution)/shard_map/ppermute | solution.py:1165
  44.4 101.2 %collective-permute-start.1 = (bf16[256,2560]{1,0:T(8,128)(2,1)}, bf16[256,2560]{1,0:T(8,128)(2,1)}, u32[]{:S(2)}, u32[]{:S(2)}) collective-permute-start(bf16[256,2560]{1,0:T(8,128)(2,1)} %refs_0_), channel_id=1, source_target_pairs={{0,16},{8,24},{16,0},{24,8},{1,17},{9,25},{17,1},{25,9},{2,18},{10... | collective-permute-start | bytes 3932168 | tf_op jit(solution)/shard_map/ppermute | solution.py:1165
  147.2 15.0 %collective-permute-start.3 = (bf16[128,2560]{1,0:T(8,128)(2,1)S(1)}, bf16[128,2560]{1,0:T(8,128)(2,1)S(1)}, u32[]{:S(2)}, u32[]{:S(2)}) collective-permute-start(bf16[128,2560]{1,0:T(8,128)(2,1)S(1)} %slice.365), channel_id=1, source_target_pairs={{0,8},{8,0},{16,24},{24,16},{1,9},{9,1},{17,25},{25,17},{2,10},{10... | collective-permute-start | bytes 1966088 | tf_op jit(solution)/shard_map/ppermute | solution.py:1165
  148.4 17.7 %collective-permute-start.2 = (bf16[128,2560]{1,0:T(8,128)(2,1)S(1)}, bf16[128,2560]{1,0:T(8,128)(2,1)S(1)}, u32[]{:S(2)}, u32[]{:S(2)}) collective-permute-start(bf16[128,2560]{1,0:T(8,128)(2,1)S(1)} %slice.364), channel_id=1, source_target_pairs={{0,16},{8,24},{16,0},{24,8},{1,17},{9,25},{17,1},{25,9},{2,18},{10... | collective-permute-start | bytes 1966088 | tf_op jit(solution)/shard_map/ppermute | solution.py:1165
  158.5 18.0 %collective-permute-start.6 = (bf16[128,2560]{1,0:T(8,128)(2,1)S(1)}, bf16[128,2560]{1,0:T(8,128)(2,1)S(1)}, u32[]{:S(2)}, u32[]{:S(2)}) collective-permute-start(bf16[128,2560]{1,0:T(8,128)(2,1)S(1)} %get-tuple-element.266), channel_id=1, source_target_pairs={{0,8},{8,0},{16,24},{24,16},{1,9},{9,1},{17,25},{25,17},{2,10},{10... | collective-permute-start | bytes 1966088 | tf_op jit(solution)/shard_map/ppermute | solution.py:1165
  159.4 28.1 %collective-permute-start.4 = (bf16[128,2560]{1,0:T(8,128)(2,1)S(1)}, bf16[128,2560]{1,0:T(8,128)(2,1)S(1)}, u32[]{:S(2)}, u32[]{:S(2)}) collective-permute-start(bf16[128,2560]{1,0:T(8,128)(2,1)S(1)} %get-tuple-element.265), channel_id=1, source_target_pairs={{0,16},{8,24},{16,0},{24,8},{1,17},{9,25},{17,1},{25,9},{2,18},{10... | collective-permute-start | bytes 1966088 | tf_op jit(solution)/shard_map/ppermute | solution.py:1165
  177.5 27.0 %collective-permute-start.7 = (bf16[256,2560]{1,0:T(8,128)(2,1)S(1)}, bf16[256,2560]{1,0:T(8,128)(2,1)S(1)}, u32[]{:S(2)}, u32[]{:S(2)}) collective-permute-start(bf16[256,2560]{1,0:T(8,128)(2,1)S(1)} %pad_maximum_fusion.3), channel_id=1, source_target_pairs={{0,16},{8,24},{16,0},{24,8},{1,17},{9,25},{17,1},{25,9},{2,18},{10... | collective-permute-start | bytes 3932168 | tf_op jit(solution)/shard_map/ppermute | solution.py:1165
  188.6 26.6 %collective-permute-start.5 = (bf16[256,2560]{1,0:T(8,128)(2,1)S(1)}, bf16[256,2560]{1,0:T(8,128)(2,1)S(1)}, u32[]{:S(2)}, u32[]{:S(2)}) collective-permute-start(bf16[256,2560]{1,0:T(8,128)(2,1)S(1)} %pad_maximum_fusion.2), channel_id=1, source_target_pairs={{0,8},{8,0},{16,24},{24,16},{1,9},{9,1},{17,25},{25,17},{2,10},{10... | collective-permute-start | bytes 3932168 | tf_op jit(solution)/shard_map/ppermute | solution.py:1165
  217.4 25.8 %collective-permute-start.8 = (bf16[256,2560]{1,0:T(8,128)(2,1)S(1)}, bf16[256,2560]{1,0:T(8,128)(2,1)S(1)}, u32[]{:S(2)}, u32[]{:S(2)}) collective-permute-start(bf16[256,2560]{1,0:T(8,128)(2,1)S(1)} %multiply_convert_fusion.1.refs_0_), channel_id=1, source_target_pairs={{0,8},{8,0},{16,24},{24,16},{1,9},{9,1},{17,25},{25,17},{2,10},{10... | collective-permute-start | bytes 3932168 | tf_op jit(solution)/shard_map/ppermute | solution.py:1165
  217.6 27.4 %collective-permute-start.9 = (bf16[256,2560]{1,0:T(8,128)(2,1)S(1)}, bf16[256,2560]{1,0:T(8,128)(2,1)S(1)}, u32[]{:S(2)}, u32[]{:S(2)}) collective-permute-start(bf16[256,2560]{1,0:T(8,128)(2,1)S(1)} %multiply_convert_fusion.1.refs_0_), channel_id=1, source_target_pairs={{0,16},{8,24},{16,0},{24,8},{1,17},{9,25},{17,1},{25,9},{2,18},{10... | collective-permute-start | bytes 3932168 | tf_op jit(solution)/shard_map/ppermute | solution.py:1165
  304.2 219.4 %reduce-scatter.7.cloned.1.call-start = ((), (), s32[]{:S(2)}) async-start(), calls=%async_computation.6 | async-start | bytes 10321920 | tf_op jit(solution)/shard_map/reduce_scatter | solution.py:1413
  360.8 14.0 %collective-permute-start.12 = (bf16[128,2560]{1,0:T(8,128)(2,1)S(1)}, bf16[128,2560]{1,0:T(8,128)(2,1)S(1)}, u32[]{:S(2)}, u32[]{:S(2)}) collective-permute-start(bf16[128,2560]{1,0:T(8,128)(2,1)S(1)} %get-tuple-element.253), channel_id=1, source_target_pairs={{0,16},{8,24},{16,0},{24,8},{1,17},{9,25},{17,1},{25,9},{2,18},{10... | collective-permute-start | bytes 1966088 | tf_op jit(solution)/shard_map/ppermute | solution.py:1165
  362.1 15.0 %collective-permute-start.14 = (bf16[128,2560]{1,0:T(8,128)(2,1)S(1)}, bf16[128,2560]{1,0:T(8,128)(2,1)S(1)}, u32[]{:S(2)}, u32[]{:S(2)}) collective-permute-start(bf16[128,2560]{1,0:T(8,128)(2,1)S(1)} %get-tuple-element.252), channel_id=1, source_target_pairs={{0,8},{8,0},{16,24},{24,16},{1,9},{9,1},{17,25},{25,17},{2,10},{10... | collective-permute-start | bytes 1966088 | tf_op jit(solution)/shard_map/ppermute | solution.py:1165
  377.6 21.9 %collective-permute-start.15 = (bf16[256,2560]{1,0:T(8,128)(2,1)S(1)}, bf16[256,2560]{1,0:T(8,128)(2,1)S(1)}, u32[]{:S(2)}, u32[]{:S(2)}) collective-permute-start(bf16[256,2560]{1,0:T(8,128)(2,1)S(1)} %pad_maximum_fusion.5), channel_id=1, source_target_pairs={{0,16},{8,24},{16,0},{24,8},{1,17},{9,25},{17,1},{25,9},{2,18},{10... | collective-permute-start | bytes 3932168 | tf_op jit(solution)/shard_map/ppermute | solution.py:1165
  377.8 23.0 %collective-permute-start.13 = (bf16[256,2560]{1,0:T(8,128)(2,1)S(1)}, bf16[256,2560]{1,0:T(8,128)(2,1)S(1)}, u32[]{:S(2)}, u32[]{:S(2)}) collective-permute-start(bf16[256,2560]{1,0:T(8,128)(2,1)S(1)} %pad_maximum_fusion.4), channel_id=1, source_target_pairs={{0,8},{8,0},{16,24},{24,16},{1,9},{9,1},{17,25},{25,17},{2,10},{10... | collective-permute-start | bytes 3932168 | tf_op jit(solution)/shard_map/ppermute | solution.py:1165
  402.8 213.9 %reduce-scatter.9.cloned.1.call-start = ((), (), s32[]{:S(2)}) async-start(), calls=%async_computation.7 | async-start | bytes 9216000 | tf_op jit(solution)/shard_map/reduce_scatter | solution.py:1479
  425.7 26.6 %collective-permute-start.16 = (bf16[256,2560]{1,0:T(8,128)(2,1)S(1)}, bf16[256,2560]{1,0:T(8,128)(2,1)S(1)}, u32[]{:S(2)}, u32[]{:S(2)}) collective-permute-start(bf16[256,2560]{1,0:T(8,128)(2,1)S(1)} %multiply_convert_fusion.grad_ref.refs_4_), channel_id=1, source_target_pairs={{0,8},{8,0},{16,24},{24,16},{1,9},{9,1},{17,25},{25,17},{2,10},{10... | collective-permute-start | bytes 3932168 | tf_op jit(solution)/shard_map/ppermute | solution.py:1165
  426.3 26.0 %collective-permute-start.17 = (bf16[256,2560]{1,0:T(8,128)(2,1)S(1)}, bf16[256,2560]{1,0:T(8,128)(2,1)S(1)}, u32[]{:S(2)}, u32[]{:S(2)}) collective-permute-start(bf16[256,2560]{1,0:T(8,128)(2,1)S(1)} %multiply_convert_fusion.grad_ref.refs_4_), channel_id=1, source_target_pairs={{0,16},{8,24},{16,0},{24,8},{1,17},{9,25},{17,1},{25,9},{2,18},{10... | collective-permute-start | bytes 3932168 | tf_op jit(solution)/shard_map/ppermute | solution.py:1165
  476.3 24.5 %collective-permute-start.26 = (bf16[128,1152]{1,0:T(8,128)(2,1)S(1)}, bf16[128,1152]{1,0:T(8,128)(2,1)S(1)}, u32[]{:S(2)}, u32[]{:S(2)}) collective-permute-start(bf16[128,1152]{1,0:T(8,128)(2,1)S(1)} %get-tuple-element.334), channel_id=1, source_target_pairs={{0,8},{8,0},{16,24},{24,16},{1,9},{9,1},{17,25},{25,17},{2,10},{10... | collective-permute-start | bytes 884744 | tf_op jit(solution)/shard_map/ppermute | solution.py:1165
  506.8 13.8 %collective-permute-start.25 = (bf16[256,1152]{1,0:T(8,128)(2,1)S(1)}, bf16[256,1152]{1,0:T(8,128)(2,1)S(1)}, u32[]{:S(2)}, u32[]{:S(2)}) collective-permute-start(bf16[256,1152]{1,0:T(8,128)(2,1)S(1)} %pad_maximum_fusion.8), channel_id=1, source_target_pairs={{0,8},{8,0},{16,24},{24,16},{1,9},{9,1},{17,25},{25,17},{2,10},{10... | collective-permute-start | bytes 1769480 | tf_op jit(solution)/shard_map/ppermute | solution.py:1165
  523.6 179.3 %reduce-scatter.11.cloned.1.call-start = ((), (), s32[]{:S(2)}) async-start(), calls=%async_computation.8 | async-start | bytes 8847360 | tf_op jit(solution)/shard_map/reduce_scatter | solution.py:1537
  524.8 15.6 %collective-permute-start.22 = (bf16[128,2560]{1,0:T(8,128)(2,1)}, bf16[128,2560]{1,0:T(8,128)(2,1)}, u32[]{:S(2)}, u32[]{:S(2)}) collective-permute-start(bf16[128,2560]{1,0:T(8,128)(2,1)} %get-tuple-element.264), channel_id=1, source_target_pairs={{0,8},{8,0},{16,24},{24,16},{1,9},{9,1},{17,25},{25,17},{2,10},{10... | collective-permute-start | bytes 1966088 | tf_op jit(solution)/shard_map/ppermute | solution.py:1165
  527.3 17.7 %collective-permute-start.20 = (bf16[128,2560]{1,0:T(8,128)(2,1)S(1)}, bf16[128,2560]{1,0:T(8,128)(2,1)S(1)}, u32[]{:S(2)}, u32[]{:S(2)}) collective-permute-start(bf16[128,2560]{1,0:T(8,128)(2,1)S(1)} %copy-done.77), channel_id=1, source_target_pairs={{0,16},{8,24},{16,0},{24,8},{1,17},{9,25},{17,1},{25,9},{2,18},{10... | collective-permute-start | bytes 1966088 | tf_op jit(solution)/shard_map/ppermute | solution.py:1165
  542.8 57.4 %collective-permute-start.23 = (bf16[256,2560]{1,0:T(8,128)(2,1)}, bf16[256,2560]{1,0:T(8,128)(2,1)}, u32[]{:S(2)}, u32[]{:S(2)}) collective-permute-start(bf16[256,2560]{1,0:T(8,128)(2,1)} %pad_maximum_fusion.7), channel_id=1, source_target_pairs={{0,16},{8,24},{16,0},{24,8},{1,17},{9,25},{17,1},{25,9},{2,18},{10... | collective-permute-start | bytes 3932168 | tf_op jit(solution)/shard_map/ppermute | solution.py:1165
  546.3 53.9 %collective-permute-start.21 = (bf16[256,2560]{1,0:T(8,128)(2,1)}, bf16[256,2560]{1,0:T(8,128)(2,1)}, u32[]{:S(2)}, u32[]{:S(2)}) collective-permute-start(bf16[256,2560]{1,0:T(8,128)(2,1)} %pad_maximum_fusion.6), channel_id=1, source_target_pairs={{0,8},{8,0},{16,24},{24,16},{1,9},{9,1},{17,25},{25,17},{2,10},{10... | collective-permute-start | bytes 3932168 | tf_op jit(solution)/shard_map/ppermute | solution.py:1165
  549.9 34.7 %collective-permute-start.28 = (bf16[256,1056]{0,1:T(8,128)(2,1)}, bf16[256,1056]{0,1:T(8,128)(2,1)}, u32[]{:S(2)}, u32[]{:S(2)}) collective-permute-start(bf16[256,1056]{0,1:T(8,128)(2,1)} %copy.61), channel_id=1, source_target_pairs={{0,8},{8,0},{16,24},{24,16},{1,9},{9,1},{17,25},{25,17},{2,10},{10... | collective-permute-start | bytes 1622024 | tf_op jit(solution)/shard_map/ppermute | solution.py:1165
  550.4 31.8 %collective-permute-start.29 = (bf16[256,1056]{0,1:T(8,128)(2,1)}, bf16[256,1056]{0,1:T(8,128)(2,1)S(1)}, u32[]{:S(2)}, u32[]{:S(2)}) collective-permute-start(bf16[256,1056]{0,1:T(8,128)(2,1)} %copy.61), channel_id=1, source_target_pairs={{0,16},{8,24},{16,0},{24,8},{1,17},{9,25},{17,1},{25,9},{2,18},{10... | collective-permute-start | bytes 1622024 | tf_op jit(solution)/shard_map/ppermute | solution.py:1165
  569.1 17.2 %collective-permute-start.37 = (bf16[1536]{0:T(1024)(128)(2,1)}, bf16[1536]{0:T(1024)(128)(2,1)S(1)}, u32[]{:S(2)}, u32[]{:S(2)}) collective-permute-start(bf16[1536]{0:T(1024)(128)(2,1)} %get-tuple-element.340), channel_id=1, source_target_pairs={{0,24},{8,16},{16,8},{24,0},{1,25},{9,17},{17,9},{25,1},{2,26},{10... | collective-permute-start | bytes 9224 | tf_op jit(solution)/shard_map/ppermute | solution.py:1165
  589.8 20.0 %collective-permute-start.34 = (bf16[256,640]{1,0:T(8,128)(2,1)}, bf16[256,640]{1,0:T(8,128)(2,1)}, u32[]{:S(2)}, u32[]{:S(2)}) collective-permute-start(bf16[256,640]{1,0:T(8,128)(2,1)} %get-tuple-element.259), channel_id=1, source_target_pairs={{0,24},{8,16},{16,8},{24,0},{1,25},{9,17},{17,9},{25,1},{2,26},{10... | collective-permute-start | bytes 983048 | tf_op jit(solution)/shard_map/ppermute | solution.py:1165
  593.2 16.6 %collective-permute-start.33 = (bf16[256,640]{1,0:T(8,128)(2,1)}, bf16[256,640]{1,0:T(8,128)(2,1)}, u32[]{:S(2)}, u32[]{:S(2)}) collective-permute-start(bf16[256,640]{1,0:T(8,128)(2,1)} %get-tuple-element.260), channel_id=1, source_target_pairs={{0,16},{8,24},{16,0},{24,8},{1,17},{9,25},{17,1},{25,9},{2,18},{10... | collective-permute-start | bytes 983048 | tf_op jit(solution)/shard_map/ppermute | solution.py:1165
  (122 other events, 1134.7 us)
Sparse Core Ops, SparseCore 0:
  43.0 119.4 all-gather.1
  304.4 84.7 reduce-scatter.4
  402.9 97.0 reduce-scatter.6
  523.7 87.2 reduce-scatter.8
  616.8 86.0 reduce-scatter.10

commit v3 on v2

--- a/solution.py
+++ b/solution.py
@@ -797,11 +797,13 @@
     hidden,
     slab,
     gate_up_ref,
+    query_ref,
     gains_ref,
     seg_ref,
     rates_ref,
     own_ref,
     pieces_ref,
+    query_pad_ref,
     gains_all_ref,
     segs_ref,
     table_ref,
@@ -895,6 +897,12 @@
     tile_format(
         shifted(own_slab.at[0], me), shifted(own_slab.at[1], me), store_own, tiles, tail
     )
+    rest = jnp.zeros((query_ref.shape[0], LANES - HD - RD), jnp.float32)
+    for h in range(H):
+        head = query_ref[:, h * (HD + RD) : (h + 1) * (HD + RD)].astype(jnp.float32)
+        query_pad_ref[:, h * LANES : (h + 1) * LANES] = jnp.concatenate(
+            [head, rest], axis=1
+        ).astype(jnp.bfloat16)
     for copy in small:
         copy.wait()
     for j in range(group):
@@ -927,7 +935,7 @@
     )(gains, seg, rotation_rates())
 
 
-def hidden_pieces(gate_up, gains, seg, group, replicas):
+def hidden_pieces(gate_up, query_up, gains, seg, group, replicas):
     rows = gate_up.shape[0]
     share = rows // replicas
     hidden = FF // group
@@ -937,11 +945,12 @@
     others = group - 1
     return pl.pallas_call(
         functools.partial(columns_kernel, group, replicas, hidden, slab),
-        in_specs=[pl.BlockSpec(memory_space=pl.ANY)] + [pl.BlockSpec(memory_space=pltpu.VMEM)] * 3,
-        out_specs=[pl.BlockSpec(memory_space=pltpu.VMEM)] * 5,
+        in_specs=[pl.BlockSpec(memory_space=pl.ANY)] + [pl.BlockSpec(memory_space=pltpu.VMEM)] * 4,
+        out_specs=[pl.BlockSpec(memory_space=pltpu.VMEM)] * 6,
         out_shape=[
             jax.ShapeDtypeStruct((rows, whole), bf16),
             jax.ShapeDtypeStruct((share, others * whole), bf16),
+            jax.ShapeDtypeStruct((query_up.shape[0], H * LANES), bf16),
         ]
         + small_shapes(gains, seg, group),
         scratch_shapes=[
@@ -957,7 +966,7 @@
         ),
         cost_estimate=pl.CostEstimate(flops=0, bytes_accessed=100_000_000, transcendentals=0),
         name="hidden_pieces",
-    )(gate_up, gains, seg, rotation_rates())
+    )(gate_up, query_up, gains, seg, rotation_rates())
 
 
 def latent_kernel(
@@ -1264,10 +1273,6 @@
     fast = group == 4 and share % 16 == 0
     gains_rows = jnp.broadcast_to(norm_gains.astype(f32), (8,) + norm_gains.shape)
     seg_rows = jnp.broadcast_to(segments.astype(f32), (8, seq_len))
-    query_pad = jnp.pad(
-        query_up.reshape(-1, H, HD + RD), ((0, 0), (0, 0), (0, LANES - HD - RD))
-    ).reshape(-1, H * LANES)
-
     def hidden_columns(array, index):
         gate = columns(array, index, hidden_part)
         up = lax.dynamic_slice_in_dim(array, FF + index * hidden_part, hidden_part, 1)
@@ -1281,11 +1286,14 @@
     share = rows_d // replicas
     cot_near = near_blocks(cotangent, group)
     if share % 16 == 0:
-        own_columns, pieces, gains_all, segs, tables = hidden_pieces(
-            gate_up, gains_rows, seg_rows, group, replicas
+        own_columns, pieces, query_pad, gains_all, segs, tables = hidden_pieces(
+            gate_up, query_up, gains_rows, seg_rows, group, replicas
         )
     else:
         gains_all, segs, tables = small_things(gains_rows, seg_rows, group)
+        query_pad = jnp.pad(
+            query_up.reshape(-1, H, HD + RD), ((0, 0), (0, 0), (0, LANES - HD - RD))
+        ).reshape(-1, H * LANES)
         own_share = lax.dynamic_slice_in_dim(gate_up, rep * share, share, 0)
         own_columns = hidden_columns(gate_up, me)
         main = 2 * tiles * TILE
@@ -1407,7 +1415,8 @@
         return place(blocks, me).reshape((group,) + blocks[0].shape)
 
     summed = [lax.psum_scatter(grad_cuts[0], "rep", scatter_dimension=0, tiled=True)]
-    grad_normed_mlp, summed[0] = lax.optimization_barrier((grad_normed_mlp, summed[0]))
+    grad_down, summed[0] = lax.optimization_barrier((grad_down, summed[0]))
+    grad_normed_mlp, grad_down = lax.optimization_barrier((grad_normed_mlp, grad_down))
     for grad_cut in grad_cuts[1:]:
         grad_cut, _ = lax.optimization_barrier((grad_cut, summed[-1]))
         summed.append(lax.psum_scatter(grad_cut, "rep", scatter_dimension=0, tiled=True))
@@ -1415,7 +1424,6 @@
     grad_gain_mlp = jnp.sum(grad_normed_mlp * hidden * inv_hidden, axis=0)
     grad_hidden = grad_top + norm_back(grad_normed_mlp * gain_mlp, hidden, inv_hidden)
     grad_attn = (residual_scale * grad_hidden).astype(bf16)
-    grad_attn, grad_down = lax.optimization_barrier((grad_attn, grad_down))
 
     def back_block(j, grad):
         return attend_back(
@@ -1442,8 +1450,6 @@
     near, back, down_terms = lax.optimization_barrier((near, back, down_terms))
     attn_parts = all_blocks(grad_attn, near, group)
     back += [back_block(j, attn_parts[j]) for j in others]
-    down_terms, _ = lax.optimization_barrier((down_terms, attn_parts[1:]))
-    block_out = (hidden + residual_scale * scatter_sum(down_terms, group)).astype(bf16)
     owned = [to_owner_rows(rows) for rows in summed]
 
     def unpack(q, second):
@@ -1460,6 +1466,8 @@
     )
     latent_terms = [part[0] for part in back]
     grad_latent_low = scatter_sum(latent_terms, group)
+    grad_down, _ = lax.optimization_barrier((grad_down, (summed[-1], grad_latent_low)))
+    down_total = lax.psum_scatter(grad_down, "rep", scatter_dimension=0, tiled=True)
     grad_normed_query = grad_latent_low[:, :QR]
     grad_normed_keyval = grad_latent_low[:, QR : QR + KR]
     grad_key_rope = grad_latent_low[:, QR + KR + HD : QR + KR + HD + RD]
@@ -1474,9 +1482,6 @@
         axis=1,
     ).astype(bf16)
     grad_latent_parts = gather_blocks(grad_latent_rows, group)
-    block_out, grad_latent_parts = lax.optimization_barrier((block_out, grad_latent_parts))
-    grad_down, _ = lax.optimization_barrier((grad_down, (summed[-1], grad_latent_rows)))
-    down_total = lax.psum_scatter(grad_down, "rep", scatter_dimension=0, tiled=True)
     mixed_late, late_query, late_keyval, _ = lax.optimization_barrier(
         (
             [part[3] for part in attention],
@@ -1533,6 +1538,8 @@
     gains_row = gains_sum.reshape(replicas, 1, -1).astype(bf16)
     gains_row = jnp.pad(gains_row, ((0, 0), (0, 15), (0, unit - gains_row.shape[2])))
     last = jnp.concatenate([pair] + grad_out + grad_latent + [gains_row], axis=1)
+    last, down_terms = lax.optimization_barrier((last, down_terms))
+    block_out = (hidden + residual_scale * scatter_sum(down_terms, group)).astype(bf16)
     last, _ = lax.optimization_barrier((last.reshape(-1, unit), down_total))
     last = lax.psum_scatter(last, "rep", scatter_dimension=0, tiled=True)
     pair_own = to_owner_rows(last[:pair_rows])

time: 737 us -> 761 us (1.033)
  waiting for transfers between devices: 194 us -> 213 us
  other arithmetic: 55.8 us -> 46 us
  Pallas kernels: 321 us -> 329 us
  starting transfers between devices: 46.9 us -> 54.9 us
    reduce_scatter x1, waiting for transfers between devices: 39.2 us -> 0.01 us  [per_device(): last = lax.psum_scatter(last, 'rep', scatter_dimension=0, tiled=True)]
    reduce_scatter x1, waiting for transfers between devices: 0.01 us -> 24.6 us  [per_device(): lax.psum_scatter(grad_down, 'rep', scatter_dimension=0, tiled=True)]
    ppermute x47, waiting for transfers between devices: 155 us -> 173 us  [hop(): lax.ppermute(array, 'shard', [(i, i ^ distance) for i in range(group)])]
    reduce_scatter x1, waiting for transfers between devices: 0.01 us -> 15.2 us  [per_device(): lax.psum_scatter(grad_cuts[0], 'rep', scatter_dimension=0, tiled=True)]
    ppermute x47, starting transfers between devices: 46.7 us -> 54.7 us  [hop(): lax.ppermute(array, 'shard', [(i, i ^ distance) for i in range(group)])]
    pallas_call x1, Pallas kernels: 85.8 us -> 93.6 us  [latent_front(): pl.pallas_call(functools.partial(latent_kernel, group), in_specs=[pl.Bloc...]
    unnamed x214 -> x240, local copies, waits for them, and re-layouts: 27.5 us -> 30.6 us
  transfers between devices with their start and end apart: 52 -> 52, of which waited for: 25 -> 24; matrix products, arithmetic and copies ran while one was open for 17% -> 15% of each run, Pallas kernels for 33% -> 33%
where the time goes in v3:
time: 761 us; the launch traced here: 753 us
  Pallas kernels  329 us (43%)
  waiting for transfers between devices  213 us (28%)
  local copies, waits for them, and re-layouts  70.6 us (9%)
  starting transfers between devices  54.9 us (7%)
  other arithmetic  46 us (6%)
  matrix products  23.4 us (3%)
  between operations  16.1 us (2%)
    ppermute x47, waiting for transfers between devices, hop(): lax.ppermute(array, 'shard', [(i, i ^ distance) for i in range(group)])  173 us
    pallas_call x2, Pallas kernels, layer_part(): pl.pallas_call(functools.partial(layer_kernel, group, tiles_from, tiles,...  99.3 us
    pallas_call x1, Pallas kernels, latent_front(): pl.pallas_call(functools.partial(latent_kernel, group), in_specs=[pl.Bloc...  93.6 us
    ppermute x47, starting transfers between devices, hop(): lax.ppermute(array, 'shard', [(i, i ^ distance) for i in range(group)])  54.7 us
    pallas_call x4, Pallas kernels, attend_back(): pl.pallas_call(functools.partial(attend_back_kernel, heads), grid=(1,), o...  42.4 us
    pallas_call x4, Pallas kernels, attend(): pl.pallas_call(functools.partial(attend_kernel, heads), grid=(1,), out_sp...  34.8 us
    pallas_call x1, Pallas kernels, hidden_pieces(): pl.pallas_call(functools.partial(columns_kernel, group, replicas, hidden,...  33.1 us
    unnamed x240, local copies, waits for them, and re-layouts  30.6 us
  transfers between devices with their start and end apart: 52, of which 24 were waited for; matrix products, arithmetic and copies ran while one was open for 15% of the time, Pallas kernels for 33%

profile of v3, /device:TPU:0, one launch (start us, length us, event | category | flops | bytes accessed | tf_op | source)
XLA Modules:
  0.0 753.1 jit_solution(10325193895071434601)
XLA Ops:
  10.6 33.1 %hidden_pieces.1 = (bf16[640,3328]{1,0:T(8,128)(2,1)}, bf16[80,9984]{1,0:T(8,128)(2,1)S(1)}, bf16[192,5120]{1,0:T(8,128)(2,1)}, f32[32,1536]{1,0:T(8,128)S(1)}, ...) custom-call(bf16[640,12800]{1,0:T(8,128)(2,1)} %gate_up_ref.1, bf16[192,3840]{1,0:T(8,128)(2,1)S(1)} %copy-done.15, ...), custom_call_target="tpu_custom_call" | custom-call | bytes 100000000 | tf_op jit(solution)/shard_map/hidden_pieces/pallas_call | solution.py:946
  53.0 93.6 %latent_front.1 = (bf16[4,256,1152]{2,1,0:T(8,128)(2,1)}, f32[256,1056]{1,0:T(8,128)S(1)}, bf16[256,2560]{1,0:T(8,128)(2,1)S(1)}, bf16[2560,1056]{1,0:T(8,128)(2...) custom-call(bf16[256,2560]{1,0:T(8,128)(2,1)S(1)} %copy-done.2, f32[1,2560]{1,0:T(1,128)S(1)} %reshape.166.gains_ref, ...), custom_call_target="tpu_custom_call" | custom-call | flops 1384120320 | bytes 60000000 | tf_op jit(solution)/shard_map/latent_front/pallas_call | solution.py:1143
  151.7 8.6 %attend.4 = (bf16[256,2560]{1,0:T(8,128)(2,1)S(1)}, bf16[256,1280]{1,0:T(8,128)(2,1)S(1)}, bf16[256,1280]{1,0:T(8,128)(2,1)S(1)}, bf16[256,640]{1,0:T(8,128)(2,1)S(1)}) custom-call(bf16[4,256,1152]{2,1,0:T(8,128)(2,1)} %get-tuple-element.134.latent_ref.refs_0_.refs_1_.refs_2_.refs_3_, f32[4,3,256,128]{3,2,1,0:T(8,128)S(1)} %get-tuple-element.117.table_ref, ...), custom_call_target="tpu_custom_call" | custom-call | flops 1845493760 | bytes 7208960 | tf_op jit(solution)/shard_map/attend/pallas_call | solution.py:557
  169.4 8.8 %attend.5 = (bf16[256,2560]{1,0:T(8,128)(2,1)S(1)}, bf16[256,1280]{1,0:T(8,128)(2,1)S(1)}, bf16[256,1280]{1,0:T(8,128)(2,1)S(1)}, bf16[256,640]{1,0:T(8,128)(2,1)S(1)}) custom-call(bf16[4,256,1152]{2,1,0:T(8,128)(2,1)} %get-tuple-element.134.latent_ref.refs_0_.refs_1_.refs_2_.refs_3_, f32[4,3,256,128]{3,2,1,0:T(8,128)S(1)} %get-tuple-element.117.table_ref, ...), custom_call_target="tpu_custom_call" | custom-call | flops 1845493760 | bytes 7208960 | tf_op jit(solution)/shard_map/attend/pallas_call | solution.py:557
  180.5 8.6 %attend.6 = (bf16[256,2560]{1,0:T(8,128)(2,1)S(1)}, bf16[256,1280]{1,0:T(8,128)(2,1)S(1)}, bf16[256,1280]{1,0:T(8,128)(2,1)S(1)}, bf16[256,640]{1,0:T(8,128)(2,1)S(1)}) custom-call(bf16[4,256,1152]{2,1,0:T(8,128)(2,1)} %get-tuple-element.134.latent_ref.refs_0_.refs_1_.refs_2_.refs_3_, f32[4,3,256,128]{3,2,1,0:T(8,128)S(1)} %get-tuple-element.117.table_ref, ...), custom_call_target="tpu_custom_call" | custom-call | flops 1845493760 | bytes 7208960 | tf_op jit(solution)/shard_map/attend/pallas_call | solution.py:557
  190.5 8.7 %attend.7 = (bf16[256,2560]{1,0:T(8,128)(2,1)S(1)}, bf16[256,1280]{1,0:T(8,128)(2,1)S(1)}, bf16[256,1280]{1,0:T(8,128)(2,1)S(1)}, bf16[256,640]{1,0:T(8,128)(2,1)S(1)}) custom-call(bf16[4,256,1152]{2,1,0:T(8,128)(2,1)} %get-tuple-element.134.latent_ref.refs_0_.refs_1_.refs_2_.refs_3_, f32[4,3,256,128]{3,2,1,0:T(8,128)S(1)} %get-tuple-element.117.table_ref, ...), custom_call_target="tpu_custom_call" | custom-call | flops 1845493760 | bytes 7208960 | tf_op jit(solution)/shard_map/attend/pallas_call | solution.py:557
  199.2 7.3 collective-permute-done.7
  206.5 10.6 %collective-permute-done.5 = bf16[256,2560]{1,0:T(8,128)(2,1)S(1)} collective-permute-done((bf16[256,2560]{1,0:T(8,128)(2,1)S(1)}, bf16[256,2560]{1,0:T(8,128)(2,1)S(1)}, u32[]{:S(2)}, u32[]{:S(2)}) %collective-permute-start.5) | collective-permute-done | bytes 1310752 | tf_op jit(solution)/shard_map/ppermute | solution.py:1174
  220.3 24.8 %collective-permute-done.8.refs_1_ = bf16[256,2560]{1,0:T(8,128)(2,1)S(1)} collective-permute-done((bf16[256,2560]{1,0:T(8,128)(2,1)S(1)}, bf16[256,2560]{1,0:T(8,128)(2,1)S(1)}, u32[]{:S(2)}, u32[]{:S(2)}) %collective-permute-start.8) | collective-permute-done | bytes 1310752 | tf_op jit(solution)/shard_map/ppermute | solution.py:1174
  249.2 8.3 %collective-permute-done.10 = bf16[128,2560]{1,0:T(8,128)(2,1)} collective-permute-done((bf16[128,2560]{1,0:T(8,128)(2,1)}, bf16[128,2560]{1,0:T(8,128)(2,1)}, u32[]{:S(2)}, u32[]{:S(2)}) %collective-permute-start.10) | collective-permute-done | bytes 655392 | tf_op jit(solution)/shard_map/ppermute | solution.py:1174
  261.4 44.7 %layer_part.2 = (bf16[1024,1664]{1,0:T(8,128)(2,1)}, bf16[8,4,80,1536]{3,2,1,0:T(8,128)(2,1)}, f32[1024,2560]{1,0:T(8,128)}) custom-call(s32[4]{0:T(128)} %pad_add_fusion.order_ref, bf16[256,2560]{1,0:T(8,128)(2,1)} %copy-done.65, bf16[256,2560]{1,0:T(8,128)(2,1)} %copy-done.74, bf16[256,2560]{1,0:T(8,128)(2,1)} %copy-done.75, ...), custom_call_target="tpu_custom_call" | custom-call | flops 28185722880 | bytes 65536000 | tf_op jit(solution)/shard_map/layer_part/pallas_call | solution.py:415
  306.3 54.5 %layer_part.3 = (bf16[1024,1664]{1,0:T(8,128)(2,1)}, bf16[8,4,80,1792]{3,2,1,0:T(8,128)(2,1)}, bf16[1024,2560]{1,0:T(8,128)(2,1)}) custom-call(s32[4]{0:T(128)} %pad_add_fusion.order_ref, bf16[256,2560]{1,0:T(8,128)(2,1)} %copy-done.65, bf16[256,2560]{1,0:T(8,128)(2,1)} %copy-done.74, ...), custom_call_target="tpu_custom_call", output_to_operand_aliasing={{0}: (19, {})} | custom-call | flops 30534533120 | bytes 67502080 | tf_op jit(solution)/shard_map/layer_part/pallas_call | solution.py:415
  360.8 15.0 %down_grad.1 = bf16[1600,2560]{1,0:T(8,128)(2,1)} custom-call(bf16[1024,1664]{1,0:T(8,128)(2,1)} %get-tuple-element.157.act_ref, bf16[256,2560]{1,0:T(8,128)(2,1)} %refs_0_, bf16[256,2560]{1,0:T(8,128)(2,1)} %collective-permute-done.refs_5_.refs_1_, bf16[256,2560]{1,0:T(8,128)(2,1)} %collective-permute-done.1.refs_6_.refs_2_, bf16[256,2560]{1,0:T(8,128)(2,1)S(1)} %copy-done.7), custom_call_target="tpu_custom_call" | custom-call | flops 8388608000 | bytes 16711680 | tf_op jit(solution)/shard_map/down_grad/pallas_call | solution.py:456
  375.8 15.2 %reduce-scatter.5.cloned.1.call-done = bf16[320,1536]{1,0:T(8,128)(2,1)} async-done(((bf16[2560,1536]{1,0:T(8,128)(2,1)}), bf16[320,1536]{1,0:T(8,128)(2,1)}) %reduce-scatter.5.cloned.1.call-update) | async-done | bytes 983056 | tf_op jit(solution)/shard_map/reduce_scatter | solution.py:1417
  396.1 11.4 %collective-permute-done.12 = bf16[128,2560]{1,0:T(8,128)(2,1)S(1)} collective-permute-done((bf16[128,2560]{1,0:T(8,128)(2,1)S(1)}, bf16[128,2560]{1,0:T(8,128)(2,1)S(1)}, u32[]{:S(2)}, u32[]{:S(2)}) %collective-permute-start.12) | collective-permute-done | bytes 655392 | tf_op jit(solution)/shard_map/ppermute | solution.py:1174
  411.3 25.1 %collective-permute-done.15 = bf16[256,2560]{1,0:T(8,128)(2,1)S(1)} collective-permute-done((bf16[256,2560]{1,0:T(8,128)(2,1)S(1)}, bf16[256,2560]{1,0:T(8,128)(2,1)S(1)}, u32[]{:S(2)}, u32[]{:S(2)}) %collective-permute-start.15) | collective-permute-done | bytes 1310752 | tf_op jit(solution)/shard_map/ppermute | solution.py:1174
  445.1 11.3 %convolution_convert_fusion = bf16[1024,2560]{1,0:T(8,128)(2,1)} fusion(bf16[1600,2560]{1,0:T(8,128)(2,1)S(1)} %bitcast.149, bf16[1024,1664]{1,0:T(8,128)(2,1)S(1)} %copy-done.72), kind=kOutput, calls=%fused_computation.1 | convolution fusion | flops 8391229440 | bytes 16842752 | tf_op jit(solution)/shard_map/dot_general | solution.py:1446
  456.4 10.4 %attend_back.4 = (bf16[256,1152]{1,0:T(8,128)(2,1)S(1)}, bf16[256,1280]{1,0:T(8,128)(2,1)S(1)}, bf16[256,1280]{1,0:T(8,128)(2,1)S(1)}) custom-call(bf16[256,2560]{1,0:T(8,128)(2,1)S(1)} %multiply_convert_fusion.grad_ref.refs_4_, bf16[256,1280]{1,0:T(8,128)(2,1)S(1)} %copy-done.35, bf16[256,1280]{1,0:T(8,128)(2,1)S(1)} %copy-done.37, ...), custom_call_target="tpu_custom_call" | custom-call | flops 2348810240 | bytes 7208960 | tf_op jit(solution)/shard_map/attend_back/pallas_call | solution.py:642
  474.6 9.0 %collective-permute-done.18 = bf16[128,2560]{1,0:T(8,128)(2,1)S(1)} collective-permute-done((bf16[128,2560]{1,0:T(8,128)(2,1)S(1)}, bf16[128,2560]{1,0:T(8,128)(2,1)S(1)}, u32[]{:S(2)}, u32[]{:S(2)}) %collective-permute-start.18) | collective-permute-done | bytes 655392 | tf_op jit(solution)/shard_map/ppermute | solution.py:1174
  484.7 10.9 %attend_back.7 = (bf16[256,1152]{1,0:T(8,128)(2,1)S(1)}, bf16[256,1280]{1,0:T(8,128)(2,1)S(1)}, bf16[256,1280]{1,0:T(8,128)(2,1)S(1)}) custom-call(bf16[256,2560]{1,0:T(8,128)(2,1)S(1)} %constant_dynamic-update-slice_fusion.2.grad_ref.refs_7_, bf16[256,1280]{1,0:T(8,128)(2,1)S(1)} %get-tuple-element.167.query_ref, bf16[256,1280]{1,0:T(8,128)(2,1)S(1)} %copy-done.21, ...), custom_call_target="tpu_custom_call" | custom-call | flops 2348810240 | bytes 7208960 | tf_op jit(solution)/shard_map/attend_back/pallas_call | solution.py:642
  497.4 10.3 %attend_back.6 = (bf16[256,1152]{1,0:T(8,128)(2,1)S(1)}, bf16[256,1280]{1,0:T(8,128)(2,1)S(1)}, bf16[256,1280]{1,0:T(8,128)(2,1)S(1)}) custom-call(bf16[256,2560]{1,0:T(8,128)(2,1)S(1)} %collective-permute-done.17.grad_ref.refs_6_, bf16[256,1280]{1,0:T(8,128)(2,1)S(1)} %copy-done.23, bf16[256,1280]{1,0:T(8,128)(2,1)S(1)} %copy-done.25, ...), custom_call_target="tpu_custom_call" | custom-call | flops 2348810240 | bytes 7208960 | tf_op jit(solution)/shard_map/attend_back/pallas_call | solution.py:642
  508.6 10.8 %attend_back.5 = (bf16[256,1152]{1,0:T(8,128)(2,1)S(1)}, bf16[256,1280]{1,0:T(8,128)(2,1)S(1)}, bf16[256,1280]{1,0:T(8,128)(2,1)S(1)}) custom-call(bf16[256,2560]{1,0:T(8,128)(2,1)S(1)} %collective-permute-done.16.grad_ref.refs_5_, bf16[256,1280]{1,0:T(8,128)(2,1)S(1)} %copy-done.27, bf16[256,1280]{1,0:T(8,128)(2,1)S(1)} %copy-done.29, ...), custom_call_target="tpu_custom_call" | custom-call | flops 2348810240 | bytes 7208960 | tf_op jit(solution)/shard_map/attend_back/pallas_call | solution.py:642
  521.7 6.3 collective-permute-done.20
  561.1 7.0 fusion.13
  571.7 6.6 out_grad.1
  600.8 5.2 convolution_convert_fusion.1
  610.7 24.6 %reduce-scatter.9.cloned.1.call-done = bf16[200,2560]{1,0:T(8,128)(2,1)} async-done(((bf16[1600,2560]{1,0:T(8,128)(2,1)}), bf16[200,2560]{1,0:T(8,128)(2,1)}) %reduce-scatter.9.cloned.1.call-update) | async-done | bytes 1024016 | tf_op jit(solution)/shard_map/reduce_scatter | solution.py:1470
  647.5 8.2 %collective-permute-done.36 = bf16[128,2560]{1,0:T(8,128)(2,1)} collective-permute-done((bf16[128,2560]{1,0:T(8,128)(2,1)}, bf16[128,2560]{1,0:T(8,128)(2,1)}, u32[]{:S(2)}, u32[]{:S(2)}) %collective-permute-start.36) | collective-permute-done | bytes 655392 | tf_op jit(solution)/shard_map/ppermute | solution.py:1174
  658.5 12.5 %collective-permute-done.34 = bf16[128,2560]{1,0:T(8,128)(2,1)S(1)} collective-permute-done((bf16[128,2560]{1,0:T(8,128)(2,1)S(1)}, bf16[128,2560]{1,0:T(8,128)(2,1)S(1)}, u32[]{:S(2)}, u32[]{:S(2)}) %collective-permute-start.34) | collective-permute-done | bytes 655392 | tf_op jit(solution)/shard_map/ppermute | solution.py:1174
  676.1 22.2 %collective-permute-done.37 = bf16[256,2560]{1,0:T(8,128)(2,1)S(1)} collective-permute-done((bf16[256,2560]{1,0:T(8,128)(2,1)S(1)}, bf16[256,2560]{1,0:T(8,128)(2,1)S(1)}, u32[]{:S(2)}, u32[]{:S(2)}) %collective-permute-start.37) | collective-permute-done | bytes 1310752 | tf_op jit(solution)/shard_map/ppermute | solution.py:1174
  715.6 7.7 %convert_subtract_fusion = (f32[80,12800]{1,0:T(8,128)}, f32[80,12800]{1,0:T(8,128)}, f32[80,12800]{1,0:T(8,128)}) fusion(bf16[640,12800]{1,0:T(8,128)(2,1)} %gate_up_ref.1, s32[]{:T(128)S(6)} %select_n.89, bf16[80,12800]{1,0:T(8,128)(2,1)S(1)} %concatenate.76, bf16[80,12800]{1,0:T(8,128)(2,1)} %param.39, bf16[80,12800]{1,0:T(8,128)(2,1)} %param.46), kind=kLoop, calls=%fused_computation.8 | loop fusion | flops 19456000 | bytes 20480004 | tf_op jit(solution)/shard_map/sub | solution.py:64
  723.3 5.2 convert_subtract_fusion.1
  (459 shorter events, 190.4 us)
Async XLA Ops:
  7.2 254.2 %all-gather.2.cloned.1.call-start = ((), (), s32[]{:S(2)}) async-start(), calls=%async_computation.4 | async-start | bytes 14376960 | tf_op jit(solution)/shard_map/all_gather | solution.py:1304
  44.9 346.1 %reduce-scatter.5.cloned.1.call-start = ((), (), s32[]{:S(2)}) async-start(), calls=%async_computation.5 | async-start | bytes 8847360 | tf_op jit(solution)/shard_map/reduce_scatter | solution.py:1417
  44.9 102.7 %collective-permute-start = (bf16[256,2560]{1,0:T(8,128)(2,1)}, bf16[256,2560]{1,0:T(8,128)(2,1)}, u32[]{:S(2)}, u32[]{:S(2)}) collective-permute-start(bf16[256,2560]{1,0:T(8,128)(2,1)} %refs_0_), channel_id=1, source_target_pairs={{0,8},{8,0},{16,24},{24,16},{1,9},{9,1},{17,25},{25,17},{2,10},{10... | collective-permute-start | bytes 3932168 | tf_op jit(solution)/shard_map/ppermute | solution.py:1174
  46.5 101.2 %collective-permute-start.1 = (bf16[256,2560]{1,0:T(8,128)(2,1)}, bf16[256,2560]{1,0:T(8,128)(2,1)}, u32[]{:S(2)}, u32[]{:S(2)}) collective-permute-start(bf16[256,2560]{1,0:T(8,128)(2,1)} %refs_0_), channel_id=1, source_target_pairs={{0,16},{8,24},{16,0},{24,8},{1,17},{9,25},{17,1},{25,9},{2,18},{10... | collective-permute-start | bytes 3932168 | tf_op jit(solution)/shard_map/ppermute | solution.py:1174
  150.4 17.7 %collective-permute-start.2 = (bf16[128,2560]{1,0:T(8,128)(2,1)S(1)}, bf16[128,2560]{1,0:T(8,128)(2,1)S(1)}, u32[]{:S(2)}, u32[]{:S(2)}) collective-permute-start(bf16[128,2560]{1,0:T(8,128)(2,1)S(1)} %slice.364), channel_id=1, source_target_pairs={{0,16},{8,24},{16,0},{24,8},{1,17},{9,25},{17,1},{25,9},{2,18},{10... | collective-permute-start | bytes 1966088 | tf_op jit(solution)/shard_map/ppermute | solution.py:1174
  160.5 17.7 %collective-permute-start.6 = (bf16[128,2560]{1,0:T(8,128)(2,1)S(1)}, bf16[128,2560]{1,0:T(8,128)(2,1)S(1)}, u32[]{:S(2)}, u32[]{:S(2)}) collective-permute-start(bf16[128,2560]{1,0:T(8,128)(2,1)S(1)} %get-tuple-element.260), channel_id=1, source_target_pairs={{0,8},{8,0},{16,24},{24,16},{1,9},{9,1},{17,25},{25,17},{2,10},{10... | collective-permute-start | bytes 1966088 | tf_op jit(solution)/shard_map/ppermute | solution.py:1174
  161.4 27.8 %collective-permute-start.4 = (bf16[128,2560]{1,0:T(8,128)(2,1)S(1)}, bf16[128,2560]{1,0:T(8,128)(2,1)S(1)}, u32[]{:S(2)}, u32[]{:S(2)}) collective-permute-start(bf16[128,2560]{1,0:T(8,128)(2,1)S(1)} %get-tuple-element.259), channel_id=1, source_target_pairs={{0,16},{8,24},{16,0},{24,8},{1,17},{9,25},{17,1},{25,9},{2,18},{10... | collective-permute-start | bytes 1966088 | tf_op jit(solution)/shard_map/ppermute | solution.py:1174
  179.3 27.2 %collective-permute-start.7 = (bf16[256,2560]{1,0:T(8,128)(2,1)S(1)}, bf16[256,2560]{1,0:T(8,128)(2,1)S(1)}, u32[]{:S(2)}, u32[]{:S(2)}) collective-permute-start(bf16[256,2560]{1,0:T(8,128)(2,1)S(1)} %pad_maximum_fusion.3), channel_id=1, source_target_pairs={{0,16},{8,24},{16,0},{24,8},{1,17},{9,25},{17,1},{25,9},{2,18},{10... | collective-permute-start | bytes 3932168 | tf_op jit(solution)/shard_map/ppermute | solution.py:1174
  190.3 26.8 %collective-permute-start.5 = (bf16[256,2560]{1,0:T(8,128)(2,1)S(1)}, bf16[256,2560]{1,0:T(8,128)(2,1)S(1)}, u32[]{:S(2)}, u32[]{:S(2)}) collective-permute-start(bf16[256,2560]{1,0:T(8,128)(2,1)S(1)} %pad_maximum_fusion.2), channel_id=1, source_target_pairs={{0,8},{8,0},{16,24},{24,16},{1,9},{9,1},{17,25},{25,17},{2,10},{10... | collective-permute-start | bytes 3932168 | tf_op jit(solution)/shard_map/ppermute | solution.py:1174
  219.2 25.9 %collective-permute-start.8 = (bf16[256,2560]{1,0:T(8,128)(2,1)S(1)}, bf16[256,2560]{1,0:T(8,128)(2,1)S(1)}, u32[]{:S(2)}, u32[]{:S(2)}) collective-permute-start(bf16[256,2560]{1,0:T(8,128)(2,1)S(1)} %multiply_convert_fusion.1.refs_0_), channel_id=1, source_target_pairs={{0,8},{8,0},{16,24},{24,16},{1,9},{9,1},{17,25},{25,17},{2,10},{10... | collective-permute-start | bytes 3932168 | tf_op jit(solution)/shard_map/ppermute | solution.py:1174
  219.4 27.4 %collective-permute-start.9 = (bf16[256,2560]{1,0:T(8,128)(2,1)S(1)}, bf16[256,2560]{1,0:T(8,128)(2,1)S(1)}, u32[]{:S(2)}, u32[]{:S(2)}) collective-permute-start(bf16[256,2560]{1,0:T(8,128)(2,1)S(1)} %multiply_convert_fusion.1.refs_0_), channel_id=1, source_target_pairs={{0,16},{8,24},{16,0},{24,8},{1,17},{9,25},{17,1},{25,9},{2,18},{10... | collective-permute-start | bytes 3932168 | tf_op jit(solution)/shard_map/ppermute | solution.py:1174
  306.2 233.2 %reduce-scatter.7.cloned.1.call-start = ((), (), s32[]{:S(2)}) async-start(), calls=%async_computation.6 | async-start | bytes 10321920 | tf_op jit(solution)/shard_map/reduce_scatter | solution.py:1422
  391.0 244.2 %reduce-scatter.9.cloned.1.call-start = ((), (), s32[]{:S(2)}) async-start(), calls=%async_computation.7 | async-start | bytes 9216000 | tf_op jit(solution)/shard_map/reduce_scatter | solution.py:1470
  409.1 27.3 %collective-permute-start.15 = (bf16[256,2560]{1,0:T(8,128)(2,1)S(1)}, bf16[256,2560]{1,0:T(8,128)(2,1)S(1)}, u32[]{:S(2)}, u32[]{:S(2)}) collective-permute-start(bf16[256,2560]{1,0:T(8,128)(2,1)S(1)} %pad_maximum_fusion.5), channel_id=1, source_target_pairs={{0,16},{8,24},{16,0},{24,8},{1,17},{9,25},{17,1},{25,9},{2,18},{10... | collective-permute-start | bytes 3932168 | tf_op jit(solution)/shard_map/ppermute | solution.py:1174
  409.8 27.1 %collective-permute-start.13 = (bf16[256,2560]{1,0:T(8,128)(2,1)S(1)}, bf16[256,2560]{1,0:T(8,128)(2,1)S(1)}, u32[]{:S(2)}, u32[]{:S(2)}) collective-permute-start(bf16[256,2560]{1,0:T(8,128)(2,1)S(1)} %pad_maximum_fusion.4), channel_id=1, source_target_pairs={{0,8},{8,0},{16,24},{24,16},{1,9},{9,1},{17,25},{25,17},{2,10},{10... | collective-permute-start | bytes 3932168 | tf_op jit(solution)/shard_map/ppermute | solution.py:1174
  442.1 27.5 %collective-permute-start.16 = (bf16[256,2560]{1,0:T(8,128)(2,1)S(1)}, bf16[256,2560]{1,0:T(8,128)(2,1)S(1)}, u32[]{:S(2)}, u32[]{:S(2)}) collective-permute-start(bf16[256,2560]{1,0:T(8,128)(2,1)S(1)} %multiply_convert_fusion.grad_ref.refs_4_), channel_id=1, source_target_pairs={{0,8},{8,0},{16,24},{24,16},{1,9},{9,1},{17,25},{25,17},{2,10},{10... | collective-permute-start | bytes 3932168 | tf_op jit(solution)/shard_map/ppermute | solution.py:1174
  443.7 28.1 %collective-permute-start.17 = (bf16[256,2560]{1,0:T(8,128)(2,1)S(1)}, bf16[256,2560]{1,0:T(8,128)(2,1)S(1)}, u32[]{:S(2)}, u32[]{:S(2)}) collective-permute-start(bf16[256,2560]{1,0:T(8,128)(2,1)S(1)} %multiply_convert_fusion.grad_ref.refs_4_), channel_id=1, source_target_pairs={{0,16},{8,24},{16,0},{24,8},{1,17},{9,25},{17,1},{25,9},{2,18},{10... | collective-permute-start | bytes 3932168 | tf_op jit(solution)/shard_map/ppermute | solution.py:1174
  496.6 23.5 %collective-permute-start.22 = (bf16[128,1152]{1,0:T(8,128)(2,1)S(1)}, bf16[128,1152]{1,0:T(8,128)(2,1)S(1)}, u32[]{:S(2)}, u32[]{:S(2)}) collective-permute-start(bf16[128,1152]{1,0:T(8,128)(2,1)S(1)} %get-tuple-element.330), channel_id=1, source_target_pairs={{0,8},{8,0},{16,24},{24,16},{1,9},{9,1},{17,25},{25,17},{2,10},{10... | collective-permute-start | bytes 884744 | tf_op jit(solution)/shard_map/ppermute | solution.py:1174
  539.4 189.2 %reduce-scatter.11.cloned.1.call-start = ((), (), s32[]{:S(2)}) async-start(), calls=%async_computation.8 | async-start | bytes 8847360 | tf_op jit(solution)/shard_map/reduce_scatter | solution.py:1544
  548.6 39.0 %collective-permute-start.27 = (bf16[256,1056]{0,1:T(8,128)(2,1)}, bf16[256,1056]{0,1:T(8,128)(2,1)}, u32[]{:S(2)}, u32[]{:S(2)}) collective-permute-start(bf16[256,1056]{0,1:T(8,128)(2,1)} %copy.63), channel_id=1, source_target_pairs={{0,8},{8,0},{16,24},{24,16},{1,9},{9,1},{17,25},{25,17},{2,10},{10... | collective-permute-start | bytes 1622024 | tf_op jit(solution)/shard_map/ppermute | solution.py:1174
  549.6 42.2 %collective-permute-start.28 = (bf16[256,1056]{0,1:T(8,128)(2,1)}, bf16[256,1056]{0,1:T(8,128)(2,1)}, u32[]{:S(2)}, u32[]{:S(2)}) collective-permute-start(bf16[256,1056]{0,1:T(8,128)(2,1)} %copy.63), channel_id=1, source_target_pairs={{0,16},{8,24},{16,0},{24,8},{1,17},{9,25},{17,1},{25,9},{2,18},{10... | collective-permute-start | bytes 1622024 | tf_op jit(solution)/shard_map/ppermute | solution.py:1174
  568.2 15.7 %collective-permute-start.33 = (bf16[1536]{0:T(1024)(128)(2,1)S(1)}, bf16[1536]{0:T(1024)(128)(2,1)S(1)}, u32[]{:S(2)}, u32[]{:S(2)}) collective-permute-start(bf16[1536]{0:T(1024)(128)(2,1)S(1)} %get-tuple-element.336), channel_id=1, source_target_pairs={{0,24},{8,16},{16,8},{24,0},{1,25},{9,17},{17,9},{25,1},{2,26},{10... | collective-permute-start | bytes 9224 | tf_op jit(solution)/shard_map/ppermute | solution.py:1174
  583.9 16.9 %collective-permute-start.26 = (bf16[256,640]{1,0:T(8,128)(2,1)S(1)}, bf16[256,640]{1,0:T(8,128)(2,1)}, u32[]{:S(2)}, u32[]{:S(2)}) collective-permute-start(bf16[256,640]{1,0:T(8,128)(2,1)S(1)} %copy-done.91), channel_id=1, source_target_pairs={{0,24},{8,16},{16,8},{24,0},{1,25},{9,17},{17,9},{25,1},{2,26},{10... | collective-permute-start | bytes 983048 | tf_op jit(solution)/shard_map/ppermute | solution.py:1174
  637.7 18.0 %collective-permute-start.36 = (bf16[128,2560]{1,0:T(8,128)(2,1)}, bf16[128,2560]{1,0:T(8,128)(2,1)}, u32[]{:S(2)}, u32[]{:S(2)}) collective-permute-start(bf16[128,2560]{1,0:T(8,128)(2,1)} %get-tuple-element.253), channel_id=1, source_target_pairs={{0,8},{8,0},{16,24},{24,16},{1,9},{9,1},{17,25},{25,17},{2,10},{10... | collective-permute-start | bytes 1966088 | tf_op jit(solution)/shard_map/ppermute | solution.py:1174
  642.6 30.6 %collective-permute-start.41 = (bf16[80,1536]{1,0:T(8,128)(2,1)S(1)}, bf16[80,1536]{1,0:T(8,128)(2,1)S(1)}, u32[]{:S(2)}, u32[]{:S(2)}) collective-permute-start(bf16[80,1536]{1,0:T(8,128)(2,1)S(1)} %get-tuple-element.323), channel_id=1, source_target_pairs={{0,8},{8,0},{16,24},{24,16},{1,9},{9,1},{17,25},{25,17},{2,10},{10... | collective-permute-start | bytes 737288 | tf_op jit(solution)/shard_map/ppermute | solution.py:1174
  642.8 30.5 %collective-permute-start.42 = (bf16[80,1536]{1,0:T(8,128)(2,1)S(1)}, bf16[80,1536]{1,0:T(8,128)(2,1)S(1)}, u32[]{:S(2)}, u32[]{:S(2)}) collective-permute-start(bf16[80,1536]{1,0:T(8,128)(2,1)S(1)} %get-tuple-element.322), channel_id=1, source_target_pairs={{0,16},{8,24},{16,0},{24,8},{1,17},{9,25},{17,1},{25,9},{2,18},{10... | collective-permute-start | bytes 737288 | tf_op jit(solution)/shard_map/ppermute | solution.py:1174
  644.3 29.0 %collective-permute-start.43 = (bf16[80,1536]{1,0:T(8,128)(2,1)S(1)}, bf16[80,1536]{1,0:T(8,128)(2,1)S(1)}, u32[]{:S(2)}, u32[]{:S(2)}) collective-permute-start(bf16[80,1536]{1,0:T(8,128)(2,1)S(1)} %get-tuple-element.321), channel_id=1, source_target_pairs={{0,24},{8,16},{16,8},{24,0},{1,25},{9,17},{17,9},{25,1},{2,26},{10... | collective-permute-start | bytes 737288 | tf_op jit(solution)/shard_map/ppermute | solution.py:1174
  646.2 24.8 %collective-permute-start.34 = (bf16[128,2560]{1,0:T(8,128)(2,1)S(1)}, bf16[128,2560]{1,0:T(8,128)(2,1)S(1)}, u32[]{:S(2)}, u32[]{:S(2)}) collective-permute-start(bf16[128,2560]{1,0:T(8,128)(2,1)S(1)} %copy-done.83), channel_id=1, source_target_pairs={{0,16},{8,24},{16,0},{24,8},{1,17},{9,25},{17,1},{25,9},{2,18},{10... | collective-permute-start | bytes 1966088 | tf_op jit(solution)/shard_map/ppermute | solution.py:1174
  657.0 41.3 %collective-permute-start.37 = (bf16[256,2560]{1,0:T(8,128)(2,1)S(1)}, bf16[256,2560]{1,0:T(8,128)(2,1)S(1)}, u32[]{:S(2)}, u32[]{:S(2)}) collective-permute-start(bf16[256,2560]{1,0:T(8,128)(2,1)S(1)} %pad_maximum_fusion.7), channel_id=1, source_target_pairs={{0,16},{8,24},{16,0},{24,8},{1,17},{9,25},{17,1},{25,9},{2,18},{10... | collective-permute-start | bytes 3932168 | tf_op jit(solution)/shard_map/ppermute | solution.py:1174
  671.3 27.0 %collective-permute-start.35 = (bf16[256,2560]{1,0:T(8,128)(2,1)S(1)}, bf16[256,2560]{1,0:T(8,128)(2,1)S(1)}, u32[]{:S(2)}, u32[]{:S(2)}) collective-permute-start(bf16[256,2560]{1,0:T(8,128)(2,1)S(1)} %pad_maximum_fusion.6), channel_id=1, source_target_pairs={{0,8},{8,0},{16,24},{24,16},{1,9},{9,1},{17,25},{25,17},{2,10},{10... | collective-permute-start | bytes 3932168 | tf_op jit(solution)/shard_map/ppermute | solution.py:1174
  674.4 31.0 %collective-permute-start.44 = (bf16[80,1792]{1,0:T(8,128)(2,1)S(1)}, bf16[80,1792]{1,0:T(8,128)(2,1)S(1)}, u32[]{:S(2)}, u32[]{:S(2)}) collective-permute-start(bf16[80,1792]{1,0:T(8,128)(2,1)S(1)} %get-tuple-element.295), channel_id=1, source_target_pairs={{0,8},{8,0},{16,24},{24,16},{1,9},{9,1},{17,25},{25,17},{2,10},{10... | collective-permute-start | bytes 860168 | tf_op jit(solution)/shard_map/ppermute | solution.py:1174
  674.9 30.6 %collective-permute-start.45 = (bf16[80,1792]{1,0:T(8,128)(2,1)S(1)}, bf16[80,1792]{1,0:T(8,128)(2,1)S(1)}, u32[]{:S(2)}, u32[]{:S(2)}) collective-permute-start(bf16[80,1792]{1,0:T(8,128)(2,1)S(1)} %get-tuple-element.294), channel_id=1, source_target_pairs={{0,16},{8,24},{16,0},{24,8},{1,17},{9,25},{17,1},{25,9},{2,18},{10... | collective-permute-start | bytes 860168 | tf_op jit(solution)/shard_map/ppermute | solution.py:1174
  (135 other events, 1649.1 us)
Sparse Core Ops, SparseCore 0:
  45.0 119.4 all-gather.1
  306.3 84.6 reduce-scatter.4
  393.3 95.3 reduce-scatter.6
  539.5 95.6 reduce-scatter.8
  637.5 83.0 reduce-scatter.10

commit v4 on v2

--- a/solution.py
+++ b/solution.py
@@ -1415,7 +1415,6 @@
     grad_gain_mlp = jnp.sum(grad_normed_mlp * hidden * inv_hidden, axis=0)
     grad_hidden = grad_top + norm_back(grad_normed_mlp * gain_mlp, hidden, inv_hidden)
     grad_attn = (residual_scale * grad_hidden).astype(bf16)
-    grad_attn, grad_down = lax.optimization_barrier((grad_attn, grad_down))
 
     def back_block(j, grad):
         return attend_back(
@@ -1433,17 +1432,9 @@
 
     near = near_blocks(grad_attn, group)
     back = [back_block(0, grad_attn)]
-    if fast:
-        act_late, _ = lax.optimization_barrier((act_all, grad_attn))
-        down_all = jnp.dot(
-            act_late[:, :hidden_part], down_proj, preferred_element_type=f32
-        ).astype(bf16)
-        down_terms = [down_all[j * seq_len : (j + 1) * seq_len] for j in range(group)]
-    near, back, down_terms = lax.optimization_barrier((near, back, down_terms))
+    near, back, grad_down = lax.optimization_barrier((near, back, grad_down))
     attn_parts = all_blocks(grad_attn, near, group)
     back += [back_block(j, attn_parts[j]) for j in others]
-    down_terms, _ = lax.optimization_barrier((down_terms, attn_parts[1:]))
-    block_out = (hidden + residual_scale * scatter_sum(down_terms, group)).astype(bf16)
     owned = [to_owner_rows(rows) for rows in summed]
 
     def unpack(q, second):
@@ -1460,6 +1451,15 @@
     )
     latent_terms = [part[0] for part in back]
     grad_latent_low = scatter_sum(latent_terms, group)
+    if fast:
+        act_late, _ = lax.optimization_barrier((act_all, latent_terms))
+        down_all = jnp.dot(
+            act_late[:, :hidden_part], down_proj, preferred_element_type=f32
+        ).astype(bf16)
+        down_terms = [down_all[j * seq_len : (j + 1) * seq_len] for j in range(group)]
+    grad_latent_low, down_terms = lax.optimization_barrier((grad_latent_low, down_terms))
+    grad_down, _ = lax.optimization_barrier((grad_down, (summed[-1], grad_latent_low)))
+    down_total = lax.psum_scatter(grad_down, "rep", scatter_dimension=0, tiled=True)
     grad_normed_query = grad_latent_low[:, :QR]
     grad_normed_keyval = grad_latent_low[:, QR : QR + KR]
     grad_key_rope = grad_latent_low[:, QR + KR + HD : QR + KR + HD + RD]
@@ -1474,9 +1474,6 @@
         axis=1,
     ).astype(bf16)
     grad_latent_parts = gather_blocks(grad_latent_rows, group)
-    block_out, grad_latent_parts = lax.optimization_barrier((block_out, grad_latent_parts))
-    grad_down, _ = lax.optimization_barrier((grad_down, (summed[-1], grad_latent_rows)))
-    down_total = lax.psum_scatter(grad_down, "rep", scatter_dimension=0, tiled=True)
     mixed_late, late_query, late_keyval, _ = lax.optimization_barrier(
         (
             [part[3] for part in attention],
@@ -1533,6 +1530,8 @@
     gains_row = gains_sum.reshape(replicas, 1, -1).astype(bf16)
     gains_row = jnp.pad(gains_row, ((0, 0), (0, 15), (0, unit - gains_row.shape[2])))
     last = jnp.concatenate([pair] + grad_out + grad_latent + [gains_row], axis=1)
+    last, down_terms = lax.optimization_barrier((last, down_terms))
+    block_out = (hidden + residual_scale * scatter_sum(down_terms, group)).astype(bf16)
     last, _ = lax.optimization_barrier((last.reshape(-1, unit), down_total))
     last = lax.psum_scatter(last, "rep", scatter_dimension=0, tiled=True)
     pair_own = to_owner_rows(last[:pair_rows])

time: 737 us -> 723 us (0.981)
  waiting for transfers between devices: 194 us -> 167 us
  local copies, waits for them, and re-layouts: 71.4 us -> 85.1 us
    reduce_scatter x1, waiting for transfers between devices: 39.2 us -> 0.01 us  [per_device(): last = lax.psum_scatter(last, 'rep', scatter_dimension=0, tiled=True)]
    reduce_scatter x1, waiting for transfers between devices: 0.01 us -> 15.8 us  [per_device(): lax.psum_scatter(grad_down, 'rep', scatter_dimension=0, tiled=True)]
    unnamed x214 -> x225, local copies, waits for them, and re-layouts: 27.5 us -> 33.8 us
  transfers between devices with their start and end apart: 52 -> 52, of which waited for: 25 -> 20; matrix products, arithmetic and copies ran while one was open for 17% -> 18% of each run, Pallas kernels for 33% -> 34%
where the time goes in v4:
time: 723 us; the launch traced here: 714 us
  Pallas kernels  322 us (45%)
  waiting for transfers between devices  167 us (23%)
  local copies, waits for them, and re-layouts  85.1 us (12%)
  starting transfers between devices  50.9 us (7%)
  other arithmetic  49.5 us (7%)
  matrix products  24.3 us (3%)
  between operations  15.7 us (2%)
    ppermute x47, waiting for transfers between devices, hop(): lax.ppermute(array, 'shard', [(i, i ^ distance) for i in range(group)])  151 us
    pallas_call x2, Pallas kernels, layer_part(): pl.pallas_call(functools.partial(layer_kernel, group, tiles_from, tiles,...  99.1 us
    pallas_call x1, Pallas kernels, latent_front(): pl.pallas_call(functools.partial(latent_kernel, group), in_specs=[pl.Bloc...  85.8 us
    ppermute x47, starting transfers between devices, hop(): lax.ppermute(array, 'shard', [(i, i ^ distance) for i in range(group)])  50.7 us
    pallas_call x4, Pallas kernels, attend_back(): pl.pallas_call(functools.partial(attend_back_kernel, heads), grid=(1,), o...  42.8 us
    pallas_call x4, Pallas kernels, attend(): pl.pallas_call(functools.partial(attend_kernel, heads), grid=(1,), out_sp...  34.9 us
    unnamed x225, local copies, waits for them, and re-layouts  33.8 us
    pallas_call x1, Pallas kernels, hidden_pieces(): pl.pallas_call(functools.partial(columns_kernel, group, replicas, hidden,...  32.4 us
  transfers between devices with their start and end apart: 52, of which 20 were waited for; matrix products, arithmetic and copies ran while one was open for 18% of the time, Pallas kernels for 34%

profile of v4, /device:TPU:0, one launch (start us, length us, event | category | flops | bytes accessed | tf_op | source)
XLA Modules:
  0.0 714.0 jit_solution(2977231555204728851)
XLA Ops:
  9.3 32.4 %hidden_pieces.1 = (bf16[640,3328]{1,0:T(8,128)(2,1)}, bf16[80,9984]{1,0:T(8,128)(2,1)S(1)}, f32[32,1536]{1,0:T(8,128)S(1)}, f32[4,8,256]{2,1,0:T(8,128)S(1)}, f32[4,3,256,128]{3,2,1,0:T(8,128)S(1)}) custom-call(bf16[640,12800]{1,0:T(8,128)(2,1)} %gate_up_ref.1, f32[8,1536]{1,0:T(8,128)S(1)} %broadcast_in_dim.12.gains_ref, ...), custom_call_target="tpu_custom_call" | custom-call | bytes 100000000 | tf_op jit(solution)/shard_map/hidden_pieces/pallas_call | solution.py:938
  49.5 5.2 reshape.174
  58.7 85.8 %latent_front.1 = (bf16[4,256,1152]{2,1,0:T(8,128)(2,1)}, f32[256,1056]{1,0:T(8,128)S(1)}, bf16[256,2560]{1,0:T(8,128)(2,1)S(1)}, bf16[2560,1056]{1,0:T(8,128)(2...) custom-call(bf16[256,2560]{1,0:T(8,128)(2,1)S(1)} %copy-done.2, f32[1,2560]{1,0:T(1,128)S(1)} %reshape.172.gains_ref, ...), custom_call_target="tpu_custom_call" | custom-call | flops 1384120320 | bytes 60000000 | tf_op jit(solution)/shard_map/latent_front/pallas_call | solution.py:1134
  149.7 8.6 %attend.4 = (bf16[256,2560]{1,0:T(8,128)(2,1)S(1)}, bf16[256,1280]{1,0:T(8,128)(2,1)S(1)}, bf16[256,1280]{1,0:T(8,128)(2,1)S(1)}, bf16[256,640]{1,0:T(8,128)(2,1)S(1)}) custom-call(bf16[4,256,1152]{2,1,0:T(8,128)(2,1)} %get-tuple-element.132.latent_ref.refs_0_.refs_1_.refs_2_.refs_3_, f32[4,3,256,128]{3,2,1,0:T(8,128)S(1)} %get-tuple-element.116.table_ref, ...), custom_call_target="tpu_custom_call" | custom-call | flops 1845493760 | bytes 7208960 | tf_op jit(solution)/shard_map/attend/pallas_call | solution.py:557
  167.3 9.0 %attend.5 = (bf16[256,2560]{1,0:T(8,128)(2,1)S(1)}, bf16[256,1280]{1,0:T(8,128)(2,1)S(1)}, bf16[256,1280]{1,0:T(8,128)(2,1)S(1)}, bf16[256,640]{1,0:T(8,128)(2,1)S(1)}) custom-call(bf16[4,256,1152]{2,1,0:T(8,128)(2,1)} %get-tuple-element.132.latent_ref.refs_0_.refs_1_.refs_2_.refs_3_, f32[4,3,256,128]{3,2,1,0:T(8,128)S(1)} %get-tuple-element.116.table_ref, ...), custom_call_target="tpu_custom_call" | custom-call | flops 1845493760 | bytes 7208960 | tf_op jit(solution)/shard_map/attend/pallas_call | solution.py:557
  178.7 8.6 %attend.6 = (bf16[256,2560]{1,0:T(8,128)(2,1)S(1)}, bf16[256,1280]{1,0:T(8,128)(2,1)S(1)}, bf16[256,1280]{1,0:T(8,128)(2,1)S(1)}, bf16[256,640]{1,0:T(8,128)(2,1)S(1)}) custom-call(bf16[4,256,1152]{2,1,0:T(8,128)(2,1)} %get-tuple-element.132.latent_ref.refs_0_.refs_1_.refs_2_.refs_3_, f32[4,3,256,128]{3,2,1,0:T(8,128)S(1)} %get-tuple-element.116.table_ref, ...), custom_call_target="tpu_custom_call" | custom-call | flops 1845493760 | bytes 7208960 | tf_op jit(solution)/shard_map/attend/pallas_call | solution.py:557
  188.6 8.6 %attend.7 = (bf16[256,2560]{1,0:T(8,128)(2,1)S(1)}, bf16[256,1280]{1,0:T(8,128)(2,1)S(1)}, bf16[256,1280]{1,0:T(8,128)(2,1)S(1)}, bf16[256,640]{1,0:T(8,128)(2,1)S(1)}) custom-call(bf16[4,256,1152]{2,1,0:T(8,128)(2,1)} %get-tuple-element.132.latent_ref.refs_0_.refs_1_.refs_2_.refs_3_, f32[4,3,256,128]{3,2,1,0:T(8,128)S(1)} %get-tuple-element.116.table_ref, ...), custom_call_target="tpu_custom_call" | custom-call | flops 1845493760 | bytes 7208960 | tf_op jit(solution)/shard_map/attend/pallas_call | solution.py:557
  197.3 7.2 %collective-permute-done.7 = bf16[256,2560]{1,0:T(8,128)(2,1)S(1)} collective-permute-done((bf16[256,2560]{1,0:T(8,128)(2,1)S(1)}, bf16[256,2560]{1,0:T(8,128)(2,1)S(1)}, u32[]{:S(2)}, u32[]{:S(2)}) %collective-permute-start.7) | collective-permute-done | bytes 1310752 | tf_op jit(solution)/shard_map/ppermute | solution.py:1165
  204.5 11.0 %collective-permute-done.5 = bf16[256,2560]{1,0:T(8,128)(2,1)S(1)} collective-permute-done((bf16[256,2560]{1,0:T(8,128)(2,1)S(1)}, bf16[256,2560]{1,0:T(8,128)(2,1)S(1)}, u32[]{:S(2)}, u32[]{:S(2)}) %collective-permute-start.5) | collective-permute-done | bytes 1310752 | tf_op jit(solution)/shard_map/ppermute | solution.py:1165
  218.5 24.7 %collective-permute-done.8.refs_1_ = bf16[256,2560]{1,0:T(8,128)(2,1)S(1)} collective-permute-done((bf16[256,2560]{1,0:T(8,128)(2,1)S(1)}, bf16[256,2560]{1,0:T(8,128)(2,1)S(1)}, u32[]{:S(2)}, u32[]{:S(2)}) %collective-permute-start.8) | collective-permute-done | bytes 1310752 | tf_op jit(solution)/shard_map/ppermute | solution.py:1165
  247.4 7.7 %collective-permute-done.10 = bf16[128,2560]{1,0:T(8,128)(2,1)} collective-permute-done((bf16[128,2560]{1,0:T(8,128)(2,1)}, bf16[128,2560]{1,0:T(8,128)(2,1)}, u32[]{:S(2)}, u32[]{:S(2)}) %collective-permute-start.10) | collective-permute-done | bytes 655392 | tf_op jit(solution)/shard_map/ppermute | solution.py:1165
  259.1 44.7 %layer_part.2 = (bf16[1024,1664]{1,0:T(8,128)(2,1)}, bf16[8,4,80,1536]{3,2,1,0:T(8,128)(2,1)}, f32[1024,2560]{1,0:T(8,128)}) custom-call(s32[4]{0:T(128)} %pad_add_fusion.order_ref, bf16[256,2560]{1,0:T(8,128)(2,1)} %copy-done.59, bf16[256,2560]{1,0:T(8,128)(2,1)} %copy-done.67, bf16[256,2560]{1,0:T(8,128)(2,1)} %copy-done.68, ...), custom_call_target="tpu_custom_call" | custom-call | flops 28185722880 | bytes 65536000 | tf_op jit(solution)/shard_map/layer_part/pallas_call | solution.py:415
  303.9 54.4 %layer_part.3 = (bf16[1024,1664]{1,0:T(8,128)(2,1)}, bf16[8,4,80,1792]{3,2,1,0:T(8,128)(2,1)}, bf16[1024,2560]{1,0:T(8,128)(2,1)}) custom-call(s32[4]{0:T(128)} %pad_add_fusion.order_ref, bf16[256,2560]{1,0:T(8,128)(2,1)} %copy-done.59, bf16[256,2560]{1,0:T(8,128)(2,1)} %copy-done.67, ...), custom_call_target="tpu_custom_call", output_to_operand_aliasing={{0}: (19, {})} | custom-call | flops 30534533120 | bytes 67502080 | tf_op jit(solution)/shard_map/layer_part/pallas_call | solution.py:415
  362.1 12.7 %collective-permute-done.12 = bf16[128,2560]{1,0:T(8,128)(2,1)S(1)} collective-permute-done((bf16[128,2560]{1,0:T(8,128)(2,1)S(1)}, bf16[128,2560]{1,0:T(8,128)(2,1)S(1)}, u32[]{:S(2)}, u32[]{:S(2)}) %collective-permute-start.12) | collective-permute-done | bytes 655392 | tf_op jit(solution)/shard_map/ppermute | solution.py:1165
  378.5 20.5 %collective-permute-done.15 = bf16[256,2560]{1,0:T(8,128)(2,1)S(1)} collective-permute-done((bf16[256,2560]{1,0:T(8,128)(2,1)S(1)}, bf16[256,2560]{1,0:T(8,128)(2,1)S(1)}, u32[]{:S(2)}, u32[]{:S(2)}) %collective-permute-start.15) | collective-permute-done | bytes 1310752 | tf_op jit(solution)/shard_map/ppermute | solution.py:1165
  410.5 14.9 %down_grad.1 = bf16[1600,2560]{1,0:T(8,128)(2,1)} custom-call(bf16[1024,1664]{1,0:T(8,128)(2,1)} %get-tuple-element.175.act_ref, bf16[256,2560]{1,0:T(8,128)(2,1)} %refs_0_, bf16[256,2560]{1,0:T(8,128)(2,1)} %collective-permute-done.refs_5_.refs_1_, bf16[256,2560]{1,0:T(8,128)(2,1)} %collective-permute-done.1.refs_6_.refs_2_, bf16[256,2560]{1,0:T(8,128)(2,1)S(1)} %copy-done.6), custom_call_target="tpu_custom_call" | custom-call | flops 8388608000 | bytes 16711680 | tf_op jit(solution)/shard_map/down_grad/pallas_call | solution.py:456
  427.6 10.3 %attend_back.4 = (bf16[256,1152]{1,0:T(8,128)(2,1)S(1)}, bf16[256,1280]{1,0:T(8,128)(2,1)S(1)}, bf16[256,1280]{1,0:T(8,128)(2,1)S(1)}) custom-call(bf16[256,2560]{1,0:T(8,128)(2,1)S(1)} %multiply_convert_fusion.grad_ref.refs_4_, bf16[256,1280]{1,0:T(8,128)(2,1)S(1)} %copy-done.33, bf16[256,1280]{1,0:T(8,128)(2,1)S(1)} %copy-done.35, ...), custom_call_target="tpu_custom_call" | custom-call | flops 2348810240 | bytes 7208960 | tf_op jit(solution)/shard_map/attend_back/pallas_call | solution.py:642
  444.6 11.1 %attend_back.6 = (bf16[256,1152]{1,0:T(8,128)(2,1)S(1)}, bf16[256,1280]{1,0:T(8,128)(2,1)S(1)}, bf16[256,1280]{1,0:T(8,128)(2,1)S(1)}) custom-call(bf16[256,2560]{1,0:T(8,128)(2,1)} %collective-permute-done.17.grad_ref.refs_6_, bf16[256,1280]{1,0:T(8,128)(2,1)S(1)} %copy-done.17, bf16[256,1280]{1,0:T(8,128)(2,1)S(1)} %copy-done.19, ...), custom_call_target="tpu_custom_call" | custom-call | flops 2348810240 | bytes 7208960 | tf_op jit(solution)/shard_map/attend_back/pallas_call | solution.py:642
  457.6 10.7 %attend_back.5 = (bf16[256,1152]{1,0:T(8,128)(2,1)S(1)}, bf16[256,1280]{1,0:T(8,128)(2,1)S(1)}, bf16[256,1280]{1,0:T(8,128)(2,1)S(1)}) custom-call(bf16[256,2560]{1,0:T(8,128)(2,1)} %collective-permute-done.16.grad_ref.refs_5_, bf16[256,1280]{1,0:T(8,128)(2,1)S(1)} %copy-done.23, bf16[256,1280]{1,0:T(8,128)(2,1)S(1)} %copy-done.25, ...), custom_call_target="tpu_custom_call" | custom-call | flops 2348810240 | bytes 7208960 | tf_op jit(solution)/shard_map/attend_back/pallas_call | solution.py:642
  470.5 10.6 %attend_back.7 = (bf16[256,1152]{1,0:T(8,128)(2,1)S(1)}, bf16[256,1280]{1,0:T(8,128)(2,1)S(1)}, bf16[256,1280]{1,0:T(8,128)(2,1)S(1)}) custom-call(bf16[256,2560]{1,0:T(8,128)(2,1)S(1)} %constant_dynamic-update-slice_fusion.2.grad_ref.refs_7_, bf16[256,1280]{1,0:T(8,128)(2,1)S(1)} %get-tuple-element.163.query_ref, bf16[256,1280]{1,0:T(8,128)(2,1)S(1)} %copy-done.15, ...), custom_call_target="tpu_custom_call" | custom-call | flops 2348810240 | bytes 7208960 | tf_op jit(solution)/shard_map/attend_back/pallas_call | solution.py:642
  482.6 12.1 %convolution_convert_fusion = bf16[1024,2560]{1,0:T(8,128)(2,1)S(1)} fusion(bf16[1600,2560]{1,0:T(8,128)(2,1)} %refs_17_.1, bf16[1024,1664]{1,0:T(8,128)(2,1)S(1)} %copy-done.65), kind=kOutput, calls=%fused_computation.1 | convolution fusion | flops 8391229440 | bytes 16842752 | tf_op jit(solution)/shard_map/dot_general | solution.py:1456
  529.6 7.0 fusion.13
  540.3 7.5 %out_grad.1 = bf16[640,2560]{1,0:T(8,128)(2,1)} custom-call(bf16[256,640]{1,0:T(8,128)(2,1)S(1)} %copy-done.52, bf16[256,640]{1,0:T(8,128)(2,1)S(1)} %copy-done.50, bf16[256,640]{1,0:T(8,128)(2,1)S(1)} %copy-done.48, bf16[256,640]{1,0:T(8,128)(2,1)S(1)} %copy-done.46, bf16[256,2560]{1,0:T(8,128)(2,1)S(1)} %copy-done.8, ...), custom_call_target="tpu_custom_call" | custom-call | flops 3355443200 | bytes 9830400 | tf_op jit(solution)/shard_map/out_grad/pallas_call | solution.py:689
  570.2 5.3 convolution_convert_fusion.1
  580.2 15.8 %reduce-scatter.9.cloned.1.call-done = bf16[200,2560]{1,0:T(8,128)(2,1)} async-done(((bf16[1600,2560]{1,0:T(8,128)(2,1)}), bf16[200,2560]{1,0:T(8,128)(2,1)}) %reduce-scatter.9.cloned.1.call-update) | async-done | bytes 1024016 | tf_op jit(solution)/shard_map/reduce_scatter | solution.py:1462
  608.3 8.2 %collective-permute-done.36 = bf16[128,2560]{1,0:T(8,128)(2,1)} collective-permute-done((bf16[128,2560]{1,0:T(8,128)(2,1)}, bf16[128,2560]{1,0:T(8,128)(2,1)}, u32[]{:S(2)}, u32[]{:S(2)}) %collective-permute-start.36) | collective-permute-done | bytes 655392 | tf_op jit(solution)/shard_map/ppermute | solution.py:1165
  619.3 12.5 %collective-permute-done.34 = bf16[128,2560]{1,0:T(8,128)(2,1)S(1)} collective-permute-done((bf16[128,2560]{1,0:T(8,128)(2,1)S(1)}, bf16[128,2560]{1,0:T(8,128)(2,1)S(1)}, u32[]{:S(2)}, u32[]{:S(2)}) %collective-permute-start.34) | collective-permute-done | bytes 655392 | tf_op jit(solution)/shard_map/ppermute | solution.py:1165
  636.8 22.2 %collective-permute-done.37 = bf16[256,2560]{1,0:T(8,128)(2,1)S(1)} collective-permute-done((bf16[256,2560]{1,0:T(8,128)(2,1)S(1)}, bf16[256,2560]{1,0:T(8,128)(2,1)S(1)}, u32[]{:S(2)}, u32[]{:S(2)}) %collective-permute-start.37) | collective-permute-done | bytes 1310752 | tf_op jit(solution)/shard_map/ppermute | solution.py:1165
  659.1 4.7 fusion.12
  666.3 5.1 collective-permute-done.46
  676.3 7.7 %convert_subtract_fusion = (f32[80,12800]{1,0:T(8,128)}, f32[80,12800]{1,0:T(8,128)}, f32[80,12800]{1,0:T(8,128)}) fusion(bf16[640,12800]{1,0:T(8,128)(2,1)} %gate_up_ref.1, s32[]{:T(128)S(6)} %select_n.89, bf16[80,12800]{1,0:T(8,128)(2,1)S(1)} %concatenate.76, bf16[80,12800]{1,0:T(8,128)(2,1)} %param.39, bf16[80,12800]{1,0:T(8,128)(2,1)} %param.46), kind=kLoop, calls=%fused_computation.8 | loop fusion | flops 19456000 | bytes 20480004 | tf_op jit(solution)/shard_map/sub | solution.py:64
  684.1 5.2 convert_subtract_fusion.1
  (445 shorter events, 186.1 us)
Async XLA Ops:
  7.2 251.9 %all-gather.2.cloned.1.call-start = ((), (), s32[]{:S(2)}) async-start(), calls=%async_computation.4 | async-start | bytes 14376960 | tf_op jit(solution)/shard_map/all_gather | solution.py:1296
  42.8 359.4 %reduce-scatter.5.cloned.1.call-start = ((), (), s32[]{:S(2)}) async-start(), calls=%async_computation.5 | async-start | bytes 8847360 | tf_op jit(solution)/shard_map/reduce_scatter | solution.py:1409
  42.9 102.7 %collective-permute-start = (bf16[256,2560]{1,0:T(8,128)(2,1)}, bf16[256,2560]{1,0:T(8,128)(2,1)}, u32[]{:S(2)}, u32[]{:S(2)}) collective-permute-start(bf16[256,2560]{1,0:T(8,128)(2,1)} %refs_0_), channel_id=1, source_target_pairs={{0,8},{8,0},{16,24},{24,16},{1,9},{9,1},{17,25},{25,17},{2,10},{10... | collective-permute-start | bytes 3932168 | tf_op jit(solution)/shard_map/ppermute | solution.py:1165
  44.4 101.2 %collective-permute-start.1 = (bf16[256,2560]{1,0:T(8,128)(2,1)}, bf16[256,2560]{1,0:T(8,128)(2,1)}, u32[]{:S(2)}, u32[]{:S(2)}) collective-permute-start(bf16[256,2560]{1,0:T(8,128)(2,1)} %refs_0_), channel_id=1, source_target_pairs={{0,16},{8,24},{16,0},{24,8},{1,17},{9,25},{17,1},{25,9},{2,18},{10... | collective-permute-start | bytes 3932168 | tf_op jit(solution)/shard_map/ppermute | solution.py:1165
  148.4 17.7 %collective-permute-start.2 = (bf16[128,2560]{1,0:T(8,128)(2,1)S(1)}, bf16[128,2560]{1,0:T(8,128)(2,1)S(1)}, u32[]{:S(2)}, u32[]{:S(2)}) collective-permute-start(bf16[128,2560]{1,0:T(8,128)(2,1)S(1)} %slice.364), channel_id=1, source_target_pairs={{0,16},{8,24},{16,0},{24,8},{1,17},{9,25},{17,1},{25,9},{2,18},{10... | collective-permute-start | bytes 1966088 | tf_op jit(solution)/shard_map/ppermute | solution.py:1165
  158.4 17.9 %collective-permute-start.6 = (bf16[128,2560]{1,0:T(8,128)(2,1)S(1)}, bf16[128,2560]{1,0:T(8,128)(2,1)S(1)}, u32[]{:S(2)}, u32[]{:S(2)}) collective-permute-start(bf16[128,2560]{1,0:T(8,128)(2,1)S(1)} %get-tuple-element.258), channel_id=1, source_target_pairs={{0,8},{8,0},{16,24},{24,16},{1,9},{9,1},{17,25},{25,17},{2,10},{10... | collective-permute-start | bytes 1966088 | tf_op jit(solution)/shard_map/ppermute | solution.py:1165
  159.4 28.0 %collective-permute-start.4 = (bf16[128,2560]{1,0:T(8,128)(2,1)S(1)}, bf16[128,2560]{1,0:T(8,128)(2,1)S(1)}, u32[]{:S(2)}, u32[]{:S(2)}) collective-permute-start(bf16[128,2560]{1,0:T(8,128)(2,1)S(1)} %get-tuple-element.257), channel_id=1, source_target_pairs={{0,16},{8,24},{16,0},{24,8},{1,17},{9,25},{17,1},{25,9},{2,18},{10... | collective-permute-start | bytes 1966088 | tf_op jit(solution)/shard_map/ppermute | solution.py:1165
  177.5 27.0 %collective-permute-start.7 = (bf16[256,2560]{1,0:T(8,128)(2,1)S(1)}, bf16[256,2560]{1,0:T(8,128)(2,1)S(1)}, u32[]{:S(2)}, u32[]{:S(2)}) collective-permute-start(bf16[256,2560]{1,0:T(8,128)(2,1)S(1)} %pad_maximum_fusion.3), channel_id=1, source_target_pairs={{0,16},{8,24},{16,0},{24,8},{1,17},{9,25},{17,1},{25,9},{2,18},{10... | collective-permute-start | bytes 3932168 | tf_op jit(solution)/shard_map/ppermute | solution.py:1165
  188.4 27.0 %collective-permute-start.5 = (bf16[256,2560]{1,0:T(8,128)(2,1)S(1)}, bf16[256,2560]{1,0:T(8,128)(2,1)S(1)}, u32[]{:S(2)}, u32[]{:S(2)}) collective-permute-start(bf16[256,2560]{1,0:T(8,128)(2,1)S(1)} %pad_maximum_fusion.2), channel_id=1, source_target_pairs={{0,8},{8,0},{16,24},{24,16},{1,9},{9,1},{17,25},{25,17},{2,10},{10... | collective-permute-start | bytes 3932168 | tf_op jit(solution)/shard_map/ppermute | solution.py:1165
  217.3 25.9 %collective-permute-start.8 = (bf16[256,2560]{1,0:T(8,128)(2,1)S(1)}, bf16[256,2560]{1,0:T(8,128)(2,1)S(1)}, u32[]{:S(2)}, u32[]{:S(2)}) collective-permute-start(bf16[256,2560]{1,0:T(8,128)(2,1)S(1)} %multiply_convert_fusion.1.refs_0_), channel_id=1, source_target_pairs={{0,8},{8,0},{16,24},{24,16},{1,9},{9,1},{17,25},{25,17},{2,10},{10... | collective-permute-start | bytes 3932168 | tf_op jit(solution)/shard_map/ppermute | solution.py:1165
  217.6 27.3 %collective-permute-start.9 = (bf16[256,2560]{1,0:T(8,128)(2,1)S(1)}, bf16[256,2560]{1,0:T(8,128)(2,1)S(1)}, u32[]{:S(2)}, u32[]{:S(2)}) collective-permute-start(bf16[256,2560]{1,0:T(8,128)(2,1)S(1)} %multiply_convert_fusion.1.refs_0_), channel_id=1, source_target_pairs={{0,16},{8,24},{16,0},{24,8},{1,17},{9,25},{17,1},{25,9},{2,18},{10... | collective-permute-start | bytes 3932168 | tf_op jit(solution)/shard_map/ppermute | solution.py:1165
  303.8 203.3 %reduce-scatter.7.cloned.1.call-start = ((), (), s32[]{:S(2)}) async-start(), calls=%async_computation.6 | async-start | bytes 10321920 | tf_op jit(solution)/shard_map/reduce_scatter | solution.py:1413
  377.5 21.5 %collective-permute-start.15 = (bf16[256,2560]{1,0:T(8,128)(2,1)S(1)}, bf16[256,2560]{1,0:T(8,128)(2,1)S(1)}, u32[]{:S(2)}, u32[]{:S(2)}) collective-permute-start(bf16[256,2560]{1,0:T(8,128)(2,1)S(1)} %pad_maximum_fusion.5), channel_id=1, source_target_pairs={{0,16},{8,24},{16,0},{24,8},{1,17},{9,25},{17,1},{25,9},{2,18},{10... | collective-permute-start | bytes 3932168 | tf_op jit(solution)/shard_map/ppermute | solution.py:1165
  377.7 22.6 %collective-permute-start.13 = (bf16[256,2560]{1,0:T(8,128)(2,1)S(1)}, bf16[256,2560]{1,0:T(8,128)(2,1)S(1)}, u32[]{:S(2)}, u32[]{:S(2)}) collective-permute-start(bf16[256,2560]{1,0:T(8,128)(2,1)S(1)} %pad_maximum_fusion.4), channel_id=1, source_target_pairs={{0,8},{8,0},{16,24},{24,16},{1,9},{9,1},{17,25},{25,17},{2,10},{10... | collective-permute-start | bytes 3932168 | tf_op jit(solution)/shard_map/ppermute | solution.py:1165
  402.3 193.7 %reduce-scatter.9.cloned.1.call-start = ((), (), s32[]{:S(2)}) async-start(), calls=%async_computation.7 | async-start | bytes 9216000 | tf_op jit(solution)/shard_map/reduce_scatter | solution.py:1462
  408.9 30.7 %collective-permute-start.16 = (bf16[256,2560]{1,0:T(8,128)(2,1)S(1)}, bf16[256,2560]{1,0:T(8,128)(2,1)}, u32[]{:S(2)}, u32[]{:S(2)}) collective-permute-start(bf16[256,2560]{1,0:T(8,128)(2,1)S(1)} %multiply_convert_fusion.grad_ref.refs_4_), channel_id=1, source_target_pairs={{0,8},{8,0},{16,24},{24,16},{1,9},{9,1},{17,25},{25,17},{2,10},{10... | collective-permute-start | bytes 3932168 | tf_op jit(solution)/shard_map/ppermute | solution.py:1165
  409.5 30.1 %collective-permute-start.17 = (bf16[256,2560]{1,0:T(8,128)(2,1)S(1)}, bf16[256,2560]{1,0:T(8,128)(2,1)}, u32[]{:S(2)}, u32[]{:S(2)}) collective-permute-start(bf16[256,2560]{1,0:T(8,128)(2,1)S(1)} %multiply_convert_fusion.grad_ref.refs_4_), channel_id=1, source_target_pairs={{0,16},{8,24},{16,0},{24,8},{1,17},{9,25},{17,1},{25,9},{2,18},{10... | collective-permute-start | bytes 3932168 | tf_op jit(solution)/shard_map/ppermute | solution.py:1165
  440.8 28.3 %collective-permute-start.18 = (bf16[128,2560]{1,0:T(8,128)(2,1)S(1)}, bf16[128,2560]{1,0:T(8,128)(2,1)S(1)}, u32[]{:S(2)}, u32[]{:S(2)}) collective-permute-start(bf16[128,2560]{1,0:T(8,128)(2,1)S(1)} %slice.382), channel_id=1, source_target_pairs={{0,16},{8,24},{16,0},{24,8},{1,17},{9,25},{17,1},{25,9},{2,18},{10... | collective-permute-start | bytes 1966088 | tf_op jit(solution)/shard_map/ppermute | solution.py:1165
  443.0 26.2 %collective-permute-start.19 = (bf16[128,2560]{1,0:T(8,128)(2,1)S(1)}, bf16[128,2560]{1,0:T(8,128)(2,1)S(1)}, u32[]{:S(2)}, u32[]{:S(2)}) collective-permute-start(bf16[128,2560]{1,0:T(8,128)(2,1)S(1)} %slice.383), channel_id=1, source_target_pairs={{0,8},{8,0},{16,24},{24,16},{1,9},{9,1},{17,25},{25,17},{2,10},{10... | collective-permute-start | bytes 1966088 | tf_op jit(solution)/shard_map/ppermute | solution.py:1165
  507.2 182.1 %reduce-scatter.11.cloned.1.call-start = ((), (), s32[]{:S(2)}) async-start(), calls=%async_computation.8 | async-start | bytes 8847360 | tf_op jit(solution)/shard_map/reduce_scatter | solution.py:1536
  516.7 40.2 %collective-permute-start.27 = (bf16[256,1056]{0,1:T(8,128)(2,1)}, bf16[256,1056]{0,1:T(8,128)(2,1)}, u32[]{:S(2)}, u32[]{:S(2)}) collective-permute-start(bf16[256,1056]{0,1:T(8,128)(2,1)} %copy.63), channel_id=1, source_target_pairs={{0,8},{8,0},{16,24},{24,16},{1,9},{9,1},{17,25},{25,17},{2,10},{10... | collective-permute-start | bytes 1622024 | tf_op jit(solution)/shard_map/ppermute | solution.py:1165
  518.4 42.9 %collective-permute-start.28 = (bf16[256,1056]{0,1:T(8,128)(2,1)}, bf16[256,1056]{0,1:T(8,128)(2,1)}, u32[]{:S(2)}, u32[]{:S(2)}) collective-permute-start(bf16[256,1056]{0,1:T(8,128)(2,1)} %copy.63), channel_id=1, source_target_pairs={{0,16},{8,24},{16,0},{24,8},{1,17},{9,25},{17,1},{25,9},{2,18},{10... | collective-permute-start | bytes 1622024 | tf_op jit(solution)/shard_map/ppermute | solution.py:1165
  553.3 16.9 %collective-permute-start.26 = (bf16[256,640]{1,0:T(8,128)(2,1)S(1)}, bf16[256,640]{1,0:T(8,128)(2,1)}, u32[]{:S(2)}, u32[]{:S(2)}) collective-permute-start(bf16[256,640]{1,0:T(8,128)(2,1)S(1)} %copy-done.84), channel_id=1, source_target_pairs={{0,24},{8,16},{16,8},{24,0},{1,25},{9,17},{17,9},{25,1},{2,26},{10... | collective-permute-start | bytes 983048 | tf_op jit(solution)/shard_map/ppermute | solution.py:1165
  598.4 18.0 %collective-permute-start.36 = (bf16[128,2560]{1,0:T(8,128)(2,1)}, bf16[128,2560]{1,0:T(8,128)(2,1)}, u32[]{:S(2)}, u32[]{:S(2)}) collective-permute-start(bf16[128,2560]{1,0:T(8,128)(2,1)} %get-tuple-element.251), channel_id=1, source_target_pairs={{0,8},{8,0},{16,24},{24,16},{1,9},{9,1},{17,25},{25,17},{2,10},{10... | collective-permute-start | bytes 1966088 | tf_op jit(solution)/shard_map/ppermute | solution.py:1165
  603.4 30.6 %collective-permute-start.41 = (bf16[80,1536]{1,0:T(8,128)(2,1)S(1)}, bf16[80,1536]{1,0:T(8,128)(2,1)S(1)}, u32[]{:S(2)}, u32[]{:S(2)}) collective-permute-start(bf16[80,1536]{1,0:T(8,128)(2,1)S(1)} %get-tuple-element.321), channel_id=1, source_target_pairs={{0,8},{8,0},{16,24},{24,16},{1,9},{9,1},{17,25},{25,17},{2,10},{10... | collective-permute-start | bytes 737288 | tf_op jit(solution)/shard_map/ppermute | solution.py:1165
  603.6 30.5 %collective-permute-start.42 = (bf16[80,1536]{1,0:T(8,128)(2,1)S(1)}, bf16[80,1536]{1,0:T(8,128)(2,1)S(1)}, u32[]{:S(2)}, u32[]{:S(2)}) collective-permute-start(bf16[80,1536]{1,0:T(8,128)(2,1)S(1)} %get-tuple-element.320), channel_id=1, source_target_pairs={{0,16},{8,24},{16,0},{24,8},{1,17},{9,25},{17,1},{25,9},{2,18},{10... | collective-permute-start | bytes 737288 | tf_op jit(solution)/shard_map/ppermute | solution.py:1165
  605.0 29.1 %collective-permute-start.43 = (bf16[80,1536]{1,0:T(8,128)(2,1)S(1)}, bf16[80,1536]{1,0:T(8,128)(2,1)S(1)}, u32[]{:S(2)}, u32[]{:S(2)}) collective-permute-start(bf16[80,1536]{1,0:T(8,128)(2,1)S(1)} %get-tuple-element.319), channel_id=1, source_target_pairs={{0,24},{8,16},{16,8},{24,0},{1,25},{9,17},{17,9},{25,1},{2,26},{10... | collective-permute-start | bytes 737288 | tf_op jit(solution)/shard_map/ppermute | solution.py:1165
  607.0 24.8 %collective-permute-start.34 = (bf16[128,2560]{1,0:T(8,128)(2,1)S(1)}, bf16[128,2560]{1,0:T(8,128)(2,1)S(1)}, u32[]{:S(2)}, u32[]{:S(2)}) collective-permute-start(bf16[128,2560]{1,0:T(8,128)(2,1)S(1)} %copy-done.76), channel_id=1, source_target_pairs={{0,16},{8,24},{16,0},{24,8},{1,17},{9,25},{17,1},{25,9},{2,18},{10... | collective-permute-start | bytes 1966088 | tf_op jit(solution)/shard_map/ppermute | solution.py:1165
  617.8 41.3 %collective-permute-start.37 = (bf16[256,2560]{1,0:T(8,128)(2,1)S(1)}, bf16[256,2560]{1,0:T(8,128)(2,1)S(1)}, u32[]{:S(2)}, u32[]{:S(2)}) collective-permute-start(bf16[256,2560]{1,0:T(8,128)(2,1)S(1)} %pad_maximum_fusion.7), channel_id=1, source_target_pairs={{0,16},{8,24},{16,0},{24,8},{1,17},{9,25},{17,1},{25,9},{2,18},{10... | collective-permute-start | bytes 3932168 | tf_op jit(solution)/shard_map/ppermute | solution.py:1165
  632.1 27.0 %collective-permute-start.35 = (bf16[256,2560]{1,0:T(8,128)(2,1)S(1)}, bf16[256,2560]{1,0:T(8,128)(2,1)S(1)}, u32[]{:S(2)}, u32[]{:S(2)}) collective-permute-start(bf16[256,2560]{1,0:T(8,128)(2,1)S(1)} %pad_maximum_fusion.6), channel_id=1, source_target_pairs={{0,8},{8,0},{16,24},{24,16},{1,9},{9,1},{17,25},{25,17},{2,10},{10... | collective-permute-start | bytes 3932168 | tf_op jit(solution)/shard_map/ppermute | solution.py:1165
  635.2 31.0 %collective-permute-start.44 = (bf16[80,1792]{1,0:T(8,128)(2,1)S(1)}, bf16[80,1792]{1,0:T(8,128)(2,1)S(1)}, u32[]{:S(2)}, u32[]{:S(2)}) collective-permute-start(bf16[80,1792]{1,0:T(8,128)(2,1)S(1)} %get-tuple-element.293), channel_id=1, source_target_pairs={{0,8},{8,0},{16,24},{24,16},{1,9},{9,1},{17,25},{25,17},{2,10},{10... | collective-permute-start | bytes 860168 | tf_op jit(solution)/shard_map/ppermute | solution.py:1165
  635.7 30.5 %collective-permute-start.45 = (bf16[80,1792]{1,0:T(8,128)(2,1)S(1)}, bf16[80,1792]{1,0:T(8,128)(2,1)S(1)}, u32[]{:S(2)}, u32[]{:S(2)}) collective-permute-start(bf16[80,1792]{1,0:T(8,128)(2,1)S(1)} %get-tuple-element.292), channel_id=1, source_target_pairs={{0,16},{8,24},{16,0},{24,8},{1,17},{9,25},{17,1},{25,9},{2,18},{10... | collective-permute-start | bytes 860168 | tf_op jit(solution)/shard_map/ppermute | solution.py:1165
  (127 other events, 1288.3 us)
Sparse Core Ops, SparseCore 0:
  43.0 119.4 all-gather.1
  304.0 85.1 reduce-scatter.4
  402.4 97.0 reduce-scatter.6
  507.3 88.6 reduce-scatter.8
  598.2 82.9 reduce-scatter.10

commit v5 on v4

--- a/solution.py
+++ b/solution.py
@@ -1435,9 +1435,8 @@
     near, back, grad_down = lax.optimization_barrier((near, back, grad_down))
     attn_parts = all_blocks(grad_attn, near, group)
     back += [back_block(j, attn_parts[j]) for j in others]
-    owned = [to_owner_rows(rows) for rows in summed]
-
-    def unpack(q, second):
+
+    def unpack(owned, q, second):
         pieces = []
         for (start, stop), rows in zip(cuts, owned):
             for t in range(stop - start):
@@ -1446,9 +1445,12 @@
         first = 2 * (cuts[-1][1] - cuts[-1][0]) * TILE + second * TAIL
         return pieces + [owned[-1][q, :, first : first + tail]]
 
-    gateup_total = jnp.concatenate(
-        [piece for second in (0, 1) for q in range(group) for piece in unpack(q, second)], axis=1
-    )
+    def unpacked(owned):
+        return jnp.concatenate(
+            [piece for second in (0, 1) for q in range(group) for piece in unpack(owned, q, second)],
+            axis=1,
+        )
+
     latent_terms = [part[0] for part in back]
     grad_latent_low = scatter_sum(latent_terms, group)
     if fast:
@@ -1474,6 +1476,10 @@
         axis=1,
     ).astype(bf16)
     grad_latent_parts = gather_blocks(grad_latent_rows, group)
+    first_rows, _ = lax.optimization_barrier((summed[0], grad_latent_low))
+    owned = [to_owner_rows(rows) for rows in [first_rows] + summed[1:]]
+    grad_latent_parts, owned = lax.optimization_barrier((grad_latent_parts, owned))
+    gateup_total = unpacked(owned)
     mixed_late, late_query, late_keyval, _ = lax.optimization_barrier(
         (
             [part[3] for part in attention],

time: 723 us -> 729 us (level)
  local copies, waits for them, and re-layouts: 85.1 us -> 97.8 us
    reduce_scatter x1, waiting for transfers between devices: 0.01 us -> 30.4 us  [per_device(): last = lax.psum_scatter(last, 'rep', scatter_dimension=0, tiled=True)]
    ppermute x47, waiting for transfers between devices: 151 us -> 133 us  [hop(): lax.ppermute(array, 'shard', [(i, i ^ distance) for i in range(group)])]
    reduce_scatter x1, waiting for transfers between devices: 15.8 us -> 0.01 us  [per_device(): lax.psum_scatter(grad_down, 'rep', scatter_dimension=0, tiled=True)]
    unnamed x225 -> x214, local copies, waits for them, and re-layouts: 33.8 us -> 32.3 us
  transfers between devices with their start and end apart: 52 -> 52, of which waited for: 20 -> 21; matrix products, arithmetic and copies ran while one was open for 18% -> 20% of each run, Pallas kernels for 34% -> 34%
where the time goes in v5:
time: 729 us; the launch traced here: 720 us
  Pallas kernels  322 us (44%)
  waiting for transfers between devices  164 us (22%)
  local copies, waits for them, and re-layouts  97.8 us (13%)
  other arithmetic  50 us (7%)
  starting transfers between devices  46.2 us (6%)
  matrix products  24.1 us (3%)
  between operations  15.8 us (2%)
    ppermute x47, waiting for transfers between devices, hop(): lax.ppermute(array, 'shard', [(i, i ^ distance) for i in range(group)])  133 us
    pallas_call x2, Pallas kernels, layer_part(): pl.pallas_call(functools.partial(layer_kernel, group, tiles_from, tiles,...  99.1 us
    pallas_call x1, Pallas kernels, latent_front(): pl.pallas_call(functools.partial(latent_kernel, group), in_specs=[pl.Bloc...  86.2 us
    ppermute x47, starting transfers between devices, hop(): lax.ppermute(array, 'shard', [(i, i ^ distance) for i in range(group)])  46 us
    pallas_call x4, Pallas kernels, attend_back(): pl.pallas_call(functools.partial(attend_back_kernel, heads), grid=(1,), o...  42.8 us
    pallas_call x4, Pallas kernels, attend(): pl.pallas_call(functools.partial(attend_kernel, heads), grid=(1,), out_sp...  34.9 us
    pallas_call x1, Pallas kernels, hidden_pieces(): pl.pallas_call(functools.partial(columns_kernel, group, replicas, hidden,...  32.4 us
    unnamed x214, local copies, waits for them, and re-layouts  32.3 us
  transfers between devices with their start and end apart: 52, of which 21 were waited for; matrix products, arithmetic and copies ran while one was open for 20% of the time, Pallas kernels for 34%

profile of v5, /device:TPU:0, one launch (start us, length us, event | category | flops | bytes accessed | tf_op | source)
XLA Modules:
  0.0 720.3 jit_solution(12257034428100152201)
XLA Ops:
  9.3 32.4 %hidden_pieces.1 = (bf16[640,3328]{1,0:T(8,128)(2,1)}, bf16[80,9984]{1,0:T(8,128)(2,1)S(1)}, f32[32,1536]{1,0:T(8,128)S(1)}, f32[4,8,256]{2,1,0:T(8,128)S(1)}, f32[4,3,256,128]{3,2,1,0:T(8,128)S(1)}) custom-call(bf16[640,12800]{1,0:T(8,128)(2,1)} %gate_up_ref.1, f32[8,1536]{1,0:T(8,128)S(1)} %broadcast_in_dim.12.gains_ref, ...), custom_call_target="tpu_custom_call" | custom-call | bytes 100000000 | tf_op jit(solution)/shard_map/hidden_pieces/pallas_call | solution.py:938
  49.5 5.2 reshape.174
  58.7 86.2 %latent_front.1 = (bf16[4,256,1152]{2,1,0:T(8,128)(2,1)}, f32[256,1056]{1,0:T(8,128)S(1)}, bf16[256,2560]{1,0:T(8,128)(2,1)S(1)}, bf16[2560,1056]{1,0:T(8,128)(2...) custom-call(bf16[256,2560]{1,0:T(8,128)(2,1)S(1)} %copy-done.2, f32[1,2560]{1,0:T(1,128)S(1)} %reshape.172.gains_ref, ...), custom_call_target="tpu_custom_call" | custom-call | flops 1384120320 | bytes 60000000 | tf_op jit(solution)/shard_map/latent_front/pallas_call | solution.py:1134
  150.1 8.6 %attend.4 = (bf16[256,2560]{1,0:T(8,128)(2,1)S(1)}, bf16[256,1280]{1,0:T(8,128)(2,1)S(1)}, bf16[256,1280]{1,0:T(8,128)(2,1)S(1)}, bf16[256,640]{1,0:T(8,128)(2,1)S(1)}) custom-call(bf16[4,256,1152]{2,1,0:T(8,128)(2,1)} %get-tuple-element.139.latent_ref.refs_0_.refs_1_.refs_2_.refs_3_, f32[4,3,256,128]{3,2,1,0:T(8,128)S(1)} %get-tuple-element.123.table_ref, ...), custom_call_target="tpu_custom_call" | custom-call | flops 1845493760 | bytes 7208960 | tf_op jit(solution)/shard_map/attend/pallas_call | solution.py:557
  162.6 4.0 collective-permute-done.2
  167.7 9.0 %attend.5 = (bf16[256,2560]{1,0:T(8,128)(2,1)S(1)}, bf16[256,1280]{1,0:T(8,128)(2,1)S(1)}, bf16[256,1280]{1,0:T(8,128)(2,1)S(1)}, bf16[256,640]{1,0:T(8,128)(2,1)S(1)}) custom-call(bf16[4,256,1152]{2,1,0:T(8,128)(2,1)} %get-tuple-element.139.latent_ref.refs_0_.refs_1_.refs_2_.refs_3_, f32[4,3,256,128]{3,2,1,0:T(8,128)S(1)} %get-tuple-element.123.table_ref, ...), custom_call_target="tpu_custom_call" | custom-call | flops 1845493760 | bytes 7208960 | tf_op jit(solution)/shard_map/attend/pallas_call | solution.py:557
  179.1 8.6 %attend.6 = (bf16[256,2560]{1,0:T(8,128)(2,1)S(1)}, bf16[256,1280]{1,0:T(8,128)(2,1)S(1)}, bf16[256,1280]{1,0:T(8,128)(2,1)S(1)}, bf16[256,640]{1,0:T(8,128)(2,1)S(1)}) custom-call(bf16[4,256,1152]{2,1,0:T(8,128)(2,1)} %get-tuple-element.139.latent_ref.refs_0_.refs_1_.refs_2_.refs_3_, f32[4,3,256,128]{3,2,1,0:T(8,128)S(1)} %get-tuple-element.123.table_ref, ...), custom_call_target="tpu_custom_call" | custom-call | flops 1845493760 | bytes 7208960 | tf_op jit(solution)/shard_map/attend/pallas_call | solution.py:557
  189.1 8.6 %attend.7 = (bf16[256,2560]{1,0:T(8,128)(2,1)S(1)}, bf16[256,1280]{1,0:T(8,128)(2,1)S(1)}, bf16[256,1280]{1,0:T(8,128)(2,1)S(1)}, bf16[256,640]{1,0:T(8,128)(2,1)S(1)}) custom-call(bf16[4,256,1152]{2,1,0:T(8,128)(2,1)} %get-tuple-element.139.latent_ref.refs_0_.refs_1_.refs_2_.refs_3_, f32[4,3,256,128]{3,2,1,0:T(8,128)S(1)} %get-tuple-element.123.table_ref, ...), custom_call_target="tpu_custom_call" | custom-call | flops 1845493760 | bytes 7208960 | tf_op jit(solution)/shard_map/attend/pallas_call | solution.py:557
  197.7 7.1 collective-permute-done.7
  204.9 11.0 %collective-permute-done.5 = bf16[256,2560]{1,0:T(8,128)(2,1)S(1)} collective-permute-done((bf16[256,2560]{1,0:T(8,128)(2,1)S(1)}, bf16[256,2560]{1,0:T(8,128)(2,1)S(1)}, u32[]{:S(2)}, u32[]{:S(2)}) %collective-permute-start.5) | collective-permute-done | bytes 1310752 | tf_op jit(solution)/shard_map/ppermute | solution.py:1165
  218.8 24.7 %collective-permute-done.8.refs_1_ = bf16[256,2560]{1,0:T(8,128)(2,1)S(1)} collective-permute-done((bf16[256,2560]{1,0:T(8,128)(2,1)S(1)}, bf16[256,2560]{1,0:T(8,128)(2,1)S(1)}, u32[]{:S(2)}, u32[]{:S(2)}) %collective-permute-start.8) | collective-permute-done | bytes 1310752 | tf_op jit(solution)/shard_map/ppermute | solution.py:1165
  247.7 7.6 %collective-permute-done.10 = bf16[128,2560]{1,0:T(8,128)(2,1)} collective-permute-done((bf16[128,2560]{1,0:T(8,128)(2,1)}, bf16[128,2560]{1,0:T(8,128)(2,1)}, u32[]{:S(2)}, u32[]{:S(2)}) %collective-permute-start.10) | collective-permute-done | bytes 655392 | tf_op jit(solution)/shard_map/ppermute | solution.py:1165
  259.7 44.7 %layer_part.2 = (bf16[1024,1664]{1,0:T(8,128)(2,1)}, bf16[8,4,80,1536]{3,2,1,0:T(8,128)(2,1)}, f32[1024,2560]{1,0:T(8,128)}) custom-call(s32[4]{0:T(128)} %pad_add_fusion.order_ref, bf16[256,2560]{1,0:T(8,128)(2,1)} %copy-done.59, bf16[256,2560]{1,0:T(8,128)(2,1)} %copy-done.69, bf16[256,2560]{1,0:T(8,128)(2,1)} %copy-done.70, ...), custom_call_target="tpu_custom_call" | custom-call | flops 28185722880 | bytes 65536000 | tf_op jit(solution)/shard_map/layer_part/pallas_call | solution.py:415
  304.5 54.4 %layer_part.3 = (bf16[1024,1664]{1,0:T(8,128)(2,1)}, bf16[8,4,80,1792]{3,2,1,0:T(8,128)(2,1)}, bf16[1024,2560]{1,0:T(8,128)(2,1)}) custom-call(s32[4]{0:T(128)} %pad_add_fusion.order_ref, bf16[256,2560]{1,0:T(8,128)(2,1)} %copy-done.59, bf16[256,2560]{1,0:T(8,128)(2,1)} %copy-done.69, ...), custom_call_target="tpu_custom_call", output_to_operand_aliasing={{0}: (19, {})} | custom-call | flops 30534533120 | bytes 67502080 | tf_op jit(solution)/shard_map/layer_part/pallas_call | solution.py:415
  362.4 13.5 %collective-permute-done.12 = bf16[128,2560]{1,0:T(8,128)(2,1)S(1)} collective-permute-done((bf16[128,2560]{1,0:T(8,128)(2,1)S(1)}, bf16[128,2560]{1,0:T(8,128)(2,1)S(1)}, u32[]{:S(2)}, u32[]{:S(2)}) %collective-permute-start.12) | collective-permute-done | bytes 655392 | tf_op jit(solution)/shard_map/ppermute | solution.py:1165
  378.8 20.8 %collective-permute-done.15 = bf16[256,2560]{1,0:T(8,128)(2,1)S(1)} collective-permute-done((bf16[256,2560]{1,0:T(8,128)(2,1)S(1)}, bf16[256,2560]{1,0:T(8,128)(2,1)S(1)}, u32[]{:S(2)}, u32[]{:S(2)}) %collective-permute-start.15) | collective-permute-done | bytes 1310752 | tf_op jit(solution)/shard_map/ppermute | solution.py:1165
  410.7 14.9 %down_grad.1 = bf16[1600,2560]{1,0:T(8,128)(2,1)} custom-call(bf16[1024,1664]{1,0:T(8,128)(2,1)} %get-tuple-element.182.act_ref, bf16[256,2560]{1,0:T(8,128)(2,1)} %refs_0_, bf16[256,2560]{1,0:T(8,128)(2,1)} %collective-permute-done.refs_5_.refs_1_, bf16[256,2560]{1,0:T(8,128)(2,1)} %collective-permute-done.1.refs_6_.refs_2_, bf16[256,2560]{1,0:T(8,128)(2,1)S(1)} %copy-done.6), custom_call_target="tpu_custom_call" | custom-call | flops 8388608000 | bytes 16711680 | tf_op jit(solution)/shard_map/down_grad/pallas_call | solution.py:456
  427.8 10.3 %attend_back.4 = (bf16[256,1152]{1,0:T(8,128)(2,1)S(1)}, bf16[256,1280]{1,0:T(8,128)(2,1)S(1)}, bf16[256,1280]{1,0:T(8,128)(2,1)S(1)}) custom-call(bf16[256,2560]{1,0:T(8,128)(2,1)S(1)} %multiply_convert_fusion.grad_ref.refs_4_, bf16[256,1280]{1,0:T(8,128)(2,1)S(1)} %copy-done.33, bf16[256,1280]{1,0:T(8,128)(2,1)S(1)} %copy-done.35, ...), custom_call_target="tpu_custom_call" | custom-call | flops 2348810240 | bytes 7208960 | tf_op jit(solution)/shard_map/attend_back/pallas_call | solution.py:642
  444.9 11.2 %attend_back.6 = (bf16[256,1152]{1,0:T(8,128)(2,1)S(1)}, bf16[256,1280]{1,0:T(8,128)(2,1)S(1)}, bf16[256,1280]{1,0:T(8,128)(2,1)S(1)}) custom-call(bf16[256,2560]{1,0:T(8,128)(2,1)} %collective-permute-done.17.grad_ref.refs_6_, bf16[256,1280]{1,0:T(8,128)(2,1)S(1)} %copy-done.19, bf16[256,1280]{1,0:T(8,128)(2,1)S(1)} %copy-done.21, ...), custom_call_target="tpu_custom_call" | custom-call | flops 2348810240 | bytes 7208960 | tf_op jit(solution)/shard_map/attend_back/pallas_call | solution.py:642
  457.9 10.7 %attend_back.5 = (bf16[256,1152]{1,0:T(8,128)(2,1)S(1)}, bf16[256,1280]{1,0:T(8,128)(2,1)S(1)}, bf16[256,1280]{1,0:T(8,128)(2,1)S(1)}) custom-call(bf16[256,2560]{1,0:T(8,128)(2,1)} %collective-permute-done.16.grad_ref.refs_5_, bf16[256,1280]{1,0:T(8,128)(2,1)S(1)} %copy-done.25, bf16[256,1280]{1,0:T(8,128)(2,1)S(1)} %copy-done.27, ...), custom_call_target="tpu_custom_call" | custom-call | flops 2348810240 | bytes 7208960 | tf_op jit(solution)/shard_map/attend_back/pallas_call | solution.py:642
  470.8 10.6 %attend_back.7 = (bf16[256,1152]{1,0:T(8,128)(2,1)S(1)}, bf16[256,1280]{1,0:T(8,128)(2,1)S(1)}, bf16[256,1280]{1,0:T(8,128)(2,1)S(1)}) custom-call(bf16[256,2560]{1,0:T(8,128)(2,1)S(1)} %constant_dynamic-update-slice_fusion.2.grad_ref.refs_7_, bf16[256,1280]{1,0:T(8,128)(2,1)S(1)} %get-tuple-element.170.query_ref, bf16[256,1280]{1,0:T(8,128)(2,1)S(1)} %copy-done.15, ...), custom_call_target="tpu_custom_call" | custom-call | flops 2348810240 | bytes 7208960 | tf_op jit(solution)/shard_map/attend_back/pallas_call | solution.py:642
  482.9 12.1 %convolution_convert_fusion = bf16[1024,2560]{1,0:T(8,128)(2,1)S(1)} fusion(bf16[1600,2560]{1,0:T(8,128)(2,1)} %refs_17_.1, bf16[1024,1664]{1,0:T(8,128)(2,1)S(1)} %copy-done.67), kind=kOutput, calls=%fused_computation.1 | convolution fusion | flops 8391229440 | bytes 16842752 | tf_op jit(solution)/shard_map/dot_general | solution.py:1458
  500.6 5.4 collective-permute-done.23
  526.7 7.1 fusion.13
  537.4 7.4 %out_grad.1 = bf16[640,2560]{1,0:T(8,128)(2,1)} custom-call(bf16[256,640]{1,0:T(8,128)(2,1)S(1)} %copy-done.52, bf16[256,640]{1,0:T(8,128)(2,1)S(1)} %copy-done.50, bf16[256,640]{1,0:T(8,128)(2,1)S(1)} %copy-done.48, bf16[256,640]{1,0:T(8,128)(2,1)S(1)} %copy-done.46, bf16[256,2560]{1,0:T(8,128)(2,1)S(1)} %copy-done.8, ...), custom_call_target="tpu_custom_call" | custom-call | flops 3355443200 | bytes 9830400 | tf_op jit(solution)/shard_map/out_grad/pallas_call | solution.py:689
  556.9 12.0 %collective-permute-done.32 = bf16[80,1536]{1,0:T(8,128)(2,1)} collective-permute-done((bf16[80,1536]{1,0:T(8,128)(2,1)}, bf16[80,1536]{1,0:T(8,128)(2,1)}, u32[]{:S(2)}, u32[]{:S(2)}) %collective-permute-start.32) | collective-permute-done | bytes 245792 | tf_op jit(solution)/shard_map/ppermute | solution.py:1165
  600.6 5.0 convolution_convert_fusion.1
  636.9 7.0 convert_subtract_fusion
  644.0 10.6 %collective-permute-done.43 = bf16[256,2560]{1,0:T(8,128)(2,1)S(1)} collective-permute-done((bf16[256,2560]{1,0:T(8,128)(2,1)S(1)}, bf16[256,2560]{1,0:T(8,128)(2,1)S(1)}, u32[]{:S(2)}, u32[]{:S(2)}) %collective-permute-start.43) | collective-permute-done | bytes 1310752 | tf_op jit(solution)/shard_map/ppermute | solution.py:1165
  654.6 5.1 fusion.12
  659.8 5.2 convert_subtract_fusion.1
  665.0 30.4 %reduce-scatter.11.cloned.1.call-done = bf16[384,1280]{1,0:T(8,128)(2,1)} async-done(((bf16[3072,1280]{1,0:T(8,128)(2,1)}), bf16[384,1280]{1,0:T(8,128)(2,1)}) %reduce-scatter.11.cloned.1.call-update) | async-done | bytes 983056 | tf_op jit(solution)/shard_map/reduce_scatter | solution.py:1542
  (434 shorter events, 192.8 us)
Async XLA Ops:
  7.2 252.5 %all-gather.2.cloned.1.call-start = ((), (), s32[]{:S(2)}) async-start(), calls=%async_computation.4 | async-start | bytes 14376960 | tf_op jit(solution)/shard_map/all_gather | solution.py:1296
  42.9 359.6 %reduce-scatter.5.cloned.1.call-start = ((), (), s32[]{:S(2)}) async-start(), calls=%async_computation.5 | async-start | bytes 8847360 | tf_op jit(solution)/shard_map/reduce_scatter | solution.py:1409
  42.9 103.1 %collective-permute-start = (bf16[256,2560]{1,0:T(8,128)(2,1)}, bf16[256,2560]{1,0:T(8,128)(2,1)}, u32[]{:S(2)}, u32[]{:S(2)}) collective-permute-start(bf16[256,2560]{1,0:T(8,128)(2,1)} %refs_0_), channel_id=1, source_target_pairs={{0,8},{8,0},{16,24},{24,16},{1,9},{9,1},{17,25},{25,17},{2,10},{10... | collective-permute-start | bytes 3932168 | tf_op jit(solution)/shard_map/ppermute | solution.py:1165
  44.4 101.6 %collective-permute-start.1 = (bf16[256,2560]{1,0:T(8,128)(2,1)}, bf16[256,2560]{1,0:T(8,128)(2,1)}, u32[]{:S(2)}, u32[]{:S(2)}) collective-permute-start(bf16[256,2560]{1,0:T(8,128)(2,1)} %refs_0_), channel_id=1, source_target_pairs={{0,16},{8,24},{16,0},{24,8},{1,17},{9,25},{17,1},{25,9},{2,18},{10... | collective-permute-start | bytes 3932168 | tf_op jit(solution)/shard_map/ppermute | solution.py:1165
  148.8 17.7 %collective-permute-start.2 = (bf16[128,2560]{1,0:T(8,128)(2,1)S(1)}, bf16[128,2560]{1,0:T(8,128)(2,1)S(1)}, u32[]{:S(2)}, u32[]{:S(2)}) collective-permute-start(bf16[128,2560]{1,0:T(8,128)(2,1)S(1)} %slice.364), channel_id=1, source_target_pairs={{0,16},{8,24},{16,0},{24,8},{1,17},{9,25},{17,1},{25,9},{2,18},{10... | collective-permute-start | bytes 1966088 | tf_op jit(solution)/shard_map/ppermute | solution.py:1165
  158.9 18.0 %collective-permute-start.6 = (bf16[128,2560]{1,0:T(8,128)(2,1)S(1)}, bf16[128,2560]{1,0:T(8,128)(2,1)S(1)}, u32[]{:S(2)}, u32[]{:S(2)}) collective-permute-start(bf16[128,2560]{1,0:T(8,128)(2,1)S(1)} %get-tuple-element.272), channel_id=1, source_target_pairs={{0,8},{8,0},{16,24},{24,16},{1,9},{9,1},{17,25},{25,17},{2,10},{10... | collective-permute-start | bytes 1966088 | tf_op jit(solution)/shard_map/ppermute | solution.py:1165
  159.8 28.0 %collective-permute-start.4 = (bf16[128,2560]{1,0:T(8,128)(2,1)S(1)}, bf16[128,2560]{1,0:T(8,128)(2,1)S(1)}, u32[]{:S(2)}, u32[]{:S(2)}) collective-permute-start(bf16[128,2560]{1,0:T(8,128)(2,1)S(1)} %get-tuple-element.271), channel_id=1, source_target_pairs={{0,16},{8,24},{16,0},{24,8},{1,17},{9,25},{17,1},{25,9},{2,18},{10... | collective-permute-start | bytes 1966088 | tf_op jit(solution)/shard_map/ppermute | solution.py:1165
  177.9 26.9 %collective-permute-start.7 = (bf16[256,2560]{1,0:T(8,128)(2,1)S(1)}, bf16[256,2560]{1,0:T(8,128)(2,1)S(1)}, u32[]{:S(2)}, u32[]{:S(2)}) collective-permute-start(bf16[256,2560]{1,0:T(8,128)(2,1)S(1)} %pad_maximum_fusion.3), channel_id=1, source_target_pairs={{0,16},{8,24},{16,0},{24,8},{1,17},{9,25},{17,1},{25,9},{2,18},{10... | collective-permute-start | bytes 3932168 | tf_op jit(solution)/shard_map/ppermute | solution.py:1165
  188.9 27.0 %collective-permute-start.5 = (bf16[256,2560]{1,0:T(8,128)(2,1)S(1)}, bf16[256,2560]{1,0:T(8,128)(2,1)S(1)}, u32[]{:S(2)}, u32[]{:S(2)}) collective-permute-start(bf16[256,2560]{1,0:T(8,128)(2,1)S(1)} %pad_maximum_fusion.2), channel_id=1, source_target_pairs={{0,8},{8,0},{16,24},{24,16},{1,9},{9,1},{17,25},{25,17},{2,10},{10... | collective-permute-start | bytes 3932168 | tf_op jit(solution)/shard_map/ppermute | solution.py:1165
  217.7 25.7 %collective-permute-start.8 = (bf16[256,2560]{1,0:T(8,128)(2,1)S(1)}, bf16[256,2560]{1,0:T(8,128)(2,1)S(1)}, u32[]{:S(2)}, u32[]{:S(2)}) collective-permute-start(bf16[256,2560]{1,0:T(8,128)(2,1)S(1)} %multiply_convert_fusion.1.refs_0_), channel_id=1, source_target_pairs={{0,8},{8,0},{16,24},{24,16},{1,9},{9,1},{17,25},{25,17},{2,10},{10... | collective-permute-start | bytes 3932168 | tf_op jit(solution)/shard_map/ppermute | solution.py:1165
  218.0 27.5 %collective-permute-start.9 = (bf16[256,2560]{1,0:T(8,128)(2,1)S(1)}, bf16[256,2560]{1,0:T(8,128)(2,1)S(1)}, u32[]{:S(2)}, u32[]{:S(2)}) collective-permute-start(bf16[256,2560]{1,0:T(8,128)(2,1)S(1)} %multiply_convert_fusion.1.refs_0_), channel_id=1, source_target_pairs={{0,16},{8,24},{16,0},{24,8},{1,17},{9,25},{17,1},{25,9},{2,18},{10... | collective-permute-start | bytes 3932168 | tf_op jit(solution)/shard_map/ppermute | solution.py:1165
  304.4 205.3 %reduce-scatter.7.cloned.1.call-start = ((), (), s32[]{:S(2)}) async-start(), calls=%async_computation.6 | async-start | bytes 10321920 | tf_op jit(solution)/shard_map/reduce_scatter | solution.py:1413
  378.0 21.6 %collective-permute-start.15 = (bf16[256,2560]{1,0:T(8,128)(2,1)S(1)}, bf16[256,2560]{1,0:T(8,128)(2,1)S(1)}, u32[]{:S(2)}, u32[]{:S(2)}) collective-permute-start(bf16[256,2560]{1,0:T(8,128)(2,1)S(1)} %pad_maximum_fusion.5), channel_id=1, source_target_pairs={{0,16},{8,24},{16,0},{24,8},{1,17},{9,25},{17,1},{25,9},{2,18},{10... | collective-permute-start | bytes 3932168 | tf_op jit(solution)/shard_map/ppermute | solution.py:1165
  378.8 21.8 %collective-permute-start.13 = (bf16[256,2560]{1,0:T(8,128)(2,1)S(1)}, bf16[256,2560]{1,0:T(8,128)(2,1)S(1)}, u32[]{:S(2)}, u32[]{:S(2)}) collective-permute-start(bf16[256,2560]{1,0:T(8,128)(2,1)S(1)} %pad_maximum_fusion.4), channel_id=1, source_target_pairs={{0,8},{8,0},{16,24},{24,16},{1,9},{9,1},{17,25},{25,17},{2,10},{10... | collective-permute-start | bytes 3932168 | tf_op jit(solution)/shard_map/ppermute | solution.py:1165
  402.5 207.7 %reduce-scatter.9.cloned.1.call-start = ((), (), s32[]{:S(2)}) async-start(), calls=%async_computation.7 | async-start | bytes 9216000 | tf_op jit(solution)/shard_map/reduce_scatter | solution.py:1464
  409.2 30.6 %collective-permute-start.16 = (bf16[256,2560]{1,0:T(8,128)(2,1)S(1)}, bf16[256,2560]{1,0:T(8,128)(2,1)}, u32[]{:S(2)}, u32[]{:S(2)}) collective-permute-start(bf16[256,2560]{1,0:T(8,128)(2,1)S(1)} %multiply_convert_fusion.grad_ref.refs_4_), channel_id=1, source_target_pairs={{0,8},{8,0},{16,24},{24,16},{1,9},{9,1},{17,25},{25,17},{2,10},{10... | collective-permute-start | bytes 3932168 | tf_op jit(solution)/shard_map/ppermute | solution.py:1165
  409.8 30.0 %collective-permute-start.17 = (bf16[256,2560]{1,0:T(8,128)(2,1)S(1)}, bf16[256,2560]{1,0:T(8,128)(2,1)}, u32[]{:S(2)}, u32[]{:S(2)}) collective-permute-start(bf16[256,2560]{1,0:T(8,128)(2,1)S(1)} %multiply_convert_fusion.grad_ref.refs_4_), channel_id=1, source_target_pairs={{0,16},{8,24},{16,0},{24,8},{1,17},{9,25},{17,1},{25,9},{2,18},{10... | collective-permute-start | bytes 3932168 | tf_op jit(solution)/shard_map/ppermute | solution.py:1165
  441.1 28.4 %collective-permute-start.18 = (bf16[128,2560]{1,0:T(8,128)(2,1)S(1)}, bf16[128,2560]{1,0:T(8,128)(2,1)S(1)}, u32[]{:S(2)}, u32[]{:S(2)}) collective-permute-start(bf16[128,2560]{1,0:T(8,128)(2,1)S(1)} %slice.382), channel_id=1, source_target_pairs={{0,16},{8,24},{16,0},{24,8},{1,17},{9,25},{17,1},{25,9},{2,18},{10... | collective-permute-start | bytes 1966088 | tf_op jit(solution)/shard_map/ppermute | solution.py:1165
  443.4 26.2 %collective-permute-start.19 = (bf16[128,2560]{1,0:T(8,128)(2,1)S(1)}, bf16[128,2560]{1,0:T(8,128)(2,1)S(1)}, u32[]{:S(2)}, u32[]{:S(2)}) collective-permute-start(bf16[128,2560]{1,0:T(8,128)(2,1)S(1)} %slice.383), channel_id=1, source_target_pairs={{0,8},{8,0},{16,24},{24,16},{1,9},{9,1},{17,25},{25,17},{2,10},{10... | collective-permute-start | bytes 1966088 | tf_op jit(solution)/shard_map/ppermute | solution.py:1165
  509.8 185.6 %reduce-scatter.11.cloned.1.call-start = ((), (), s32[]{:S(2)}) async-start(), calls=%async_computation.8 | async-start | bytes 8847360 | tf_op jit(solution)/shard_map/reduce_scatter | solution.py:1542
  512.8 87.8 %collective-permute-start.26 = (bf16[256,640]{1,0:T(8,128)(2,1)}, bf16[256,640]{1,0:T(8,128)(2,1)}, u32[]{:S(2)}, u32[]{:S(2)}) collective-permute-start(bf16[256,640]{1,0:T(8,128)(2,1)} %get-tuple-element.268), channel_id=1, source_target_pairs={{0,24},{8,16},{16,8},{24,0},{1,25},{9,17},{17,9},{25,1},{2,26},{10... | collective-permute-start | bytes 983048 | tf_op jit(solution)/shard_map/ppermute | solution.py:1165
  526.7 29.0 %collective-permute-start.31 = (bf16[80,1536]{1,0:T(8,128)(2,1)}, bf16[80,1536]{1,0:T(8,128)(2,1)}, u32[]{:S(2)}, u32[]{:S(2)}) collective-permute-start(bf16[80,1536]{1,0:T(8,128)(2,1)} %get-tuple-element.337), channel_id=1, source_target_pairs={{0,8},{8,0},{16,24},{24,16},{1,9},{9,1},{17,25},{25,17},{2,10},{10... | collective-permute-start | bytes 737288 | tf_op jit(solution)/shard_map/ppermute | solution.py:1165
  533.9 17.4 %collective-permute-start.39 = (bf16[1536]{0:T(1024)(128)(2,1)S(1)}, bf16[1536]{0:T(1024)(128)(2,1)S(1)}, u32[]{:S(2)}, u32[]{:S(2)}) collective-permute-start(bf16[1536]{0:T(1024)(128)(2,1)S(1)} %get-tuple-element.346), channel_id=1, source_target_pairs={{0,24},{8,16},{16,8},{24,0},{1,25},{9,17},{17,9},{25,1},{2,26},{10... | collective-permute-start | bytes 9224 | tf_op jit(solution)/shard_map/ppermute | solution.py:1165
  535.8 17.7 %collective-permute-start.38 = (bf16[1536]{0:T(1024)(128)(2,1)S(1)}, bf16[1536]{0:T(1024)(128)(2,1)S(1)}, u32[]{:S(2)}, u32[]{:S(2)}) collective-permute-start(bf16[1536]{0:T(1024)(128)(2,1)S(1)} %get-tuple-element.347), channel_id=1, source_target_pairs={{0,16},{8,24},{16,0},{24,8},{1,17},{9,25},{17,1},{25,9},{2,18},{10... | collective-permute-start | bytes 9224 | tf_op jit(solution)/shard_map/ppermute | solution.py:1165
  537.4 16.4 %collective-permute-start.37 = (bf16[1536]{0:T(1024)(128)(2,1)S(1)}, bf16[1536]{0:T(1024)(128)(2,1)S(1)}, u32[]{:S(2)}, u32[]{:S(2)}) collective-permute-start(bf16[1536]{0:T(1024)(128)(2,1)S(1)} %get-tuple-element.345), channel_id=1, source_target_pairs={{0,8},{8,0},{16,24},{24,16},{1,9},{9,1},{17,25},{25,17},{2,10},{10... | collective-permute-start | bytes 9224 | tf_op jit(solution)/shard_map/ppermute | solution.py:1165
  551.3 23.8 %collective-permute-start.27 = (bf16[256,1056]{0,1:T(8,128)(2,1)}, bf16[256,1056]{0,1:T(8,128)(2,1)S(1)}, u32[]{:S(2)}, u32[]{:S(2)}) collective-permute-start(bf16[256,1056]{0,1:T(8,128)(2,1)} %copy.63), channel_id=1, source_target_pairs={{0,8},{8,0},{16,24},{24,16},{1,9},{9,1},{17,25},{25,17},{2,10},{10... | collective-permute-start | bytes 1622024 | tf_op jit(solution)/shard_map/ppermute | solution.py:1165
  553.4 16.4 %collective-permute-start.28 = (bf16[256,1056]{0,1:T(8,128)(2,1)}, bf16[256,1056]{0,1:T(8,128)(2,1)}, u32[]{:S(2)}, u32[]{:S(2)}) collective-permute-start(bf16[256,1056]{0,1:T(8,128)(2,1)} %copy.63), channel_id=1, source_target_pairs={{0,16},{8,24},{16,0},{24,8},{1,17},{9,25},{17,1},{25,9},{2,18},{10... | collective-permute-start | bytes 1622024 | tf_op jit(solution)/shard_map/ppermute | solution.py:1165
  555.6 45.0 %collective-permute-start.25 = (bf16[256,640]{1,0:T(8,128)(2,1)}, bf16[256,640]{1,0:T(8,128)(2,1)}, u32[]{:S(2)}, u32[]{:S(2)}) collective-permute-start(bf16[256,640]{1,0:T(8,128)(2,1)} %get-tuple-element.269), channel_id=1, source_target_pairs={{0,16},{8,24},{16,0},{24,8},{1,17},{9,25},{17,1},{25,9},{2,18},{10... | collective-permute-start | bytes 983048 | tf_op jit(solution)/shard_map/ppermute | solution.py:1165
  583.6 17.0 %collective-permute-start.24 = (bf16[256,640]{1,0:T(8,128)(2,1)}, bf16[256,640]{1,0:T(8,128)(2,1)}, u32[]{:S(2)}, u32[]{:S(2)}) collective-permute-start(bf16[256,640]{1,0:T(8,128)(2,1)} %get-tuple-element.270), channel_id=1, source_target_pairs={{0,8},{8,0},{16,24},{24,16},{1,9},{9,1},{17,25},{25,17},{2,10},{10... | collective-permute-start | bytes 983048 | tf_op jit(solution)/shard_map/ppermute | solution.py:1165
  615.6 16.7 %collective-permute-start.40 = (bf16[128,2560]{1,0:T(8,128)(2,1)}, bf16[128,2560]{1,0:T(8,128)(2,1)}, u32[]{:S(2)}, u32[]{:S(2)}) collective-permute-start(bf16[128,2560]{1,0:T(8,128)(2,1)} %get-tuple-element.264), channel_id=1, source_target_pairs={{0,16},{8,24},{16,0},{24,8},{1,17},{9,25},{17,1},{25,9},{2,18},{10... | collective-permute-start | bytes 1966088 | tf_op jit(solution)/shard_map/ppermute | solution.py:1165
  631.4 23.2 %collective-permute-start.43 = (bf16[256,2560]{1,0:T(8,128)(2,1)S(1)}, bf16[256,2560]{1,0:T(8,128)(2,1)S(1)}, u32[]{:S(2)}, u32[]{:S(2)}) collective-permute-start(bf16[256,2560]{1,0:T(8,128)(2,1)S(1)} %pad_maximum_fusion.7), channel_id=1, source_target_pairs={{0,16},{8,24},{16,0},{24,8},{1,17},{9,25},{17,1},{25,9},{2,18},{10... | collective-permute-start | bytes 3932168 | tf_op jit(solution)/shard_map/ppermute | solution.py:1165
  634.2 20.3 %collective-permute-start.41 = (bf16[256,2560]{1,0:T(8,128)(2,1)S(1)}, bf16[256,2560]{1,0:T(8,128)(2,1)S(1)}, u32[]{:S(2)}, u32[]{:S(2)}) collective-permute-start(bf16[256,2560]{1,0:T(8,128)(2,1)S(1)} %pad_maximum_fusion.6), channel_id=1, source_target_pairs={{0,8},{8,0},{16,24},{24,16},{1,9},{9,1},{17,25},{25,17},{2,10},{10... | collective-permute-start | bytes 3932168 | tf_op jit(solution)/shard_map/ppermute | solution.py:1165
  (122 other events, 1341.5 us)
Sparse Core Ops, SparseCore 0:
  43.0 119.4 all-gather.1
  304.5 84.8 reduce-scatter.4
  402.7 97.0 reduce-scatter.6
  509.9 89.6 reduce-scatter.8
  610.4 84.9 reduce-scatter.10
